TPU v7x, 32 devices: a whole 2x2x4 slice. The times are simulated.
32 devices in a mesh: row: 4 (over y, x), col: 8 (over z, core).
Axes of the slice: x: 2, y: 2, z: 4, core: 2. Of those that a mesh axis runs over, the one named last changes fastest.
Arguments:
- kernel: bfloat16 [4, 4, 8, 2, 256, 256], P('row', None, 'col'), as said below
Outputs:
- panels: float32 [4, 4, 2, 256, 256], P('row')
- schur: bfloat16 [4, 4, 8, 2, 256, 256], P('row', None, 'col')
Inputs may be any that keep to these rules, and one draw needn't show every extreme that they name: kernel describes a symmetric matrix whose leading 2 * 256 rows and columns form a positive definite block.
All inputs are finite; a program needn't handle non-finite values.
Results may differ from a plain program's by a relative error of at most 0.005.
Values may be sent and summed in bfloat16 or wider, within the bound.
No kernel may reach another device: no remote copies, remote signals or barrier semaphores. Data moves between devices by JAX's collectives and lax.ppermute only.
A program may use at most 64 MiB of HBM per device.

v0:
```python
import jax
import jax.numpy as jnp
from jax import lax
from jax.sharding import PartitionSpec as P

PANELS = 2


def from_root(block, axis, source):
    block = jnp.where(lax.axis_index(axis) == source, block, jnp.zeros_like(block))
    return lax.psum(block, axis)


def factorize(block):
    lower_factor = jnp.linalg.cholesky(block)
    identity = jnp.eye(block.shape[0], dtype=jnp.float32)
    inverse = lax.linalg.triangular_solve(lower_factor, identity, left_side=True, lower=True)
    return (lower_factor, inverse)


def solve_rows(column, inverse):
    row_blocks = column.shape[0]
    block_width = column.shape[1]
    flat = column.astype(jnp.float32).reshape(row_blocks * block_width, block_width)
    solved = jnp.dot(flat, inverse.T, precision=lax.Precision.HIGHEST)
    return solved.reshape(row_blocks, block_width, block_width)


def per_device(kernel):
    row_count = lax.axis_size("row")
    col_count = lax.axis_size("col")
    my_row = lax.axis_index("row")
    my_col = lax.axis_index("col")
    blocks_here = kernel[0, :, 0]
    row_blocks = blocks_here.shape[0]
    col_blocks = blocks_here.shape[1]
    block_width = blocks_here.shape[2]
    stride = col_count // row_count
    row_ids = jnp.arange(row_blocks, dtype=jnp.int32) * row_count + my_row
    col_ids = jnp.arange(col_blocks, dtype=jnp.int32) * col_count + my_col
    panel_list = []
    for current in range(PANELS):
        below = (row_ids > current)[:, None, None]
        at_diagonal = (row_ids == current)[:, None, None]
        lower_factor, inverse = factorize(blocks_here[0, 0].astype(jnp.float32))
        inverse = from_root(inverse, "row", current)
        solved = solve_rows(blocks_here[:, 0], inverse)
        strict = jnp.where(below, solved, jnp.float32(0.0))
        panel_step = jnp.where(at_diagonal, lower_factor[None], strict)
        panel_step = from_root(panel_step, "col", current)
        rounded = jnp.where(below, panel_step, jnp.float32(0.0)).astype(jnp.bfloat16)
        grouped = rounded.reshape(col_blocks, stride, block_width, block_width)
        picked = lax.dynamic_index_in_dim(grouped, my_col // row_count, 1, keepdims=False)
        mirror = from_root(picked, "row", my_col % row_count)
        panel_list.append(panel_step)
        update = jnp.einsum("iab,jcb->ijac", rounded, mirror, preferred_element_type=jnp.float32)
        blocks_here = (blocks_here.astype(jnp.float32) - update).astype(jnp.bfloat16)
    keep = (row_ids[:, None] >= PANELS) & (col_ids[None, :] >= PANELS)
    schur = jnp.where(keep[:, :, None, None], blocks_here, jnp.zeros((), jnp.bfloat16))
    panels = jnp.stack(panel_list, axis=1)
    return (panels[None], schur[None, :, None])


def solution(mesh):
    in_specs = (P("row", None, "col", None, None, None),)
    out_specs = (P("row", None, None, None, None), P("row", None, "col", None, None, None))
    return jax.shard_map(
        per_device, mesh=mesh, in_specs=in_specs, out_specs=out_specs, check_vma=False
    )
```

profile of v0, /device:TPU:1, one launch (start us, length us, event | category | flops | bytes accessed | tf_op | source)
XLA Modules:
  0.0 447.7 jit_solution(1968847662834866415)
XLA Ops:
  7.3 1.5 copy.12
  9.0 11.7 %cholesky.130 = f32[128,128]{1,0:T(8,128)S(1)} custom-call(f32[128,128]{1,0:T(8,128)S(1)} %cholesky.194), custom_call_target="Cholesky" | custom-call | tf_op jit(solution)/shard_map/jit(cholesky)/cholesky | solution.py:15
  20.7 9.8 %custom-call.13 = f32[1,128,128]{1,2,0:T(8,128)S(1)} custom-call(f32[1,128,128]{2,1,0:T(8,128)S(1)} %get-tuple-element.55), custom_call_target="InvertDiagBlocksLowerTriangular" | custom-call | tf_op jit(solution)/shard_map/jit(cholesky)/cholesky | solution.py:15
  31.0 11.7 %cholesky.147 = f32[128,128]{1,0:T(8,128)S(1)} custom-call(f32[128,128]{1,0:T(8,128)S(1)} %convolution_subtract_fusion.3), custom_call_target="Cholesky" | custom-call | tf_op jit(solution)/shard_map/jit(cholesky)/cholesky | solution.py:15
  44.9 0.7 fusion.16
  45.7 4.1 while.4
  46.4 1.3 bitcast_dynamic-update-slice_fusion.4
  48.4 1.3 bitcast_dynamic-update-slice_fusion.4
  49.8 19.9 %custom-call.14 = f32[2,128,128]{1,2,0:T(8,128)S(1)} custom-call(f32[2,128,128]{2,1,0:T(8,128)S(1)} %get-tuple-element.18), custom_call_target="InvertDiagBlocksLowerTriangular" | custom-call | tf_op jit(solution)/shard_map/triangular_solve/custom-call.0 | solution.py:17
  71.6 44.4 %all-reduce.8.cloned.1.call-done = f32[256,256]{1,0:T(8,128)} async-done(((f32[256,256]{1,0:T(8,128)}), f32[256,256]{1,0:T(8,128)}) %all-reduce.8.cloned.1.call-update) | async-done | bytes 262160 | tf_op jit(solution)/shard_map/psum | solution.py:11
  116.0 1.6 convolution_bitcast_fusion
  117.9 2.1 select_select_fusion
  120.1 57.5 %all-reduce.10.cloned.1.call-done = f32[4,256,256]{2,1,0:T(8,128)} async-done(((f32[4,256,256]{2,1,0:T(8,128)}), f32[4,256,256]{2,1,0:T(8,128)}) %all-reduce.10.cloned.1.call-update) | async-done | bytes 1048592 | tf_op jit(solution)/shard_map/psum | solution.py:11
  177.6 1.4 select_convert_fusion.1
  179.8 44.9 %all-reduce.12.cloned.1.call-done = bf16[2,256,256]{2,1,0:T(8,128)(2,1)} async-done(((bf16[2,256,256]{2,1,0:T(8,128)(2,1)}), bf16[2,256,256]{2,1,0:T(8,128)(2,1)}) %all-reduce.12.cloned.1.call-update) | async-done | bytes 262160 | tf_op jit(solution)/shard_map/psum | solution.py:11
  224.7 1.4 fusion.1
  226.4 11.7 %cholesky.164 = f32[128,128]{1,0:T(8,128)S(1)} custom-call(f32[128,128]{1,0:T(8,128)S(1)} %cholesky.197), custom_call_target="Cholesky" | custom-call | tf_op jit(solution)/shard_map/jit(cholesky)/cholesky | solution.py:15
  238.7 9.8 %custom-call.15 = f32[1,128,128]{1,2,0:T(8,128)S(1)} custom-call(f32[1,128,128]{2,1,0:T(8,128)S(1)} %get-tuple-element.51), custom_call_target="InvertDiagBlocksLowerTriangular" | custom-call | tf_op jit(solution)/shard_map/jit(cholesky)/cholesky | solution.py:15
  249.1 11.7 %cholesky.181 = f32[128,128]{1,0:T(8,128)S(1)} custom-call(f32[128,128]{1,0:T(8,128)S(1)} %convolution_subtract_fusion.2), custom_call_target="Cholesky" | custom-call | tf_op jit(solution)/shard_map/jit(cholesky)/cholesky | solution.py:15
  262.8 4.2 while.5
  263.7 1.4 bitcast_dynamic-update-slice_fusion.5
  265.7 1.4 bitcast_dynamic-update-slice_fusion.5
  267.1 19.7 %custom-call.16 = f32[2,128,128]{1,2,0:T(8,128)S(1)} custom-call(f32[2,128,128]{2,1,0:T(8,128)S(1)} %get-tuple-element.19), custom_call_target="InvertDiagBlocksLowerTriangular" | custom-call | tf_op jit(solution)/shard_map/triangular_solve/custom-call.0 | solution.py:17
  288.4 43.0 %all-reduce.14.cloned.1.call-done = f32[256,256]{1,0:T(8,128)} async-done(((f32[256,256]{1,0:T(8,128)}), f32[256,256]{1,0:T(8,128)}) %all-reduce.14.cloned.1.call-update) | async-done | bytes 262160 | tf_op jit(solution)/shard_map/psum | solution.py:11
  331.5 2.7 fusion.5
  334.3 57.4 %all-reduce.16.cloned.1.call-done = f32[4,256,256]{2,1,0:T(8,128)} async-done(((f32[4,256,256]{2,1,0:T(8,128)}), f32[4,256,256]{2,1,0:T(8,128)}) %all-reduce.16.cloned.1.call-update) | async-done | bytes 1048592 | tf_op jit(solution)/shard_map/psum | solution.py:11
  391.6 1.5 select_convert_fusion
  393.1 0.8 copy-done.2
  394.9 1.5 copy.22
  396.3 41.8 %all-reduce.18.cloned.1.call-done = bf16[2,256,256]{2,1,0:T(8,128)(2,1)} async-done(((bf16[2,256,256]{2,1,0:T(8,128)(2,1)}), bf16[2,256,256]{2,1,0:T(8,128)(2,1)}) %all-reduce.18.cloned.1.call-update) | async-done | bytes 262160 | tf_op jit(solution)/shard_map/psum | solution.py:11
  438.1 1.4 fusion.3
  439.5 1.3 copy.23
  (73 shorter events, 12.0 us)
Async XLA Ops:
  7.2 108.9 %all-reduce.8.cloned.1.call-start = ((), (), s32[]{:S(2)}) async-start(), calls=%async_computation | async-start | bytes 524288 | tf_op jit(solution)/shard_map/psum | solution.py:11
  71.3 106.4 %all-reduce.10.cloned.1.call-start = ((), (), s32[]{:S(2)}) async-start(), calls=%async_computation.1 | async-start | bytes 2097152 | tf_op jit(solution)/shard_map/psum | solution.py:11
  120.1 104.6 %all-reduce.12.cloned.1.call-start = ((), (), s32[]{:S(2)}) async-start(), calls=%async_computation.2 | async-start | bytes 524288 | tf_op jit(solution)/shard_map/psum | solution.py:11
  179.7 151.7 %all-reduce.14.cloned.1.call-start = ((), (), s32[]{:S(2)}) async-start(), calls=%async_computation.3 | async-start | bytes 524288 | tf_op jit(solution)/shard_map/psum | solution.py:11
  288.4 103.3 %all-reduce.16.cloned.1.call-start = ((), (), s32[]{:S(2)}) async-start(), calls=%async_computation.4 | async-start | bytes 2097152 | tf_op jit(solution)/shard_map/psum | solution.py:11
  334.2 60.6 %copy-start = (f32[4,256,256]{2,1,0:T(8,128)S(1)}, f32[4,256,256]{2,1,0:T(8,128)}, u32[]{:S(2)}) copy-start(f32[4,256,256]{2,1,0:T(8,128)} %all-reduce.10.cloned.1.call-done) | copy-start | bytes 3145732
  334.2 103.9 %all-reduce.18.cloned.1.call-start = ((), (), s32[]{:S(2)}) async-start(), calls=%async_computation.5 | async-start | bytes 524288 | tf_op jit(solution)/shard_map/psum | solution.py:11
  391.6 3.1 copy-start.1
  393.1 0.8 copy-start.2
  394.9 43.2 %copy-start.3 = (bf16[4,256,256]{2,1,0:T(8,128)(2,1)S(1)}, bf16[4,256,256]{2,1,0:T(8,128)(2,1)}, u32[]{:S(2)}) copy-start(bf16[4,256,256]{2,1,0:T(8,128)(2,1)} %copy-done.2) | copy-start | bytes 1572868
Sparse Core Ops, SparseCore 0:
  71.4 44.6 all-reduce.7
  120.2 57.3 all-reduce.9
  181.4 43.2 all-reduce.11
  288.5 42.9 all-reduce.13
  334.4 57.2 all-reduce.15
  394.8 43.2 all-reduce.17
where the time goes:
time: 449 us; the launch traced here: 448 us
  waiting for transfers between devices  289 us (64%)
  other arithmetic  117 us (26%)
  between operations  17.1 us (4%)
  local copies, waits for them, and re-layouts  14 us (3%)
  matrix products  9.77 us (2%)
    psum x6, waiting for transfers between devices, from_root(): return lax.psum(block, axis)  289 us
    another operation x13, other arithmetic, factorize(): lower_factor = jnp.linalg.cholesky(block)  68.6 us
    another operation x5, other arithmetic, factorize(): lax.linalg.triangular_solve(lower_factor, identity, left_side=True, lower...  40.3 us
  transfers between devices with their start and end apart: 6, of which 6 were waited for; matrix products, arithmetic and copies ran while one was open for 0% of the time, Pallas kernels for 0%

commit v1 on v0

v1 whole, which is shorter than its diff:
```python
import jax
import jax.numpy as jnp
from jax import lax
from jax.experimental import pallas as pl
from jax.experimental.pallas import tpu as pltpu
from jax.sharding import PartitionSpec as P

PANELS = 2
HIGHEST = lax.Precision.HIGHEST
VMEM_LIMIT = 48 * 1024 * 1024


def reciprocal(x):
    r = pl.reciprocal(x, approx=True)
    return r * (2.0 - x * r)

def spread(row):
    return jnp.broadcast_to(row, (8, row.shape[1]))

def lane(tile, k):
    return jnp.broadcast_to(tile[:, k:k + 1], (8, 128))

def factor_tile(matrix):
    groups = 16
    rows_of = lax.broadcasted_iota(jnp.int32, (8, 128), 0)
    cols_of = lax.broadcasted_iota(jnp.int32, (8, 128), 1)
    left = [matrix[8 * g:8 * g + 8, :] for g in range(groups)]
    right = [(cols_of == rows_of + 8 * g).astype(jnp.float32) for g in range(groups)]
    upper, inverse = [], []
    for s in range(groups):
        y = [spread(left[s][k:k + 1, :]) for k in range(8)]
        v = [spread(right[s][k:k + 1, :]) for k in range(8)]
        d = [[lane(y[i], 8 * s + k) if k >= i else None for k in range(8)] for i in range(8)]
        ratio = [[None] * 8 for _ in range(8)]
        inv = []
        for k in range(8):
            inv.append(reciprocal(d[k][k]))
            for i in range(k + 1, 8):
                ratio[i][k] = d[k][i] * inv[k]
                for j in range(i, 8):
                    d[i][j] = d[i][j] - ratio[i][k] * d[k][j]
                y[i] = y[i] - ratio[i][k] * y[k]
                v[i] = v[i] - ratio[i][k] * v[k]
        up = jnp.zeros((8, 128), jnp.float32)
        low = jnp.zeros((8, 128), jnp.float32)
        for k in range(8):
            root = lax.rsqrt(d[k][k])
            up = jnp.where(rows_of == k, y[k] * root, up)
            low = jnp.where(rows_of == k, v[k] * root, low)
        upper.append(jnp.where(cols_of >= rows_of + 8 * s, up, 0.0))
        inverse.append(low)
        if s + 1 == groups:
            break
        x, w = [None] * 8, [None] * 8
        for k in reversed(range(8)):
            x[k] = y[k] * inv[k]
            w[k] = v[k] * inv[k]
            for j in range(k + 1, 8):
                x[k] = x[k] - ratio[j][k] * x[j]
                w[k] = w[k] - ratio[j][k] * w[j]
        for g in range(s + 1, groups):
            f = [lane(left[g], 8 * s + k) for k in range(8)]
            for k in range(8):
                left[g] = left[g] - f[k] * x[k]
                right[g] = right[g] - f[k] * w[k]
    return jnp.concatenate(upper, axis=0), jnp.concatenate(inverse, axis=0)

def dot(a, b, dims=((1,), (0,))):
    return lax.dot_general(a, b, (dims, ((), ())), precision=HIGHEST, preferred_element_type=jnp.float32)

ROWS = ((1,), (1,))

def factor_rest(upper_1, inv_1, side, rest, lower_ref, inverse_ref):
    half = side.shape[0]
    lower_21 = dot(side, inv_1, ROWS)
    rest = rest - dot(lower_21, lower_21, ROWS)
    beside = dot(lower_21, inv_1)
    upper_2, inv_2 = factor_tile(rest)
    zero = jnp.zeros((half, half), jnp.float32)
    lower_ref[:half, :half] = upper_1.T
    lower_ref[:half, half:] = zero
    lower_ref[half:, :half] = lower_21
    lower_ref[half:, half:] = upper_2.T
    inverse_ref[:half, :half] = inv_1
    inverse_ref[:half, half:] = zero
    inverse_ref[half:, :half] = -dot(inv_2, beside)
    inverse_ref[half:, half:] = inv_2


def mul(a, b, dims=((1,), (0,))):
    return lax.dot_general(a, b, (dims, ((), ())), preferred_element_type=jnp.float32)


def start_kernel(quarter_ref, upper_ref, inverse_ref):
    upper, inverse = factor_tile(quarter_ref[...].astype(jnp.float32))
    upper_ref[...] = upper
    inverse_ref[...] = inverse


def first_kernel(rest_ref, upper_ref, tile_inverse_ref, lower_ref, inverse_ref):
    half = rest_ref.shape[1]
    side = rest_ref[:half].astype(jnp.float32)
    rest = rest_ref[half:].astype(jnp.float32)
    factor_rest(upper_ref[...], tile_inverse_ref[...], side, rest, lower_ref, inverse_ref)


def second_kernel(
    top_10_ref, rest_10_ref, rest_01_ref, top_11_ref, rest_11_ref, inverse_0_ref, panel_ref, lower_ref, inverse_ref,
):
    half = top_11_ref.shape[1]
    left = jnp.concatenate([top_10_ref[...], rest_10_ref[:half]], axis=0).astype(jnp.float32)
    right = jnp.concatenate([rest_01_ref[:half].astype(jnp.float32).T, rest_10_ref[half:].astype(jnp.float32)], axis=0)
    panel = dot(jnp.concatenate([left, right], axis=1), inverse_0_ref[...], ROWS).astype(jnp.bfloat16)
    panel_ref[...] = panel
    above, below = panel[:half], panel[half:]
    top = (top_11_ref[...].astype(jnp.float32) - mul(above, above, ROWS)).astype(jnp.bfloat16)
    side = (rest_11_ref[:half].astype(jnp.float32) - mul(below, above, ROWS)).astype(jnp.bfloat16)
    rest = (rest_11_ref[half:].astype(jnp.float32) - mul(below, below, ROWS)).astype(jnp.bfloat16)
    upper, inverse = factor_tile(top.astype(jnp.float32))
    factor_rest(upper, inverse, side.astype(jnp.float32), rest.astype(jnp.float32), lower_ref, inverse_ref)


def split(x, pieces_ref):
    for piece in range(3):
        high = x.astype(jnp.bfloat16)
        pieces_ref[piece] = high
        x = x - high.astype(jnp.float32)


def update_kernel(
    ids_ref, column_0_ref, column_1_ref, above_0_ref, above_1_ref, blocks_ref,
    lower_0_ref, lower_1_ref, inverse_0_ref, inverse_1_ref, panel_10_ref,
    panels_ref, schur_ref, pieces_0_ref, pieces_1_ref, mirror_0_ref, mirror_1_ref,
):
    step = pl.program_id(0)
    col_blocks = blocks_ref.shape[1]

    @pl.when(step == 0)
    def _():
        split(inverse_0_ref[...], pieces_0_ref)
        split(inverse_1_ref[...], pieces_1_ref)
        for m in range(col_blocks):
            above = above_0_ref[m]
            mirror = sum(mul(pieces_0_ref[p], above) for p in (2, 1, 0)).astype(jnp.bfloat16)
            mirror_0_ref[m] = mirror
            above = above_1_ref[m].astype(jnp.float32) - mul(panel_10_ref[...], mirror)
            above = above.astype(jnp.bfloat16)
            mirror_1_ref[m] = sum(mul(pieces_1_ref[p], above) for p in (2, 1, 0)).astype(jnp.bfloat16)

    block_row = step * ids_ref[2] + ids_ref[0]
    column = column_0_ref[0]
    solved = sum(mul(column, pieces_0_ref[p], ROWS) for p in (2, 1, 0))
    solved = jnp.where(block_row > 0, solved, 0.0)
    rounded_0 = solved.astype(jnp.bfloat16)
    panels_ref[0, 0] = jnp.where(block_row == 0, lower_0_ref[...], solved)
    column = column_1_ref[0].astype(jnp.float32) - mul(rounded_0, panel_10_ref[...], ROWS)
    column = column.astype(jnp.bfloat16)
    solved = sum(mul(column, pieces_1_ref[p], ROWS) for p in (2, 1, 0))
    solved = jnp.where(block_row > 1, solved, 0.0)
    rounded_1 = solved.astype(jnp.bfloat16)
    panels_ref[0, 1] = jnp.where(block_row == 1, lower_1_ref[...], solved)
    for m in range(col_blocks):
        block = blocks_ref[0, m].astype(jnp.float32) - mul(rounded_0, mirror_0_ref[m])
        block = block.astype(jnp.bfloat16).astype(jnp.float32) - mul(rounded_1, mirror_1_ref[m])
        keep = (block_row >= PANELS) & (m * ids_ref[3] + ids_ref[1] >= PANELS)
        schur_ref[0, m] = jnp.where(keep, block, 0.0).astype(jnp.bfloat16)


FACTOR_COST = pl.CostEstimate(flops=10**6, bytes_accessed=10**4, transcendentals=0)


def call_factor(kernel, name, shapes, *operands):
    return pl.pallas_call(
        kernel, out_shape=shapes, name=name, cost_estimate=FACTOR_COST,
        compiler_params=pltpu.CompilerParams(vmem_limit_bytes=VMEM_LIMIT),
    )(*operands)


def square(width, dtype=jnp.float32):
    return jax.ShapeDtypeStruct((width, width), dtype)


def update(ids, column_0, column_1, above_0, above_1, blocks, lower_0, lower_1, inverse_0, inverse_1, panel_10):
    row_blocks, col_blocks, width = blocks.shape[:3]
    one_row = pl.BlockSpec((1, width, width), lambda i: (i, 0, 0))
    whole_square = pl.BlockSpec((width, width), lambda i: (0, 0))
    above_spec = pl.BlockSpec((col_blocks, width, width), lambda i: (0, 0, 0))
    block_spec = pl.BlockSpec((1, col_blocks, width, width), lambda i: (i, 0, 0, 0))
    return pl.pallas_call(
        update_kernel,
        grid=(row_blocks,),
        in_specs=[pl.BlockSpec(memory_space=pltpu.SMEM), one_row, one_row, above_spec, above_spec, block_spec]
        + [whole_square] * 5,
        out_specs=[pl.BlockSpec((1, PANELS, width, width), lambda i: (i, 0, 0, 0)), block_spec],
        out_shape=[
            jax.ShapeDtypeStruct((row_blocks, PANELS, width, width), jnp.float32),
            jax.ShapeDtypeStruct(blocks.shape, jnp.bfloat16),
        ],
        scratch_shapes=[
            pltpu.VMEM((3, width, width), jnp.bfloat16),
            pltpu.VMEM((3, width, width), jnp.bfloat16),
            pltpu.VMEM((col_blocks, width, width), jnp.bfloat16),
            pltpu.VMEM((col_blocks, width, width), jnp.bfloat16),
        ],
        compiler_params=pltpu.CompilerParams(vmem_limit_bytes=VMEM_LIMIT),
        cost_estimate=pl.CostEstimate(flops=2 * 10**9, bytes_accessed=6 * 10**6, transcendentals=0),
        name="solve_and_update",
    )(ids, column_0, column_1, above_0, above_1, blocks, lower_0, lower_1, inverse_0, inverse_1, panel_10)


def corner_kernel(kernel_ref, quarters_ref, semaphores):
    half = quarters_ref.shape[1]
    copies = []
    for q, (row, col) in enumerate(((0, 0), (1, 0), (1, 1))):
        source = kernel_ref.at[0, 0, 0, 0, pl.ds(row * half, half), pl.ds(col * half, half)]
        copies.append(pltpu.make_async_copy(source, quarters_ref.at[pl.ds(q * half, half)], semaphores.at[q]))
    for copy in copies:
        copy.start()
    for copy in copies:
        copy.wait()


def corner_quarters(kernel):
    half = kernel.shape[-1] // 2
    return pl.pallas_call(
        corner_kernel,
        in_specs=[pl.BlockSpec(memory_space=pltpu.HBM)],
        out_specs=pl.BlockSpec(memory_space=pltpu.VMEM),
        out_shape=jax.ShapeDtypeStruct((3 * half, half), kernel.dtype),
        scratch_shapes=[pltpu.SemaphoreType.DMA((3,))],
        compiler_params=pltpu.CompilerParams(vmem_limit_bytes=60 * 1024 * 1024),
        name="corner_quarters",
    )(kernel)


def swap(block, axis, distance):
    count = lax.axis_size(axis)
    return lax.ppermute(block, axis, [(d, d ^ distance) for d in range(count)])


HOLDERS = ((0, 0), (0, 1), (1, 0), (1, 1))


def diagonal_along(quarters, my_col):
    col_count = lax.axis_size("col")
    along = quarters
    for chip in range(1, col_count // 2):
        pairs = [(r * col_count + core, r * col_count + chip * 2 + core) for r, core in HOLDERS]
        got = lax.ppermute(quarters, ("row", "col"), pairs)
        along = jnp.where(my_col // 2 == chip, got, along)
    return along


def diagonal_down(along, my_row, my_col):
    row_count, col_count = lax.axis_size("row"), lax.axis_size("col")
    first, second = along, along
    for step in range(1, row_count):
        pairs = []
        for chip in range(col_count // 2):
            for r, core in HOLDERS:
                col = chip * 2 + core
                pairs.append((r * col_count + col, (step ^ r) * col_count + col))
        got = lax.ppermute(along, ("row", "col"), pairs)
        first = jnp.where(my_row == step, got, first)
        second = jnp.where(my_row == step ^ 1, got, second)
    pair = jnp.stack([first, second])
    other = swap(pair, "col", 1)
    even = my_col % 2 == 0
    left = jnp.where(even, pair, other)
    right = jnp.where(even, other, pair)
    return left[0], right[0], left[1], right[1]


def rows_down(block, my_row):
    reach = 2
    while reach < lax.axis_size("row"):
        got = swap(block, "row", reach)
        block = jnp.where((my_row >= reach) & (my_row < 2 * reach), got, block)
        reach *= 2
    return block


def row_swap(block, my_row):
    other = swap(block, "row", 1)
    even = my_row % 2 == 0
    return jnp.where(even, block, other), jnp.where(even, other, block)


def first_stride(block):
    chips = lax.axis_size("col") // 2
    pairs = [(core, core + chips) for core in range(2)]
    return block, lax.ppermute(block, "col", pairs)


def other_strides(block, got, my_col):
    chips = lax.axis_size("col") // 2
    stride = chips // 2
    while True:
        block = jnp.where((my_col // 2) % (2 * stride) == stride, got, block)
        stride //= 2
        if stride == 0:
            return block
        if stride == 1:
            got = swap(block, "col", 2)
        else:
            sources = [chip * 2 + core for chip in range(0, chips, 2 * stride) for core in range(2)]
            got = lax.ppermute(block, "col", [(s, s + 2 * stride) for s in sources])


def per_device(kernel):
    my_row = lax.axis_index("row")
    my_col = lax.axis_index("col")
    even = my_col % 2 == 0
    blocks = kernel[0, :, 0]
    width = blocks.shape[2]
    half = width // 2
    quarters = corner_quarters(kernel)
    along = diagonal_along(quarters, my_col)
    rows, along = lax.optimization_barrier((blocks[:, 0], along))
    rows, rows_got = first_stride(rows)
    block_00, block_01, block_10, block_11 = diagonal_down(along, my_row, my_col)
    above, block_00 = lax.optimization_barrier((blocks[0], block_00))
    above = rows_down(above, my_row)
    upper_0, tile_inverse_0 = call_factor(start_kernel, "factor_start", [square(half)] * 2, block_00[:half])
    rows, rows_got, tile_inverse_0 = lax.optimization_barrier((rows, rows_got, tile_inverse_0))
    rows = other_strides(rows, rows_got, my_col)
    lower_0, inverse_0 = call_factor(
        first_kernel, "factor_first", [square(width)] * 2, block_00[half:], upper_0, tile_inverse_0)
    above, inverse_0 = lax.optimization_barrier((above, inverse_0))
    above_0, above_1 = row_swap(above, my_row)
    panel_10, lower_1, inverse_1 = call_factor(
        second_kernel, "factor_second", [square(width, jnp.bfloat16)] + [square(width)] * 2,
        block_10[:half], block_10[half:], block_01[half:], block_11[:half], block_11[half:], inverse_0)
    rows, above_0, above_1, inverse_1 = lax.optimization_barrier((rows, above_0, above_1, inverse_1))
    other = swap(rows, "col", 1)
    column_0 = jnp.where(even, rows, other)
    column_1 = jnp.where(even, other, rows)
    ids = jnp.stack([my_row, my_col, lax.axis_size("row"), lax.axis_size("col")]).astype(jnp.int32)
    panels, schur = update(
        ids, column_0, column_1, above_0, above_1, blocks,
        lower_0, lower_1, inverse_0, inverse_1, panel_10,
    )
    return (panels[None], schur[None, :, None])


def solution(mesh):
    in_specs = (P("row", None, "col", None, None, None),)
    out_specs = (P("row", None, None, None, None), P("row", None, "col", None, None, None))
    return jax.shard_map(
        per_device, mesh=mesh, in_specs=in_specs, out_specs=out_specs, check_vma=False
    )
```

time: 449 us -> 64.9 us (0.14)
  waiting for transfers between devices: 289 us -> 4.52 us
  other arithmetic: 117 us -> 1.33 us
  Pallas kernels: 0 us -> 34 us
  starting transfers between devices: 0.25 us -> 21.8 us
  between operations: 17.1 us -> 0.99 us
  local copies, waits for them, and re-layouts: 14 us -> 1.14 us
  matrix products: 9.77 us -> 0 us
    psum x6 -> x0, waiting for transfers between devices: 289 us -> none  [from_root(): return lax.psum(block, axis)]
    another operation x18 -> x3, other arithmetic: 109 us -> 0.13 us  [the longest x1 0.08 us: per_device(): jnp.stack([my_row, my_col, lax.axis_size('row'), lax.axis_size('col')])]
    pallas_call x0 -> x5, Pallas kernels: none -> 34 us  [the longest x3 26 us: call_factor(): pl.pallas_call(kernel, out_shape=shapes, name=name, cost_estimate=FACTOR_...]
    ppermute x0 -> x12, starting transfers between devices: none -> 21.8 us  [the longest x3 7.39 us: diagonal_along(): got = lax.ppermute(quarters, ('row', 'col'), pairs)]
    another operation x19 -> x0, local copies, waits for them, and re-layouts: 8.11 us -> none  [the longest x15 8.06 us: factorize(): lax.linalg.triangular_solve(lower_factor, identity, left_side=True, lower...]
    dot_general x4 -> x0, matrix products: 7.08 us -> none  [the longest x2 4.24 us: solve_rows(): solved = jnp.dot(flat, inverse.T, precision=lax.Precision.HIGHEST)]
    unnamed x11 -> x2, local copies, waits for them, and re-layouts: 5.06 us -> 0.01 us
    ppermute x0 -> x12, waiting for transfers between devices: none -> 4.52 us  [the longest x5 2.46 us: swap(): return lax.ppermute(block, axis, [(d, d ^ distance) for d in range(count)])]
  transfers between devices with their start and end apart: 6 -> 12, of which waited for: 6 -> 3; matrix products, arithmetic and copies ran while one was open for 0% -> 2% of each run, Pallas kernels for 0% -> 41%
where the time goes in v1:
time: 64.9 us; the launch traced here: 63.8 us
  Pallas kernels  34 us (52%)
  starting transfers between devices  21.8 us (34%)
  waiting for transfers between devices  4.52 us (7%)
  other arithmetic  1.33 us (2%)
  local copies, waits for them, and re-layouts  1.14 us (2%)
  between operations  0.99 us (2%)
    pallas_call x3, Pallas kernels, call_factor(): pl.pallas_call(kernel, out_shape=shapes, name=name, cost_estimate=FACTOR_...  26 us
    ppermute x3, starting transfers between devices, diagonal_along(): got = lax.ppermute(quarters, ('row', 'col'), pairs)  7.39 us
    pallas_call x1, Pallas kernels, update(): pl.pallas_call(update_kernel, grid=(row_blocks,), in_specs=[pl.BlockSpec(...  6.5 us
    ppermute x5, starting transfers between devices, swap(): return lax.ppermute(block, axis, [(d, d ^ distance) for d in range(count)])  5.85 us
    ppermute x3, starting transfers between devices, diagonal_down(): got = lax.ppermute(along, ('row', 'col'), pairs)  5.71 us
    ppermute x1, starting transfers between devices, first_stride(): return (block, lax.ppermute(block, 'col', pairs))  2.83 us
    ppermute x5, waiting for transfers between devices, swap(): return lax.ppermute(block, axis, [(d, d ^ distance) for d in range(count)])  2.46 us
    ppermute x3, waiting for transfers between devices, diagonal_along(): got = lax.ppermute(quarters, ('row', 'col'), pairs)  2.05 us
  transfers between devices with their start and end apart: 12, of which 3 were waited for; matrix products, arithmetic and copies ran while one was open for 2% of the time, Pallas kernels for 41%

profile of v1, /device:TPU:1, one launch (start us, length us, event | category | flops | bytes accessed | tf_op | source)
XLA Modules:
  0.0 63.8 jit_solution(15733551264447529684)
XLA Ops:
  0.6 0.0 copy-start
  0.6 1.5 %corner_quarters.1 = bf16[384,128]{1,0:T(8,128)(2,1)} custom-call(bf16[1,4,1,2,256,256]{5,4,3,2,1,0:T(8,128)(2,1)} %kernel_ref.1), custom_call_target="tpu_custom_call" | custom-call | tf_op jit(solution)/shard_map/corner_quarters/pallas_call | solution.py:225
  2.2 4.0 %collective-permute-start.2 = (bf16[384,128]{1,0:T(8,128)(2,1)}, bf16[384,128]{1,0:T(8,128)(2,1)S(1)}, u32[]{:S(2)}, u32[]{:S(2)}) collective-permute-start(bf16[384,128]{1,0:T(8,128)(2,1)} %corner_quarters.1), channel_id=1, source_target_pairs={{0,2},{1,3},{8,10},{9,11}} | collective-permute-start | bytes 294920 | tf_op jit(solution)/shard_map/ppermute | solution.py:249
  6.2 1.7 %collective-permute-start.1 = (bf16[384,128]{1,0:T(8,128)(2,1)}, bf16[384,128]{1,0:T(8,128)(2,1)S(1)}, u32[]{:S(2)}, u32[]{:S(2)}) collective-permute-start(bf16[384,128]{1,0:T(8,128)(2,1)} %corner_quarters.1), channel_id=1, source_target_pairs={{0,4},{1,5},{8,12},{9,13}} | collective-permute-start | bytes 294920 | tf_op jit(solution)/shard_map/ppermute | solution.py:249
  7.9 1.7 %collective-permute-start = (bf16[384,128]{1,0:T(8,128)(2,1)}, bf16[384,128]{1,0:T(8,128)(2,1)S(1)}, u32[]{:S(2)}, u32[]{:S(2)}) collective-permute-start(bf16[384,128]{1,0:T(8,128)(2,1)} %corner_quarters.1), channel_id=1, source_target_pairs={{0,6},{1,7},{8,14},{9,15}} | collective-permute-start | bytes 294920 | tf_op jit(solution)/shard_map/ppermute | solution.py:249
  9.6 1.1 %slice_bitcast_fusion = bf16[4,256,256]{2,1,0:T(8,128)(2,1)S(1)} fusion(bf16[4,2,256,256]{3,2,1,0:T(8,128)(2,1)} %bitcast.27), kind=kLoop, calls=%fused_computation | loop fusion | bytes 1048576 | tf_op jit(solution)/shard_map/squeeze | solution.py:319
  10.7 0.0 collective-permute-done.2
  10.7 2.0 %collective-permute-done = bf16[384,128]{1,0:T(8,128)(2,1)S(1)} collective-permute-done((bf16[384,128]{1,0:T(8,128)(2,1)}, bf16[384,128]{1,0:T(8,128)(2,1)S(1)}, u32[]{:S(2)}, u32[]{:S(2)}) %collective-permute-start) | collective-permute-done | bytes 98336 | tf_op jit(solution)/shard_map/ppermute | solution.py:249
  12.8 0.9 %select_select_fusion = bf16[384,128]{1,0:T(8,128)(2,1)S(1)} fusion(bf16[384,128]{1,0:T(8,128)(2,1)S(1)} %collective-permute-done, bf16[384,128]{1,0:T(8,128)(2,1)S(1)} %collective-permute-done.1, bf16[384,128]{1,0:T(8,128)(2,1)S(1)} %collective-permute-done.2, bf16[384,128]{1,0:T(8,128)(2,1)} %corner_quarters.1, pred[]{:T(512)S(6)} %eq.47, pred[]{:T(512)S(6)} %eq.46, ...), kind=kLoop, calls=%fused_computation.15 | loop fusion | flops 147456 | bytes 491523 | tf_op jit(solution)/shard_map/jit(_where)/select_n | solution.py:250
  13.7 3.1 %collective-permute-start.6 = (bf16[384,128]{1,0:T(8,128)(2,1)S(1)}, bf16[384,128]{1,0:T(8,128)(2,1)S(1)}, u32[]{:S(2)}, u32[]{:S(2)}) collective-permute-start(bf16[384,128]{1,0:T(8,128)(2,1)S(1)} %select_select_fusion), channel_id=1, source_target_pairs={{0,8},{1,9},{8,0},{9,1},{2,10},{3,11},{10,2},{11,3},{4,12},{5,13},... | collective-permute-start | bytes 294920 | tf_op jit(solution)/shard_map/ppermute | solution.py:263
  16.8 1.3 %collective-permute-start.5 = (bf16[384,128]{1,0:T(8,128)(2,1)S(1)}, bf16[384,128]{1,0:T(8,128)(2,1)S(1)}, u32[]{:S(2)}, u32[]{:S(2)}) collective-permute-start(bf16[384,128]{1,0:T(8,128)(2,1)S(1)} %select_select_fusion), channel_id=1, source_target_pairs={{0,16},{1,17},{8,24},{9,25},{2,18},{3,19},{10,26},{11,27},{4,20},{... | collective-permute-start | bytes 294920 | tf_op jit(solution)/shard_map/ppermute | solution.py:263
  18.1 1.3 %collective-permute-start.4 = (bf16[384,128]{1,0:T(8,128)(2,1)S(1)}, bf16[384,128]{1,0:T(8,128)(2,1)S(1)}, u32[]{:S(2)}, u32[]{:S(2)}) collective-permute-start(bf16[384,128]{1,0:T(8,128)(2,1)S(1)} %select_select_fusion), channel_id=1, source_target_pairs={{0,24},{1,25},{8,16},{9,17},{2,26},{3,27},{10,18},{11,19},{4,28},{... | collective-permute-start | bytes 294920 | tf_op jit(solution)/shard_map/ppermute | solution.py:263
  19.4 2.8 %collective-permute-start.3 = (bf16[4,256,256]{2,1,0:T(8,128)(2,1)S(1)}, bf16[4,256,256]{2,1,0:T(8,128)(2,1)S(1)}, u32[]{:S(2)}, u32[]{:S(2)}) collective-permute-start(bf16[4,256,256]{2,1,0:T(8,128)(2,1)S(1)} %slice_bitcast_fusion), channel_id=1, source_target_pairs={{0,4},{1,5},{8,12},{9,13},{16,20},{17,21},{24,28},{25,29}} | collective-permute-start | bytes 1572872 | tf_op jit(solution)/shard_map/ppermute | solution.py:292
  22.3 0.0 collective-permute-done.5
  22.3 0.0 collective-permute-done.4
  22.4 2.3 %collective-permute-start.7 = (bf16[2,384,128]{2,1,0:T(8,128)(2,1)S(1)}, bf16[2,384,128]{2,1,0:T(8,128)(2,1)S(1)}, u32[]{:S(2)}, u32[]{:S(2)}) collective-permute-start(bf16[2,384,128]{2,1,0:T(8,128)(2,1)S(1)} %pad_maximum_fusion), channel_id=1, source_target_pairs={{0,1},{1,0},{2,3},{3,2},{4,5},{5,4},{6,7},{7,6},{8,9},{9,8},{10,11... | collective-permute-start | bytes 589832 | tf_op jit(solution)/shard_map/ppermute | solution.py:238
  24.8 1.0 %collective-permute-done.7 = bf16[2,384,128]{2,1,0:T(8,128)(2,1)S(1)} collective-permute-done((bf16[2,384,128]{2,1,0:T(8,128)(2,1)S(1)}, bf16[2,384,128]{2,1,0:T(8,128)(2,1)S(1)}, u32[]{:S(2)}, u32[]{:S(2)}) %collective-permute-start.7) | collective-permute-done | bytes 196640 | tf_op jit(solution)/shard_map/ppermute | solution.py:238
  25.8 1.1 %collective-permute-start.9 = (bf16[2,256,256]{2,1,0:T(8,128)(2,1)S(1)}, bf16[2,256,256]{2,1,0:T(8,128)(2,1)S(1)}, u32[]{:S(2)}, u32[]{:S(2)}) collective-permute-start(bf16[2,256,256]{2,1,0:T(8,128)(2,1)S(1)} %slice_bitcast_fusion.1), channel_id=1, source_target_pairs={{0,16},{8,24},{16,0},{24,8},{1,17},{9,25},{17,1},{25,9},{2,18},{10... | collective-permute-start | bytes 786440 | tf_op jit(solution)/shard_map/ppermute | solution.py:238
  27.0 5.8 %factor_start.1 = (f32[128,128]{1,0:T(8,128)S(1)}, f32[128,128]{1,0:T(8,128)S(1)}) custom-call(bf16[128,128]{1,0:T(8,128)(2,1)S(1)} %slice.57.quarter_ref), custom_call_target="tpu_custom_call" | custom-call | flops 1000000 | bytes 10000 | tf_op jit(solution)/shard_map/factor_start/pallas_call | solution.py:173
  32.8 0.0 collective-permute-done.3
  32.8 0.1 broadcast_select_fusion
  32.9 0.1 collective-permute-start.8
  33.0 6.7 %factor_first.1 = (f32[256,256]{1,0:T(8,128)S(1)}, f32[256,256]{1,0:T(8,128)S(1)}) custom-call(bf16[256,128]{1,0:T(8,128)(2,1)S(1)} %slice.58.rest_ref, f32[128,128]{1,0:T(8,128)S(1)} %get-tuple-element.31.upper_ref, f32[128,128]{1,0:T(8,128)S(1)} %get-tuple-element.32.tile_inverse_ref), custom_call_target="tpu_custom_call" | custom-call | flops 1000000 | bytes 10000 | tf_op jit(solution)/shard_map/factor_first/pallas_call | solution.py:173
  39.8 0.7 %collective-permute-start.10 = (bf16[2,256,256]{2,1,0:T(8,128)(2,1)S(1)}, bf16[2,256,256]{2,1,0:T(8,128)(2,1)S(1)}, u32[]{:S(2)}, u32[]{:S(2)}) collective-permute-start(bf16[2,256,256]{2,1,0:T(8,128)(2,1)S(1)} %broadcast_select_fusion.4), channel_id=1, source_target_pairs={{0,8},{8,0},{16,24},{24,16},{1,9},{9,1},{17,25},{25,17},{2,10},{10... | collective-permute-start | bytes 786440 | tf_op jit(solution)/shard_map/ppermute | solution.py:238
  40.5 13.4 %factor_second.1 = (bf16[256,256]{1,0:T(8,128)(2,1)S(1)}, f32[256,256]{1,0:T(8,128)S(1)}, f32[256,256]{1,0:T(8,128)S(1)}) custom-call(bf16[128,128]{1,0:T(8,128)(2,1)S(1)} %get-tuple-element.60.top_10_ref, bf16[256,128]{1,0:T(8,128)(2,1)S(1)} %get-tuple-element.58.rest_10_ref, bf16[256,128]{1,0:T(8,128)(2,1)S(1)} %get-tuple-element.57.rest_01_ref, ...), custom_call_target="tpu_custom_call" | custom-call | flops 1000000 | bytes 10000 | tf_op jit(solution)/shard_map/factor_second/pallas_call | solution.py:173
  53.9 0.0 collective-permute-done.10
  54.0 0.1 broadcast_select_fusion.1
  54.0 1.6 %collective-permute-start.11 = (bf16[4,256,256]{2,1,0:T(8,128)(2,1)S(1)}, bf16[4,256,256]{2,1,0:T(8,128)(2,1)S(1)}, u32[]{:S(2)}, u32[]{:S(2)}) collective-permute-start(bf16[4,256,256]{2,1,0:T(8,128)(2,1)S(1)} %broadcast_select_fusion.1), channel_id=1, source_target_pairs={{0,1},{1,0},{2,3},{3,2},{4,5},{5,4},{6,7},{7,6},{8,9},{9,8},{10,11... | collective-permute-start | bytes 1572872 | tf_op jit(solution)/shard_map/ppermute | solution.py:238
  55.7 0.1 pad_add_fusion.ids_ref
  55.8 1.5 %collective-permute-done.11 = bf16[4,256,256]{2,1,0:T(8,128)(2,1)S(1)} collective-permute-done((bf16[4,256,256]{2,1,0:T(8,128)(2,1)S(1)}, bf16[4,256,256]{2,1,0:T(8,128)(2,1)S(1)}, u32[]{:S(2)}, u32[]{:S(2)}) %collective-permute-start.11) | collective-permute-done | bytes 524320 | tf_op jit(solution)/shard_map/ppermute | solution.py:238
  57.2 0.1 broadcast_select_fusion.2
  57.3 6.5 %solve_and_update.1 = (f32[4,2,256,256]{3,2,1,0:T(8,128)}, bf16[4,2,256,256]{3,2,1,0:T(8,128)(2,1)}) custom-call(s32[4]{0:T(128)S(1)} %pad_add_fusion.ids_ref, bf16[4,256,256]{2,1,0:T(8,128)(2,1)S(1)} %get-tuple-element.49.column_0_ref, bf16[4,256,256]{2,1,0:T(8,128)(2,1)S(1)} %get-tuple-element.48.column_1_ref, ...), custom_call_target="tpu_custom_call" | custom-call | flops 2000000000 | bytes 6000000 | tf_op jit(solution)/shard_map/solve_and_update/pallas_call | solution.py:189
  (16 shorter events, 0.2 us)
Async XLA Ops:
  0.6 24.1 %copy-start = (bf16[1,4,1,2,256,256]{5,4,3,2,1,0:T(8,128)(2,1)S(1)}, bf16[1,4,1,2,256,256]{5,4,3,2,1,0:T(8,128)(2,1)}, u32[]{:S(2)}) copy-start(bf16[1,4,1,2,256,256]{5,4,3,2,1,0:T(8,128)(2,1)} %kernel_ref.1) | copy-start | bytes 3145732
  2.2 8.5 %collective-permute-start.2 = (bf16[384,128]{1,0:T(8,128)(2,1)}, bf16[384,128]{1,0:T(8,128)(2,1)S(1)}, u32[]{:S(2)}, u32[]{:S(2)}) collective-permute-start(bf16[384,128]{1,0:T(8,128)(2,1)} %corner_quarters.1), channel_id=1, source_target_pairs={{0,2},{1,3},{8,10},{9,11}} | collective-permute-start | bytes 294920 | tf_op jit(solution)/shard_map/ppermute | solution.py:249
  6.2 4.5 %collective-permute-start.1 = (bf16[384,128]{1,0:T(8,128)(2,1)}, bf16[384,128]{1,0:T(8,128)(2,1)S(1)}, u32[]{:S(2)}, u32[]{:S(2)}) collective-permute-start(bf16[384,128]{1,0:T(8,128)(2,1)} %corner_quarters.1), channel_id=1, source_target_pairs={{0,4},{1,5},{8,12},{9,13}} | collective-permute-start | bytes 294920 | tf_op jit(solution)/shard_map/ppermute | solution.py:249
  7.9 4.9 %collective-permute-start = (bf16[384,128]{1,0:T(8,128)(2,1)}, bf16[384,128]{1,0:T(8,128)(2,1)S(1)}, u32[]{:S(2)}, u32[]{:S(2)}) collective-permute-start(bf16[384,128]{1,0:T(8,128)(2,1)} %corner_quarters.1), channel_id=1, source_target_pairs={{0,6},{1,7},{8,14},{9,15}} | collective-permute-start | bytes 294920 | tf_op jit(solution)/shard_map/ppermute | solution.py:249
  13.7 8.6 %collective-permute-start.6 = (bf16[384,128]{1,0:T(8,128)(2,1)S(1)}, bf16[384,128]{1,0:T(8,128)(2,1)S(1)}, u32[]{:S(2)}, u32[]{:S(2)}) collective-permute-start(bf16[384,128]{1,0:T(8,128)(2,1)S(1)} %select_select_fusion), channel_id=1, source_target_pairs={{0,8},{1,9},{8,0},{9,1},{2,10},{3,11},{10,2},{11,3},{4,12},{5,13},... | collective-permute-start | bytes 294920 | tf_op jit(solution)/shard_map/ppermute | solution.py:263
  16.8 5.5 %collective-permute-start.5 = (bf16[384,128]{1,0:T(8,128)(2,1)S(1)}, bf16[384,128]{1,0:T(8,128)(2,1)S(1)}, u32[]{:S(2)}, u32[]{:S(2)}) collective-permute-start(bf16[384,128]{1,0:T(8,128)(2,1)S(1)} %select_select_fusion), channel_id=1, source_target_pairs={{0,16},{1,17},{8,24},{9,25},{2,18},{3,19},{10,26},{11,27},{4,20},{... | collective-permute-start | bytes 294920 | tf_op jit(solution)/shard_map/ppermute | solution.py:263
  18.1 4.2 %collective-permute-start.4 = (bf16[384,128]{1,0:T(8,128)(2,1)S(1)}, bf16[384,128]{1,0:T(8,128)(2,1)S(1)}, u32[]{:S(2)}, u32[]{:S(2)}) collective-permute-start(bf16[384,128]{1,0:T(8,128)(2,1)S(1)} %select_select_fusion), channel_id=1, source_target_pairs={{0,24},{1,25},{8,16},{9,17},{2,26},{3,27},{10,18},{11,19},{4,28},{... | collective-permute-start | bytes 294920 | tf_op jit(solution)/shard_map/ppermute | solution.py:263
  19.4 13.4 %collective-permute-start.3 = (bf16[4,256,256]{2,1,0:T(8,128)(2,1)S(1)}, bf16[4,256,256]{2,1,0:T(8,128)(2,1)S(1)}, u32[]{:S(2)}, u32[]{:S(2)}) collective-permute-start(bf16[4,256,256]{2,1,0:T(8,128)(2,1)S(1)} %slice_bitcast_fusion), channel_id=1, source_target_pairs={{0,4},{1,5},{8,12},{9,13},{16,20},{17,21},{24,28},{25,29}} | collective-permute-start | bytes 1572872 | tf_op jit(solution)/shard_map/ppermute | solution.py:292
  22.4 3.4 %collective-permute-start.7 = (bf16[2,384,128]{2,1,0:T(8,128)(2,1)S(1)}, bf16[2,384,128]{2,1,0:T(8,128)(2,1)S(1)}, u32[]{:S(2)}, u32[]{:S(2)}) collective-permute-start(bf16[2,384,128]{2,1,0:T(8,128)(2,1)S(1)} %pad_maximum_fusion), channel_id=1, source_target_pairs={{0,1},{1,0},{2,3},{3,2},{4,5},{5,4},{6,7},{7,6},{8,9},{9,8},{10,11... | collective-permute-start | bytes 589832 | tf_op jit(solution)/shard_map/ppermute | solution.py:238
  25.8 13.9 %collective-permute-start.9 = (bf16[2,256,256]{2,1,0:T(8,128)(2,1)S(1)}, bf16[2,256,256]{2,1,0:T(8,128)(2,1)S(1)}, u32[]{:S(2)}, u32[]{:S(2)}) collective-permute-start(bf16[2,256,256]{2,1,0:T(8,128)(2,1)S(1)} %slice_bitcast_fusion.1), channel_id=1, source_target_pairs={{0,16},{8,24},{16,0},{24,8},{1,17},{9,25},{17,1},{25,9},{2,18},{10... | collective-permute-start | bytes 786440 | tf_op jit(solution)/shard_map/ppermute | solution.py:238
  32.9 21.1 %collective-permute-start.8 = (bf16[4,256,256]{2,1,0:T(8,128)(2,1)S(1)}, bf16[4,256,256]{2,1,0:T(8,128)(2,1)S(1)}, u32[]{:S(2)}, u32[]{:S(2)}) collective-permute-start(bf16[4,256,256]{2,1,0:T(8,128)(2,1)S(1)} %broadcast_select_fusion), channel_id=1, source_target_pairs={{0,2},{1,3},{2,0},{3,1},{4,6},{5,7},{6,4},{7,5},{8,10},{9,11},{10,... | collective-permute-start | bytes 1572872 | tf_op jit(solution)/shard_map/ppermute | solution.py:238
  39.8 14.2 %collective-permute-start.10 = (bf16[2,256,256]{2,1,0:T(8,128)(2,1)S(1)}, bf16[2,256,256]{2,1,0:T(8,128)(2,1)S(1)}, u32[]{:S(2)}, u32[]{:S(2)}) collective-permute-start(bf16[2,256,256]{2,1,0:T(8,128)(2,1)S(1)} %broadcast_select_fusion.4), channel_id=1, source_target_pairs={{0,8},{8,0},{16,24},{24,16},{1,9},{9,1},{17,25},{25,17},{2,10},{10... | collective-permute-start | bytes 786440 | tf_op jit(solution)/shard_map/ppermute | solution.py:238
  54.0 3.2 %collective-permute-start.11 = (bf16[4,256,256]{2,1,0:T(8,128)(2,1)S(1)}, bf16[4,256,256]{2,1,0:T(8,128)(2,1)S(1)}, u32[]{:S(2)}, u32[]{:S(2)}) collective-permute-start(bf16[4,256,256]{2,1,0:T(8,128)(2,1)S(1)} %broadcast_select_fusion.1), channel_id=1, source_target_pairs={{0,1},{1,0},{2,3},{3,2},{4,5},{5,4},{6,7},{7,6},{8,9},{9,8},{10,11... | collective-permute-start | bytes 1572872 | tf_op jit(solution)/shard_map/ppermute | solution.py:238

commit v2 on v1

v2 whole, which is shorter than its diff:
```python
import jax
import jax.numpy as jnp
from jax import lax
from jax.experimental import pallas as pl
from jax.experimental.pallas import tpu as pltpu
from jax.sharding import PartitionSpec as P

PANELS = 2
HIGHEST = lax.Precision.HIGHEST
VMEM_LIMIT = 48 * 1024 * 1024

def spread(row):
    return jnp.broadcast_to(row, (8, row.shape[1]))


def lane(tile, k):
    return jnp.broadcast_to(tile[:, k:k + 1], (8, 128))


def factor_tile(matrix):
    groups = 16
    rows_of = lax.broadcasted_iota(jnp.int32, (8, 128), 0)
    cols_of = lax.broadcasted_iota(jnp.int32, (8, 128), 1)
    left = [matrix[8 * g:8 * g + 8, :] for g in range(groups)]
    right = [(cols_of == rows_of + 8 * g).astype(jnp.float32) for g in range(groups)]
    upper, inverse = [], []
    for s in range(groups):
        y = [spread(left[s][k:k + 1, :]) for k in range(8)]
        v = [spread(right[s][k:k + 1, :]) for k in range(8)]
        d = [[lane(y[i], 8 * s + k) if k >= i else None for k in range(8)] for i in range(8)]
        last = s + 1 == groups
        columns = [[lane(left[g], 8 * s + k) for k in range(8)] for g in range(s + 1, groups)]
        e = list(columns[0]) if not last else None
        ratio = [[None] * 8 for _ in range(8)]
        inv = []
        for k in range(8):
            guess = pl.reciprocal(d[k][k], approx=True)
            correction = 2.0 - d[k][k] * guess
            inv.append(guess * correction)
            if k < 7:
                for j in range(k + 1, 8):
                    d[k + 1][j] = d[k + 1][j] - d[k][k + 1] * guess * d[k][j] * correction
            for i in range(k + 1, 8):
                ratio[i][k] = d[k][i] * inv[k]
                if i > k + 1:
                    for j in range(i, 8):
                        d[i][j] = d[i][j] - ratio[i][k] * d[k][j]
                y[i] = y[i] - ratio[i][k] * y[k]
                v[i] = v[i] - ratio[i][k] * v[k]
            if not last:
                left[s + 1] = left[s + 1] - e[k] * guess * y[k] * correction
                for j in range(k + 1, 8):
                    e[j] = e[j] - e[k] * ratio[j][k]
        up = jnp.zeros((8, 128), jnp.float32)
        low = jnp.zeros((8, 128), jnp.float32)
        for k in range(8):
            root = lax.rsqrt(d[k][k])
            up = jnp.where(rows_of == k, y[k] * root, up)
            low = jnp.where(rows_of == k, v[k] * root, low)
        upper.append(jnp.where(cols_of >= rows_of + 8 * s, up, 0.0))
        inverse.append(low)
        if last:
            break
        x, w = [None] * 8, [None] * 8
        for k in reversed(range(8)):
            x[k] = y[k] * inv[k]
            w[k] = v[k] * inv[k]
            for j in reversed(range(k + 1, 8)):
                x[k] = x[k] - ratio[j][k] * x[j]
                w[k] = w[k] - ratio[j][k] * w[j]
        for g in range(s + 1, groups):
            f = columns[g - s - 1]
            for k in reversed(range(8)):
                if g > s + 1:
                    left[g] = left[g] - f[k] * x[k]
                right[g] = right[g] - f[k] * w[k]
    return jnp.concatenate(upper, axis=0), jnp.concatenate(inverse, axis=0)


def dot(a, b, dims=((1,), (0,))):
    return lax.dot_general(a, b, (dims, ((), ())), precision=HIGHEST, preferred_element_type=jnp.float32)

ROWS = ((1,), (1,))

def factor_rest(upper_1, inv_1, side, rest, lower_ref, inverse_ref):
    half = side.shape[0]
    lower_21 = dot(side, inv_1, ROWS)
    rest = rest - dot(lower_21, lower_21, ROWS)
    beside = dot(lower_21, inv_1)
    upper_2, inv_2 = factor_tile(rest)
    zero = jnp.zeros((half, half), jnp.float32)
    lower_ref[:half, :half] = upper_1.T
    lower_ref[:half, half:] = zero
    lower_ref[half:, :half] = lower_21
    lower_ref[half:, half:] = upper_2.T
    inverse_ref[:half, :half] = inv_1
    inverse_ref[:half, half:] = zero
    inverse_ref[half:, :half] = -dot(inv_2, beside)
    inverse_ref[half:, half:] = inv_2


def mul(a, b, dims=((1,), (0,))):
    return lax.dot_general(a, b, (dims, ((), ())), preferred_element_type=jnp.float32)


def start_kernel(quarter_ref, upper_ref, inverse_ref):
    upper, inverse = factor_tile(quarter_ref[...].astype(jnp.float32))
    upper_ref[...] = upper
    inverse_ref[...] = inverse


def first_kernel(rest_ref, upper_ref, tile_inverse_ref, lower_ref, inverse_ref):
    half = rest_ref.shape[1]
    side = rest_ref[:half].astype(jnp.float32)
    rest = rest_ref[half:].astype(jnp.float32)
    factor_rest(upper_ref[...], tile_inverse_ref[...], side, rest, lower_ref, inverse_ref)


def second_start_kernel(
    top_10_ref, rest_10_ref, rest_01_ref, top_11_ref, rest_11_ref, inverse_0_ref,
    panel_ref, later_ref, upper_ref, inverse_ref,
):
    half = top_11_ref.shape[1]
    left = jnp.concatenate([top_10_ref[...], rest_10_ref[:half]], axis=0).astype(jnp.float32)
    right = jnp.concatenate([rest_01_ref[:half].astype(jnp.float32).T, rest_10_ref[half:].astype(jnp.float32)], axis=0)
    panel = dot(jnp.concatenate([left, right], axis=1), inverse_0_ref[...], ROWS).astype(jnp.bfloat16)
    panel_ref[...] = panel
    above, below = panel[:half], panel[half:]
    top = (top_11_ref[...].astype(jnp.float32) - mul(above, above, ROWS)).astype(jnp.bfloat16)
    later_ref[:half] = (rest_11_ref[:half].astype(jnp.float32) - mul(below, above, ROWS)).astype(jnp.bfloat16)
    later_ref[half:] = (rest_11_ref[half:].astype(jnp.float32) - mul(below, below, ROWS)).astype(jnp.bfloat16)
    upper, inverse = factor_tile(top.astype(jnp.float32))
    upper_ref[...] = upper
    inverse_ref[...] = inverse


def second_kernel(
    rest_ref, upper_ref, tile_inverse_ref, inverse_0_ref, panel_ref, above_0_ref, above_1_ref,
    lower_ref, pieces_0_ref, pieces_1_ref, mirror_ref, later_ref, inverse_ref,
):
    split(inverse_0_ref[...], pieces_0_ref)
    for m in range(above_0_ref.shape[0]):
        mirror = product(pieces_0_ref, above_0_ref[m]).astype(jnp.bfloat16)
        mirror_ref[m] = mirror
        later = above_1_ref[m].astype(jnp.float32) - mul(panel_ref[...], mirror)
        later_ref[m] = later.astype(jnp.bfloat16)
    first_kernel(rest_ref, upper_ref, tile_inverse_ref, lower_ref, inverse_ref)
    split(inverse_ref[...], pieces_1_ref)


def product(pieces_ref, block):
    return sum(mul(pieces_ref[p], block) for p in (2, 1, 0))


def solve(rows, pieces_ref):
    return sum(mul(rows, pieces_ref[p], ROWS) for p in (2, 1, 0))


def split(x, pieces_ref):
    for piece in range(3):
        high = x.astype(jnp.bfloat16)
        pieces_ref[piece] = high
        x = x - high.astype(jnp.float32)


def update_kernel(
    ids_ref, column_0_ref, column_1_ref, blocks_ref, mirror_0_ref, later_ref,
    lower_0_ref, lower_1_ref, pieces_0_ref, pieces_1_ref, panel_10_ref,
    panels_ref, schur_ref, mirror_1_ref,
):
    step = pl.program_id(0)
    batch, col_blocks, width = blocks_ref.shape[:3]

    @pl.when(step == 0)
    def _():
        for m in range(col_blocks):
            mirror_1_ref[m] = product(pieces_1_ref, later_ref[m]).astype(jnp.bfloat16)

    ids = [(step * batch + i) * ids_ref[2] + ids_ref[0] for i in range(batch)]

    def below(solved, panel, lower_ref):
        parts = []
        for i, block_row in enumerate(ids):
            part = jnp.where(block_row > panel, solved[i * width:(i + 1) * width], 0.0)
            panels_ref[i, panel] = jnp.where(block_row == panel, lower_ref[...], part)
            parts.append(part)
        return jnp.concatenate(parts, axis=0).astype(jnp.bfloat16)

    rounded_0 = below(solve(column_0_ref[...].reshape(batch * width, width), pieces_0_ref), 0, lower_0_ref)
    column = column_1_ref[...].reshape(batch * width, width).astype(jnp.float32)
    column = (column - mul(rounded_0, panel_10_ref[...], ROWS)).astype(jnp.bfloat16)
    rounded_1 = below(solve(column, pieces_1_ref), 1, lower_1_ref)
    for m in range(col_blocks):
        change_0 = mul(rounded_0, mirror_0_ref[m])
        change_1 = mul(rounded_1, mirror_1_ref[m])
        for i, block_row in enumerate(ids):
            part = slice(i * width, (i + 1) * width)
            block = blocks_ref[i, m].astype(jnp.float32) - change_0[part]
            block = block.astype(jnp.bfloat16).astype(jnp.float32) - change_1[part]
            keep = (block_row >= PANELS) & (m * ids_ref[3] + ids_ref[1] >= PANELS)
            schur_ref[i, m] = jnp.where(keep, block, 0.0).astype(jnp.bfloat16)


FACTOR_COST = pl.CostEstimate(flops=10**6, bytes_accessed=10**4, transcendentals=0)


def call_factor(kernel, name, shapes, *operands):
    return pl.pallas_call(
        kernel, out_shape=shapes, name=name, cost_estimate=FACTOR_COST,
        compiler_params=pltpu.CompilerParams(vmem_limit_bytes=VMEM_LIMIT),
    )(*operands)


def square(width, dtype=jnp.float32):
    return jax.ShapeDtypeStruct((width, width), dtype)


def update(ids, column_0, column_1, blocks, mirror_0, later, lower_0, lower_1, pieces_0, pieces_1, panel_10):
    row_blocks, col_blocks, width = blocks.shape[:3]
    batch = 2 if row_blocks % 2 == 0 else 1
    rows_spec = pl.BlockSpec((batch, width, width), lambda i: (i, 0, 0))
    square_spec = pl.BlockSpec((width, width), lambda i: (0, 0))
    mirror_spec = pl.BlockSpec((col_blocks, width, width), lambda i: (0, 0, 0))
    pieces_spec = pl.BlockSpec((3, width, width), lambda i: (0, 0, 0))
    block_spec = pl.BlockSpec((batch, col_blocks, width, width), lambda i: (i, 0, 0, 0))
    return pl.pallas_call(
        update_kernel,
        grid=(row_blocks // batch,),
        in_specs=[pl.BlockSpec(memory_space=pltpu.SMEM), rows_spec, rows_spec, block_spec, mirror_spec, mirror_spec]
        + [square_spec] * 2 + [pieces_spec] * 2 + [square_spec],
        out_specs=[pl.BlockSpec((batch, PANELS, width, width), lambda i: (i, 0, 0, 0)), block_spec],
        out_shape=[
            jax.ShapeDtypeStruct((row_blocks, PANELS, width, width), jnp.float32),
            jax.ShapeDtypeStruct(blocks.shape, jnp.bfloat16),
        ],
        scratch_shapes=[pltpu.VMEM((col_blocks, width, width), jnp.bfloat16)],
        compiler_params=pltpu.CompilerParams(vmem_limit_bytes=VMEM_LIMIT),
        cost_estimate=pl.CostEstimate(flops=2 * 10**9, bytes_accessed=6 * 10**6, transcendentals=0),
        name="solve_and_update",
    )(ids, column_0, column_1, blocks, mirror_0, later, lower_0, lower_1, pieces_0, pieces_1, panel_10)


def pack_kernel(kernel_ref, quarters_ref, semaphores):
    half = quarters_ref.shape[1]
    copies = []
    for q, (row, col) in enumerate(((0, 0), (1, 0), (1, 1))):
        source = kernel_ref.at[0, 0, 0, 0, pl.ds(row * half, half), pl.ds(col * half, half)]
        copies.append(pltpu.make_async_copy(source, quarters_ref.at[pl.ds(q * half, half)], semaphores.at[q]))
    for copy in copies:
        copy.start()
    for copy in copies:
        copy.wait()


def pack(kernel):
    half = kernel.shape[-1] // 2
    return pl.pallas_call(
        pack_kernel,
        in_specs=[pl.BlockSpec(memory_space=pltpu.HBM)],
        out_shape=jax.ShapeDtypeStruct((3 * half, half), kernel.dtype),
        scratch_shapes=[pltpu.SemaphoreType.DMA((3,))],
        compiler_params=pltpu.CompilerParams(vmem_limit_bytes=2 * 1024 * 1024),
        name="pack",
    )(kernel)


def swap(block, axis, distance):
    count = lax.axis_size(axis)
    return lax.ppermute(block, axis, [(d, d ^ distance) for d in range(count)])


HOLDERS = ((0, 0), (0, 1), (1, 0), (1, 1))


def diagonal_along(quarters, my_col):
    col_count = lax.axis_size("col")
    along = quarters
    for chip in range(1, col_count // 2):
        pairs = [(r * col_count + core, r * col_count + chip * 2 + core) for r, core in HOLDERS]
        got = lax.ppermute(quarters, ("row", "col"), pairs)
        along = jnp.where(my_col // 2 == chip, got, along)
    return along


def diagonal_down(along, my_row):
    row_count, col_count = lax.axis_size("row"), lax.axis_size("col")
    first, second = along, along
    for step in range(1, row_count):
        pairs = []
        for chip in range(col_count // 2):
            for r, core in HOLDERS:
                col = chip * 2 + core
                pairs.append((r * col_count + col, (step ^ r) * col_count + col))
        got = lax.ppermute(along, ("row", "col"), pairs)
        first = jnp.where(my_row == step, got, first)
        second = jnp.where(my_row == step ^ 1, got, second)
    return jnp.stack([first, second])


def both_cores(pair, my_col):
    other = swap(pair, "col", 1)
    even = my_col % 2 == 0
    left = jnp.where(even, pair, other)
    right = jnp.where(even, other, pair)
    return left[0], right[0], left[1], right[1]


def first_reach(block):
    return block, swap(block, "row", 2)


def other_reaches(block, got, my_row):
    reach = 2
    while True:
        block = jnp.where((my_row >= reach) & (my_row < 2 * reach), got, block)
        reach *= 2
        if reach >= lax.axis_size("row"):
            return block
        got = swap(block, "row", reach)


def by_row(block, other, my_row):
    even = my_row % 2 == 0
    return jnp.where(even, block, other), jnp.where(even, other, block)


def first_stride(block):
    chips = lax.axis_size("col") // 2
    pairs = [(core, core + chips) for core in range(2)]
    return block, lax.ppermute(block, "col", pairs)


def other_strides(block, got, my_col):
    chips = lax.axis_size("col") // 2
    stride = chips // 2
    while True:
        block = jnp.where((my_col // 2) % (2 * stride) == stride, got, block)
        stride //= 2
        if stride == 0:
            return block
        if stride == 1:
            got = swap(block, "col", 2)
        else:
            sources = [chip * 2 + core for chip in range(0, chips, 2 * stride) for core in range(2)]
            got = lax.ppermute(block, "col", [(s, s + 2 * stride) for s in sources])


def per_device(kernel):
    my_row = lax.axis_index("row")
    my_col = lax.axis_index("col")
    even = my_col % 2 == 0
    blocks = kernel[0, :, 0]
    col_blocks, width = blocks.shape[1:3]
    half = width // 2
    quarters = pack(kernel)
    rows, above, _ = lax.optimization_barrier((blocks[:, 0], blocks[0], quarters))
    rows, rows_got = first_stride(rows)
    above, above_got = first_reach(above)
    along = diagonal_along(quarters, my_col)
    pair = diagonal_down(along, my_row)
    pair, rows, rows_got = lax.optimization_barrier((pair, rows, rows_got))
    block_00, block_01, block_10, block_11 = both_cores(pair, my_col)
    rows = other_strides(rows, rows_got, my_col)
    upper_0, tile_inverse_0 = call_factor(start_kernel, "factor_start", [square(half)] * 2, block_00[:half])
    above, above_got, tile_inverse_0 = lax.optimization_barrier((above, above_got, tile_inverse_0))
    above = other_reaches(above, above_got, my_row)
    above_other = swap(above, "row", 1)
    lower_0, inverse_0 = call_factor(
        first_kernel, "factor_first", [square(width)] * 2, block_00[half:], upper_0, tile_inverse_0)
    panel_10, rest_11, upper_1, tile_inverse_1 = call_factor(
        second_start_kernel, "factor_second_start",
        [square(width, jnp.bfloat16), jax.ShapeDtypeStruct((width, half), jnp.bfloat16), square(half), square(half)],
        block_10[:half], block_10[half:], block_01[half:], block_11[:half], block_11[half:], inverse_0)
    rows, above, above_other, tile_inverse_1 = lax.optimization_barrier((rows, above, above_other, tile_inverse_1))
    above_0, above_1 = by_row(above, above_other, my_row)
    other = swap(rows, "col", 1)
    pieces = jax.ShapeDtypeStruct((3, width, width), jnp.bfloat16)
    mirror = jax.ShapeDtypeStruct((col_blocks, width, width), jnp.bfloat16)
    lower_1, pieces_0, pieces_1, mirror_0, later, _ = call_factor(
        second_kernel, "factor_second", [square(width), pieces, pieces, mirror, mirror, square(width)],
        rest_11, upper_1, tile_inverse_1, inverse_0, panel_10, above_0, above_1)
    other, lower_1 = lax.optimization_barrier((other, lower_1))
    column_0 = jnp.where(even, rows, other)
    column_1 = jnp.where(even, other, rows)
    ids = jnp.stack([my_row, my_col, lax.axis_size("row"), lax.axis_size("col")]).astype(jnp.int32)
    panels, schur = update(
        ids, column_0, column_1, blocks, mirror_0, later, lower_0, lower_1, pieces_0, pieces_1, panel_10)
    return (panels[None], schur[None, :, None])


def solution(mesh):
    in_specs = (P("row", None, "col", None, None, None),)
    out_specs = (P("row", None, None, None, None), P("row", None, "col", None, None, None))
    return jax.shard_map(
        per_device, mesh=mesh, in_specs=in_specs, out_specs=out_specs, check_vma=False
    )
```

time: 64.9 us -> 54.6 us (0.84); the launches traced: 63.8 us -> 54.3 us
  Pallas kernels: 34 us -> 26.2 us
  starting transfers between devices: 21.8 us -> 17.6 us
  waiting for transfers between devices: 4.52 us -> 6.69 us
  local copies, waits for them, and re-layouts: 1.14 us -> 2.35 us
  other arithmetic: 1.33 us -> 0.43 us
    pallas_call x3 -> x4, Pallas kernels: 26 us -> 21.6 us  [call_factor(): pl.pallas_call(kernel, out_shape=shapes, name=name, cost_estimate=FACTOR_...]
    ppermute x1, waiting for transfers between devices: 0.01 us -> 3.49 us  [first_stride(): return (block, lax.ppermute(block, 'col', pairs))]
    pallas_call x2, Pallas kernels: 8.05 us -> 4.56 us  [the longest x1 4.51 us: update(): pl.pallas_call(update_kernel, grid=(row_blocks // batch,), in_specs=[pl.B...]
    ppermute x5, starting transfers between devices: 5.85 us -> 3.09 us  [swap(): return lax.ppermute(block, axis, [(d, d ^ distance) for d in range(count)])]
    ppermute x3, waiting for transfers between devices: 0.01 us -> 1.88 us  [diagonal_down(): got = lax.ppermute(along, ('row', 'col'), pairs)]
    ppermute x3, waiting for transfers between devices: 2.05 us -> 0.37 us  [diagonal_along(): got = lax.ppermute(quarters, ('row', 'col'), pairs)]
    ppermute x5, waiting for transfers between devices: 2.46 us -> 0.94 us  [swap(): return lax.ppermute(block, axis, [(d, d ^ distance) for d in range(count)])]
    ppermute x1, starting transfers between devices: 2.83 us -> 1.32 us  [first_stride(): return (block, lax.ppermute(block, 'col', pairs))]
  transfers between devices with their start and end apart: 12 -> 12, of which waited for: 3 -> 5; matrix products, arithmetic and copies ran while one was open for 2% -> 3% of each run, Pallas kernels for 41% -> 40%
where the time goes in v2:
time: 54.6 us; the launch traced here: 54.3 us
  Pallas kernels  26.2 us (48%)
  starting transfers between devices  17.6 us (32%)
  waiting for transfers between devices  6.69 us (12%)
  local copies, waits for them, and re-layouts  2.35 us (4%)
  between operations  0.95 us (2%)
    pallas_call x4, Pallas kernels, call_factor(): pl.pallas_call(kernel, out_shape=shapes, name=name, cost_estimate=FACTOR_...  21.6 us
    ppermute x3, starting transfers between devices, diagonal_along(): got = lax.ppermute(quarters, ('row', 'col'), pairs)  7.53 us
    ppermute x3, starting transfers between devices, diagonal_down(): got = lax.ppermute(along, ('row', 'col'), pairs)  5.71 us
    pallas_call x1, Pallas kernels, update(): pl.pallas_call(update_kernel, grid=(row_blocks // batch,), in_specs=[pl.B...  4.51 us
    ppermute x1, waiting for transfers between devices, first_stride(): return (block, lax.ppermute(block, 'col', pairs))  3.49 us
    ppermute x5, starting transfers between devices, swap(): return lax.ppermute(block, axis, [(d, d ^ distance) for d in range(count)])  3.09 us
    ppermute x3, waiting for transfers between devices, diagonal_down(): got = lax.ppermute(along, ('row', 'col'), pairs)  1.88 us
    ppermute x1, starting transfers between devices, first_stride(): return (block, lax.ppermute(block, 'col', pairs))  1.32 us
  transfers between devices with their start and end apart: 12, of which 5 were waited for; matrix products, arithmetic and copies ran while one was open for 3% of the time, Pallas kernels for 40%

profile of v2, /device:TPU:1, one launch (start us, length us, event | category | flops | bytes accessed | tf_op | source)
XLA Modules:
  0.0 54.3 jit_solution(5663731572034560996)
XLA Ops:
  0.6 0.0 copy-start
  0.6 1.2 %copy-done = bf16[1,4,1,2,256,256]{5,4,3,2,1,0:T(8,128)(2,1)S(1)} copy-done((bf16[1,4,1,2,256,256]{5,4,3,2,1,0:T(8,128)(2,1)S(1)}, bf16[1,4,1,2,256,256]{5,4,3,2,1,0:T(8,128)(2,1)}, u32[]{:S(2)}) %copy-start) | copy-done | bytes 1048600
  1.9 0.1 pack.1
  1.9 4.2 %collective-permute-start.2 = (bf16[384,128]{1,0:T(8,128)(2,1)S(1)}, bf16[384,128]{1,0:T(8,128)(2,1)S(1)}, u32[]{:S(2)}, u32[]{:S(2)}) collective-permute-start(bf16[384,128]{1,0:T(8,128)(2,1)S(1)} %pack.1), channel_id=1, source_target_pairs={{0,2},{1,3},{8,10},{9,11}} | collective-permute-start | bytes 294920 | tf_op jit(solution)/shard_map/ppermute | solution.py:280
  6.1 1.7 %collective-permute-start.1 = (bf16[384,128]{1,0:T(8,128)(2,1)S(1)}, bf16[384,128]{1,0:T(8,128)(2,1)S(1)}, u32[]{:S(2)}, u32[]{:S(2)}) collective-permute-start(bf16[384,128]{1,0:T(8,128)(2,1)S(1)} %pack.1), channel_id=1, source_target_pairs={{0,4},{1,5},{8,12},{9,13}} | collective-permute-start | bytes 294920 | tf_op jit(solution)/shard_map/ppermute | solution.py:280
  7.8 1.7 %collective-permute-start = (bf16[384,128]{1,0:T(8,128)(2,1)S(1)}, bf16[384,128]{1,0:T(8,128)(2,1)S(1)}, u32[]{:S(2)}, u32[]{:S(2)}) collective-permute-start(bf16[384,128]{1,0:T(8,128)(2,1)S(1)} %pack.1), channel_id=1, source_target_pairs={{0,6},{1,7},{8,14},{9,15}} | collective-permute-start | bytes 294920 | tf_op jit(solution)/shard_map/ppermute | solution.py:280
  9.5 1.1 %slice_bitcast_fusion = bf16[4,256,256]{2,1,0:T(8,128)(2,1)S(1)} fusion(bf16[4,2,256,256]{3,2,1,0:T(8,128)(2,1)} %bitcast.29), kind=kLoop, calls=%fused_computation | loop fusion | bytes 1048576 | tf_op jit(solution)/shard_map/squeeze | solution.py:356
  10.6 1.3 %collective-permute-start.6 = (bf16[4,256,256]{2,1,0:T(8,128)(2,1)S(1)}, bf16[4,256,256]{2,1,0:T(8,128)(2,1)S(1)}, u32[]{:S(2)}, u32[]{:S(2)}) collective-permute-start(bf16[4,256,256]{2,1,0:T(8,128)(2,1)S(1)} %slice_bitcast_fusion), channel_id=1, source_target_pairs={{0,4},{1,5},{8,12},{9,13},{16,20},{17,21},{24,28},{25,29}} | collective-permute-start | bytes 1572872 | tf_op jit(solution)/shard_map/ppermute | solution.py:330
  12.0 0.4 collective-permute-done
  12.3 3.1 %collective-permute-start.5 = (bf16[384,128]{1,0:T(8,128)(2,1)S(1)}, bf16[384,128]{1,0:T(8,128)(2,1)S(1)}, u32[]{:S(2)}, u32[]{:S(2)}) collective-permute-start(bf16[384,128]{1,0:T(8,128)(2,1)S(1)} %select_select_fusion), channel_id=1, source_target_pairs={{0,8},{1,9},{8,0},{9,1},{2,10},{3,11},{10,2},{11,3},{4,12},{5,13},... | collective-permute-start | bytes 294920 | tf_op jit(solution)/shard_map/ppermute | solution.py:294
  15.5 1.3 %collective-permute-start.4 = (bf16[384,128]{1,0:T(8,128)(2,1)S(1)}, bf16[384,128]{1,0:T(8,128)(2,1)S(1)}, u32[]{:S(2)}, u32[]{:S(2)}) collective-permute-start(bf16[384,128]{1,0:T(8,128)(2,1)S(1)} %select_select_fusion), channel_id=1, source_target_pairs={{0,16},{1,17},{8,24},{9,25},{2,18},{3,19},{10,26},{11,27},{4,20},{... | collective-permute-start | bytes 294920 | tf_op jit(solution)/shard_map/ppermute | solution.py:294
  16.8 1.3 %collective-permute-start.3 = (bf16[384,128]{1,0:T(8,128)(2,1)S(1)}, bf16[384,128]{1,0:T(8,128)(2,1)S(1)}, u32[]{:S(2)}, u32[]{:S(2)}) collective-permute-start(bf16[384,128]{1,0:T(8,128)(2,1)S(1)} %select_select_fusion), channel_id=1, source_target_pairs={{0,24},{1,25},{8,16},{9,17},{2,26},{3,27},{10,18},{11,19},{4,28},{... | collective-permute-start | bytes 294920 | tf_op jit(solution)/shard_map/ppermute | solution.py:294
  18.1 0.1 collective-permute-start.8
  18.2 0.0 collective-permute-done.5
  18.2 0.2 collective-permute-done.4
  18.4 1.7 %collective-permute-done.3 = bf16[384,128]{1,0:T(8,128)(2,1)S(1)} collective-permute-done((bf16[384,128]{1,0:T(8,128)(2,1)S(1)}, bf16[384,128]{1,0:T(8,128)(2,1)S(1)}, u32[]{:S(2)}, u32[]{:S(2)}) %collective-permute-start.3) | collective-permute-done | bytes 98336 | tf_op jit(solution)/shard_map/ppermute | solution.py:294
  20.2 3.5 %collective-permute-done.6 = bf16[4,256,256]{2,1,0:T(8,128)(2,1)S(1)} collective-permute-done((bf16[4,256,256]{2,1,0:T(8,128)(2,1)S(1)}, bf16[4,256,256]{2,1,0:T(8,128)(2,1)S(1)}, u32[]{:S(2)}, u32[]{:S(2)}) %collective-permute-start.6) | collective-permute-done | bytes 524320 | tf_op jit(solution)/shard_map/ppermute | solution.py:330
  23.7 0.9 %collective-permute-start.9 = (bf16[2,384,128]{2,1,0:T(8,128)(2,1)S(1)}, bf16[2,384,128]{2,1,0:T(8,128)(2,1)S(1)}, u32[]{:S(2)}, u32[]{:S(2)}) collective-permute-start(bf16[2,384,128]{2,1,0:T(8,128)(2,1)S(1)} %pad_maximum_fusion), channel_id=1, source_target_pairs={{0,1},{1,0},{2,3},{3,2},{4,5},{5,4},{6,7},{7,6},{8,9},{9,8},{10,11... | collective-permute-start | bytes 589832 | tf_op jit(solution)/shard_map/ppermute | solution.py:269
  24.6 0.1 broadcast_select_fusion
  24.7 0.1 collective-permute-start.7
  24.7 0.9 %collective-permute-done.9 = bf16[2,384,128]{2,1,0:T(8,128)(2,1)S(1)} collective-permute-done((bf16[2,384,128]{2,1,0:T(8,128)(2,1)S(1)}, bf16[2,384,128]{2,1,0:T(8,128)(2,1)S(1)}, u32[]{:S(2)}, u32[]{:S(2)}) %collective-permute-start.9) | collective-permute-done | bytes 196640 | tf_op jit(solution)/shard_map/ppermute | solution.py:269
  25.7 4.3 %factor_start.1 = (f32[128,128]{1,0:T(8,128)S(1)}, f32[128,128]{1,0:T(8,128)S(1)}) custom-call(bf16[128,128]{1,0:T(8,128)(2,1)S(1)} %get-tuple-element.75.quarter_ref), custom_call_target="tpu_custom_call" | custom-call | flops 1000000 | bytes 10000 | tf_op jit(solution)/shard_map/factor_start/pallas_call | solution.py:208
  30.1 0.0 collective-permute-done.8
  30.1 1.3 %collective-permute-start.10 = (bf16[2,256,256]{2,1,0:T(8,128)(2,1)S(1)}, bf16[2,256,256]{2,1,0:T(8,128)(2,1)S(1)}, u32[]{:S(2)}, u32[]{:S(2)}) collective-permute-start(bf16[2,256,256]{2,1,0:T(8,128)(2,1)S(1)} %broadcast_select_fusion.6), channel_id=1, source_target_pairs={{0,8},{8,0},{16,24},{24,16},{1,9},{9,1},{17,25},{25,17},{2,10},{10... | collective-permute-start | bytes 786440 | tf_op jit(solution)/shard_map/ppermute | solution.py:269
  31.4 5.3 %factor_first.1 = (f32[256,256]{1,0:T(8,128)S(1)}, f32[256,256]{1,0:T(8,128)S(1)}) custom-call(bf16[256,128]{1,0:T(8,128)(2,1)S(1)} %get-tuple-element.70.rest_ref, f32[128,128]{1,0:T(8,128)S(1)} %get-tuple-element.39.upper_ref, f32[128,128]{1,0:T(8,128)S(1)} %get-tuple-element.40.tile_inverse_ref), custom_call_target="tpu_custom_call" | custom-call | flops 1000000 | bytes 10000 | tf_op jit(solution)/shard_map/factor_first/pallas_call | solution.py:208
  36.8 5.1 %factor_second_start.1 = (bf16[256,256]{1,0:T(8,128)(2,1)S(1)}, bf16[256,128]{1,0:T(8,128)(2,1)S(1)}, f32[128,128]{1,0:T(8,128)S(1)}, f32[128,128]{1,0:T(8,128)S(1)}) custom-call(bf16[128,128]{1,0:T(8,128)(2,1)S(1)} %get-tuple-element.74.top_10_ref, bf16[256,128]{1,0:T(8,128)(2,1)S(1)} %get-tuple-element.71.rest_10_ref, ...), custom_call_target="tpu_custom_call" | custom-call | flops 1000000 | bytes 10000 | tf_op jit(solution)/shard_map/factor_second_start/pallas_call | solution.py:208
  41.9 0.1 broadcast_select_fusion.1
  42.0 0.7 %collective-permute-start.11 = (bf16[4,256,256]{2,1,0:T(8,128)(2,1)S(1)}, bf16[4,256,256]{2,1,0:T(8,128)(2,1)S(1)}, u32[]{:S(2)}, u32[]{:S(2)}) collective-permute-start(bf16[4,256,256]{2,1,0:T(8,128)(2,1)S(1)} %broadcast_select_fusion.1), channel_id=1, source_target_pairs={{0,1},{1,0},{2,3},{3,2},{4,5},{5,4},{6,7},{7,6},{8,9},{9,8},{10,11... | collective-permute-start | bytes 1572872 | tf_op jit(solution)/shard_map/ppermute | solution.py:269
  42.7 0.1 pad_add_fusion.ids_ref
  42.8 6.9 %factor_second.1 = (f32[256,256]{1,0:T(8,128)S(1)}, bf16[3,256,256]{2,1,0:T(8,128)(2,1)S(1)}, bf16[3,256,256]{2,1,0:T(8,128)(2,1)S(1)}, bf16[2,256,256]{2,1,0:T(...) custom-call(bf16[256,128]{1,0:T(8,128)(2,1)S(1)} %get-tuple-element.44.rest_ref, ...), custom_call_target="tpu_custom_call" | custom-call | flops 1000000 | bytes 10000 | tf_op jit(solution)/shard_map/factor_second/pallas_call | solution.py:208
  49.7 0.1 broadcast_select_fusion.2
  49.8 4.5 %solve_and_update.1 = (f32[4,2,256,256]{3,2,1,0:T(8,128)}, bf16[4,2,256,256]{3,2,1,0:T(8,128)(2,1)}) custom-call(s32[4]{0:T(128)S(1)} %pad_add_fusion.ids_ref, bf16[4,256,256]{2,1,0:T(8,128)(2,1)S(1)} %get-tuple-element.63.column_0_ref, bf16[4,256,256]{2,1,0:T(8,128)(2,1)S(1)} %get-tuple-element.62.column_1_ref, bf16[4,2,256,256]{3,2,1,0:T(8,128)(2,1)S(1)} %bitcast.30, ...), custom_call_target="tpu_custom_call" | custom-call | flops 2000000000 | bytes 6000000 | tf_op jit(solution)/shard_map/solve_and_update/pallas_call | solution.py:226
  (17 shorter events, 0.2 us)
Async XLA Ops:
  0.6 1.2 %copy-start = (bf16[1,4,1,2,256,256]{5,4,3,2,1,0:T(8,128)(2,1)S(1)}, bf16[1,4,1,2,256,256]{5,4,3,2,1,0:T(8,128)(2,1)}, u32[]{:S(2)}) copy-start(bf16[1,4,1,2,256,256]{5,4,3,2,1,0:T(8,128)(2,1)} %kernel_ref.1) | copy-start | bytes 3145732
  1.9 8.7 %copy-start.1 = (bf16[1,4,1,2,256,256]{5,4,3,2,1,0:T(8,128)(2,1)S(1)}, bf16[1,4,1,2,256,256]{5,4,3,2,1,0:T(8,128)(2,1)}, u32[]{:S(2)}) copy-start(bf16[1,4,1,2,256,256]{5,4,3,2,1,0:T(8,128)(2,1)} %kernel_ref.1) | copy-start | bytes 3145732
  1.9 10.0 %collective-permute-start.2 = (bf16[384,128]{1,0:T(8,128)(2,1)S(1)}, bf16[384,128]{1,0:T(8,128)(2,1)S(1)}, u32[]{:S(2)}, u32[]{:S(2)}) collective-permute-start(bf16[384,128]{1,0:T(8,128)(2,1)S(1)} %pack.1), channel_id=1, source_target_pairs={{0,2},{1,3},{8,10},{9,11}} | collective-permute-start | bytes 294920 | tf_op jit(solution)/shard_map/ppermute | solution.py:280
  6.1 5.9 %collective-permute-start.1 = (bf16[384,128]{1,0:T(8,128)(2,1)S(1)}, bf16[384,128]{1,0:T(8,128)(2,1)S(1)}, u32[]{:S(2)}, u32[]{:S(2)}) collective-permute-start(bf16[384,128]{1,0:T(8,128)(2,1)S(1)} %pack.1), channel_id=1, source_target_pairs={{0,4},{1,5},{8,12},{9,13}} | collective-permute-start | bytes 294920 | tf_op jit(solution)/shard_map/ppermute | solution.py:280
  7.8 4.5 %collective-permute-start = (bf16[384,128]{1,0:T(8,128)(2,1)S(1)}, bf16[384,128]{1,0:T(8,128)(2,1)S(1)}, u32[]{:S(2)}, u32[]{:S(2)}) collective-permute-start(bf16[384,128]{1,0:T(8,128)(2,1)S(1)} %pack.1), channel_id=1, source_target_pairs={{0,6},{1,7},{8,14},{9,15}} | collective-permute-start | bytes 294920 | tf_op jit(solution)/shard_map/ppermute | solution.py:280
  10.6 13.1 %collective-permute-start.6 = (bf16[4,256,256]{2,1,0:T(8,128)(2,1)S(1)}, bf16[4,256,256]{2,1,0:T(8,128)(2,1)S(1)}, u32[]{:S(2)}, u32[]{:S(2)}) collective-permute-start(bf16[4,256,256]{2,1,0:T(8,128)(2,1)S(1)} %slice_bitcast_fusion), channel_id=1, source_target_pairs={{0,4},{1,5},{8,12},{9,13},{16,20},{17,21},{24,28},{25,29}} | collective-permute-start | bytes 1572872 | tf_op jit(solution)/shard_map/ppermute | solution.py:330
  12.3 5.9 %collective-permute-start.5 = (bf16[384,128]{1,0:T(8,128)(2,1)S(1)}, bf16[384,128]{1,0:T(8,128)(2,1)S(1)}, u32[]{:S(2)}, u32[]{:S(2)}) collective-permute-start(bf16[384,128]{1,0:T(8,128)(2,1)S(1)} %select_select_fusion), channel_id=1, source_target_pairs={{0,8},{1,9},{8,0},{9,1},{2,10},{3,11},{10,2},{11,3},{4,12},{5,13},... | collective-permute-start | bytes 294920 | tf_op jit(solution)/shard_map/ppermute | solution.py:294
  15.5 2.9 %collective-permute-start.4 = (bf16[384,128]{1,0:T(8,128)(2,1)S(1)}, bf16[384,128]{1,0:T(8,128)(2,1)S(1)}, u32[]{:S(2)}, u32[]{:S(2)}) collective-permute-start(bf16[384,128]{1,0:T(8,128)(2,1)S(1)} %select_select_fusion), channel_id=1, source_target_pairs={{0,16},{1,17},{8,24},{9,25},{2,18},{3,19},{10,26},{11,27},{4,20},{... | collective-permute-start | bytes 294920 | tf_op jit(solution)/shard_map/ppermute | solution.py:294
  16.8 3.3 %collective-permute-start.3 = (bf16[384,128]{1,0:T(8,128)(2,1)S(1)}, bf16[384,128]{1,0:T(8,128)(2,1)S(1)}, u32[]{:S(2)}, u32[]{:S(2)}) collective-permute-start(bf16[384,128]{1,0:T(8,128)(2,1)S(1)} %select_select_fusion), channel_id=1, source_target_pairs={{0,24},{1,25},{8,16},{9,17},{2,26},{3,27},{10,18},{11,19},{4,28},{... | collective-permute-start | bytes 294920 | tf_op jit(solution)/shard_map/ppermute | solution.py:294
  18.1 12.0 %collective-permute-start.8 = (bf16[2,256,256]{2,1,0:T(8,128)(2,1)S(1)}, bf16[2,256,256]{2,1,0:T(8,128)(2,1)S(1)}, u32[]{:S(2)}, u32[]{:S(2)}) collective-permute-start(bf16[2,256,256]{2,1,0:T(8,128)(2,1)S(1)} %slice_bitcast_fusion.1), channel_id=1, source_target_pairs={{0,16},{8,24},{16,0},{24,8},{1,17},{9,25},{17,1},{25,9},{2,18},{10... | collective-permute-start | bytes 786440 | tf_op jit(solution)/shard_map/ppermute | solution.py:269
  23.7 2.0 %collective-permute-start.9 = (bf16[2,384,128]{2,1,0:T(8,128)(2,1)S(1)}, bf16[2,384,128]{2,1,0:T(8,128)(2,1)S(1)}, u32[]{:S(2)}, u32[]{:S(2)}) collective-permute-start(bf16[2,384,128]{2,1,0:T(8,128)(2,1)S(1)} %pad_maximum_fusion), channel_id=1, source_target_pairs={{0,1},{1,0},{2,3},{3,2},{4,5},{5,4},{6,7},{7,6},{8,9},{9,8},{10,11... | collective-permute-start | bytes 589832 | tf_op jit(solution)/shard_map/ppermute | solution.py:269
  24.7 17.2 %collective-permute-start.7 = (bf16[4,256,256]{2,1,0:T(8,128)(2,1)S(1)}, bf16[4,256,256]{2,1,0:T(8,128)(2,1)S(1)}, u32[]{:S(2)}, u32[]{:S(2)}) collective-permute-start(bf16[4,256,256]{2,1,0:T(8,128)(2,1)S(1)} %broadcast_select_fusion), channel_id=1, source_target_pairs={{0,2},{1,3},{2,0},{3,1},{4,6},{5,7},{6,4},{7,5},{8,10},{9,11},{10,... | collective-permute-start | bytes 1572872 | tf_op jit(solution)/shard_map/ppermute | solution.py:269
  30.1 11.8 %collective-permute-start.10 = (bf16[2,256,256]{2,1,0:T(8,128)(2,1)S(1)}, bf16[2,256,256]{2,1,0:T(8,128)(2,1)S(1)}, u32[]{:S(2)}, u32[]{:S(2)}) collective-permute-start(bf16[2,256,256]{2,1,0:T(8,128)(2,1)S(1)} %broadcast_select_fusion.6), channel_id=1, source_target_pairs={{0,8},{8,0},{16,24},{24,16},{1,9},{9,1},{17,25},{25,17},{2,10},{10... | collective-permute-start | bytes 786440 | tf_op jit(solution)/shard_map/ppermute | solution.py:269
  42.0 7.7 %collective-permute-start.11 = (bf16[4,256,256]{2,1,0:T(8,128)(2,1)S(1)}, bf16[4,256,256]{2,1,0:T(8,128)(2,1)S(1)}, u32[]{:S(2)}, u32[]{:S(2)}) collective-permute-start(bf16[4,256,256]{2,1,0:T(8,128)(2,1)S(1)} %broadcast_select_fusion.1), channel_id=1, source_target_pairs={{0,1},{1,0},{2,3},{3,2},{4,5},{5,4},{6,7},{7,6},{8,9},{9,8},{10,11... | collective-permute-start | bytes 1572872 | tf_op jit(solution)/shard_map/ppermute | solution.py:269

commit v3 on v2

--- a/solution.py
+++ b/solution.py
@@ -7,7 +7,7 @@
 
 PANELS = 2
 HIGHEST = lax.Precision.HIGHEST
-VMEM_LIMIT = 48 * 1024 * 1024
+VMEM_LIMIT = 20 * 1024 * 1024
 
 def spread(row):
     return jnp.broadcast_to(row, (8, row.shape[1]))
@@ -17,7 +17,7 @@
     return jnp.broadcast_to(tile[:, k:k + 1], (8, 128))
 
 
-def factor_tile(matrix):
+def factor_tile(matrix, tasks=()):
     groups = 16
     rows_of = lax.broadcasted_iota(jnp.int32, (8, 128), 0)
     cols_of = lax.broadcasted_iota(jnp.int32, (8, 128), 1)
@@ -34,21 +34,15 @@
         ratio = [[None] * 8 for _ in range(8)]
         inv = []
         for k in range(8):
-            guess = pl.reciprocal(d[k][k], approx=True)
-            correction = 2.0 - d[k][k] * guess
-            inv.append(guess * correction)
-            if k < 7:
-                for j in range(k + 1, 8):
-                    d[k + 1][j] = d[k + 1][j] - d[k][k + 1] * guess * d[k][j] * correction
+            inv.append(pl.reciprocal(d[k][k], approx=True))
             for i in range(k + 1, 8):
                 ratio[i][k] = d[k][i] * inv[k]
-                if i > k + 1:
-                    for j in range(i, 8):
-                        d[i][j] = d[i][j] - ratio[i][k] * d[k][j]
+                for j in range(i, 8):
+                    d[i][j] = d[i][j] - ratio[i][k] * d[k][j]
                 y[i] = y[i] - ratio[i][k] * y[k]
                 v[i] = v[i] - ratio[i][k] * v[k]
             if not last:
-                left[s + 1] = left[s + 1] - e[k] * guess * y[k] * correction
+                left[s + 1] = left[s + 1] - e[k] * inv[k] * y[k]
                 for j in range(k + 1, 8):
                     e[j] = e[j] - e[k] * ratio[j][k]
         up = jnp.zeros((8, 128), jnp.float32)
@@ -59,6 +53,8 @@
             low = jnp.where(rows_of == k, v[k] * root, low)
         upper.append(jnp.where(cols_of >= rows_of + 8 * s, up, 0.0))
         inverse.append(low)
+        if s < len(tasks):
+            tasks[s]()
         if last:
             break
         x, w = [None] * 8, [None] * 8
@@ -82,25 +78,49 @@
 
 ROWS = ((1,), (1,))
 
-def factor_rest(upper_1, inv_1, side, rest, lower_ref, inverse_ref):
-    half = side.shape[0]
-    lower_21 = dot(side, inv_1, ROWS)
-    rest = rest - dot(lower_21, lower_21, ROWS)
-    beside = dot(lower_21, inv_1)
-    upper_2, inv_2 = factor_tile(rest)
-    zero = jnp.zeros((half, half), jnp.float32)
-    lower_ref[:half, :half] = upper_1.T
-    lower_ref[:half, half:] = zero
-    lower_ref[half:, :half] = lower_21
-    lower_ref[half:, half:] = upper_2.T
-    inverse_ref[:half, :half] = inv_1
-    inverse_ref[:half, half:] = zero
-    inverse_ref[half:, :half] = -dot(inv_2, beside)
-    inverse_ref[half:, half:] = inv_2
-
-
 def mul(a, b, dims=((1,), (0,))):
     return lax.dot_general(a, b, (dims, ((), ())), preferred_element_type=jnp.float32)
+
+
+def split(x):
+    pieces = []
+    for _ in range(3):
+        pieces.append(x.astype(jnp.bfloat16))
+        x = x - pieces[-1].astype(jnp.float32)
+    return pieces
+
+
+def product(pieces, block):
+    return sum(mul(pieces[p], block) for p in (2, 1, 0))
+
+
+def solve(rows, pieces):
+    return sum(mul(rows, pieces[p], ROWS) for p in (2, 1, 0))
+
+
+def factor_rest(upper_1, inv_1, side, rest, lower_ref, pieces_ref, tasks=()):
+    half = side.shape[0]
+    pieces = split(inv_1)
+    lower_21 = solve(side, pieces)
+    rest = rest.astype(jnp.float32) - dot(lower_21, lower_21, ROWS)
+    beside = dot(lower_21, inv_1)
+
+    def store_left():
+        lower_ref[half:, :half] = lower_21
+        lower_ref[:half, half:] = jnp.zeros((half, half), jnp.float32)
+        lower_ref[:half, :half] = upper_1.T
+
+    def store_pieces():
+        for p in range(3):
+            pieces_ref[p, :half, :half] = pieces[p]
+            pieces_ref[p, :half, half:] = jnp.zeros((half, half), jnp.bfloat16)
+
+    upper_2, inv_2 = factor_tile(rest, [store_left, store_pieces] + list(tasks))
+    inv_21 = -dot(inv_2, beside)
+    lower_ref[half:, half:] = upper_2.T
+    for p, (left, right) in enumerate(zip(split(inv_21), split(inv_2))):
+        pieces_ref[p, half:, :half] = left
+        pieces_ref[p, half:, half:] = right
 
 
 def start_kernel(quarter_ref, upper_ref, inverse_ref):
@@ -109,58 +129,54 @@
     inverse_ref[...] = inverse
 
 
-def first_kernel(rest_ref, upper_ref, tile_inverse_ref, lower_ref, inverse_ref):
+def first_kernel(rest_ref, upper_ref, tile_inverse_ref, lower_ref, pieces_ref):
     half = rest_ref.shape[1]
-    side = rest_ref[:half].astype(jnp.float32)
-    rest = rest_ref[half:].astype(jnp.float32)
-    factor_rest(upper_ref[...], tile_inverse_ref[...], side, rest, lower_ref, inverse_ref)
+    factor_rest(upper_ref[...], tile_inverse_ref[...], rest_ref[:half], rest_ref[half:], lower_ref, pieces_ref)
 
 
 def second_start_kernel(
-    top_10_ref, rest_10_ref, rest_01_ref, top_11_ref, rest_11_ref, inverse_0_ref,
+    top_10_ref, rest_10_ref, rest_01_ref, top_11_ref, rest_11_ref, pieces_0_ref,
     panel_ref, later_ref, upper_ref, inverse_ref,
 ):
     half = top_11_ref.shape[1]
-    left = jnp.concatenate([top_10_ref[...], rest_10_ref[:half]], axis=0).astype(jnp.float32)
-    right = jnp.concatenate([rest_01_ref[:half].astype(jnp.float32).T, rest_10_ref[half:].astype(jnp.float32)], axis=0)
-    panel = dot(jnp.concatenate([left, right], axis=1), inverse_0_ref[...], ROWS).astype(jnp.bfloat16)
-    panel_ref[...] = panel
+    corner = rest_01_ref[:half].astype(jnp.float32).T.astype(jnp.bfloat16)
+    left = jnp.concatenate([top_10_ref[...], rest_10_ref[:half]], axis=0)
+    right = jnp.concatenate([corner, rest_10_ref[half:]], axis=0)
+    panel = solve(jnp.concatenate([left, right], axis=1), pieces_0_ref).astype(jnp.bfloat16)
     above, below = panel[:half], panel[half:]
     top = (top_11_ref[...].astype(jnp.float32) - mul(above, above, ROWS)).astype(jnp.bfloat16)
-    later_ref[:half] = (rest_11_ref[:half].astype(jnp.float32) - mul(below, above, ROWS)).astype(jnp.bfloat16)
-    later_ref[half:] = (rest_11_ref[half:].astype(jnp.float32) - mul(below, below, ROWS)).astype(jnp.bfloat16)
-    upper, inverse = factor_tile(top.astype(jnp.float32))
+
+    def side():
+        panel_ref[...] = panel
+        later_ref[:half] = (rest_11_ref[:half].astype(jnp.float32) - mul(below, above, ROWS)).astype(jnp.bfloat16)
+
+    def rest():
+        later_ref[half:] = (rest_11_ref[half:].astype(jnp.float32) - mul(below, below, ROWS)).astype(jnp.bfloat16)
+
+    upper, inverse = factor_tile(top.astype(jnp.float32), (side, rest))
     upper_ref[...] = upper
     inverse_ref[...] = inverse
 
 
 def second_kernel(
-    rest_ref, upper_ref, tile_inverse_ref, inverse_0_ref, panel_ref, above_0_ref, above_1_ref,
-    lower_ref, pieces_0_ref, pieces_1_ref, mirror_ref, later_ref, inverse_ref,
+    rest_ref, upper_ref, tile_inverse_ref, pieces_0_ref, panel_ref, above_0_ref, above_1_ref,
+    lower_ref, pieces_1_ref, mirror_ref, later_ref,
 ):
-    split(inverse_0_ref[...], pieces_0_ref)
+    half = rest_ref.shape[1]
+    tasks = []
     for m in range(above_0_ref.shape[0]):
-        mirror = product(pieces_0_ref, above_0_ref[m]).astype(jnp.bfloat16)
-        mirror_ref[m] = mirror
-        later = above_1_ref[m].astype(jnp.float32) - mul(panel_ref[...], mirror)
-        later_ref[m] = later.astype(jnp.bfloat16)
-    first_kernel(rest_ref, upper_ref, tile_inverse_ref, lower_ref, inverse_ref)
-    split(inverse_ref[...], pieces_1_ref)
-
-
-def product(pieces_ref, block):
-    return sum(mul(pieces_ref[p], block) for p in (2, 1, 0))
-
-
-def solve(rows, pieces_ref):
-    return sum(mul(rows, pieces_ref[p], ROWS) for p in (2, 1, 0))
-
-
-def split(x, pieces_ref):
-    for piece in range(3):
-        high = x.astype(jnp.bfloat16)
-        pieces_ref[piece] = high
-        x = x - high.astype(jnp.float32)
+        for part in (pl.ds(0, half), pl.ds(half, half)):
+            def mirror(m=m, part=part):
+                mirror_ref[m, part] = sum(mul(pieces_0_ref[p, part], above_0_ref[m]) for p in (2, 1, 0)).astype(jnp.bfloat16)
+            tasks.append(mirror)
+    for m in range(above_0_ref.shape[0]):
+        for part in (pl.ds(0, half), pl.ds(half, half)):
+            def later(m=m, part=part):
+                change = mul(panel_ref[part], mirror_ref[m])
+                later_ref[m, part] = (above_1_ref[m, part].astype(jnp.float32) - change).astype(jnp.bfloat16)
+            tasks.append(later)
+    factor_rest(
+        upper_ref[...], tile_inverse_ref[...], rest_ref[:half], rest_ref[half:], lower_ref, pieces_1_ref, tasks)
 
 
 def update_kernel(
@@ -283,15 +299,9 @@
 
 
 def diagonal_down(along, my_row):
-    row_count, col_count = lax.axis_size("row"), lax.axis_size("col")
     first, second = along, along
-    for step in range(1, row_count):
-        pairs = []
-        for chip in range(col_count // 2):
-            for r, core in HOLDERS:
-                col = chip * 2 + core
-                pairs.append((r * col_count + col, (step ^ r) * col_count + col))
-        got = lax.ppermute(along, ("row", "col"), pairs)
+    for step in range(1, lax.axis_size("row")):
+        got = swap(along, "row", step)
         first = jnp.where(my_row == step, got, first)
         second = jnp.where(my_row == step ^ 1, got, second)
     return jnp.stack([first, second])
@@ -365,20 +375,20 @@
     above, above_got, tile_inverse_0 = lax.optimization_barrier((above, above_got, tile_inverse_0))
     above = other_reaches(above, above_got, my_row)
     above_other = swap(above, "row", 1)
-    lower_0, inverse_0 = call_factor(
-        first_kernel, "factor_first", [square(width)] * 2, block_00[half:], upper_0, tile_inverse_0)
+    pieces = jax.ShapeDtypeStruct((3, width, width), jnp.bfloat16)
+    lower_0, pieces_0 = call_factor(
+        first_kernel, "factor_first", [square(width), pieces], block_00[half:], upper_0, tile_inverse_0)
     panel_10, rest_11, upper_1, tile_inverse_1 = call_factor(
         second_start_kernel, "factor_second_start",
         [square(width, jnp.bfloat16), jax.ShapeDtypeStruct((width, half), jnp.bfloat16), square(half), square(half)],
-        block_10[:half], block_10[half:], block_01[half:], block_11[:half], block_11[half:], inverse_0)
+        block_10[:half], block_10[half:], block_01[half:], block_11[:half], block_11[half:], pieces_0)
     rows, above, above_other, tile_inverse_1 = lax.optimization_barrier((rows, above, above_other, tile_inverse_1))
     above_0, above_1 = by_row(above, above_other, my_row)
     other = swap(rows, "col", 1)
-    pieces = jax.ShapeDtypeStruct((3, width, width), jnp.bfloat16)
     mirror = jax.ShapeDtypeStruct((col_blocks, width, width), jnp.bfloat16)
-    lower_1, pieces_0, pieces_1, mirror_0, later, _ = call_factor(
-        second_kernel, "factor_second", [square(width), pieces, pieces, mirror, mirror, square(width)],
-        rest_11, upper_1, tile_inverse_1, inverse_0, panel_10, above_0, above_1)
+    lower_1, pieces_1, mirror_0, later = call_factor(
+        second_kernel, "factor_second", [square(width), pieces, mirror, mirror],
+        rest_11, upper_1, tile_inverse_1, pieces_0, panel_10, above_0, above_1)
     other, lower_1 = lax.optimization_barrier((other, lower_1))
     column_0 = jnp.where(even, rows, other)
     column_1 = jnp.where(even, other, rows)

time: 54.6 us -> 54.5 us (level)
  waiting for transfers between devices: 6.69 us -> 9.81 us
  starting transfers between devices: 17.6 us -> 14.5 us
  Pallas kernels: 26.2 us -> 24.5 us
  other arithmetic: 0.43 us -> 1.38 us
  local copies, waits for them, and re-layouts: 2.35 us -> 3.05 us
    ppermute x3 -> x0, starting transfers between devices: 5.71 us -> none  [diagonal_down(): got = lax.ppermute(along, ('row', 'col'), pairs)]
    ppermute x5 -> x8, waiting for transfers between devices: 0.94 us -> 4.29 us  [swap(): return lax.ppermute(block, axis, [(d, d ^ distance) for d in range(count)])]
    ppermute x5 -> x8, starting transfers between devices: 3.09 us -> 5.69 us  [swap(): return lax.ppermute(block, axis, [(d, d ^ distance) for d in range(count)])]
    ppermute x3 -> x0, waiting for transfers between devices: 1.88 us -> none  [diagonal_down(): got = lax.ppermute(along, ('row', 'col'), pairs)]
    pallas_call x4, Pallas kernels: 21.6 us -> 19.9 us  [call_factor(): pl.pallas_call(kernel, out_shape=shapes, name=name, cost_estimate=FACTOR_...]
    ppermute x1, waiting for transfers between devices: 3.49 us -> 5.15 us  [first_stride(): return (block, lax.ppermute(block, 'col', pairs))]
    select_n x1, other arithmetic: 0.04 us -> 0.99 us  [by_row(): return (jnp.where(even, block, other), jnp.where(even, other, block))]
    unnamed x4 -> x6, local copies, waits for them, and re-layouts: 1.22 us -> 1.92 us
  transfers between devices with their start and end apart: 12 -> 12, of which waited for: 5 -> 5; matrix products, arithmetic and copies ran while one was open for 3% -> 4% of each run, Pallas kernels for 40% -> 37%
where the time goes in v3:
time: 54.5 us; the launch traced here: 54.2 us
  Pallas kernels  24.5 us (45%)
  starting transfers between devices  14.5 us (27%)
  waiting for transfers between devices  9.81 us (18%)
  local copies, waits for them, and re-layouts  3.05 us (6%)
  other arithmetic  1.38 us (3%)
  between operations  0.88 us (2%)
    pallas_call x4, Pallas kernels, call_factor(): pl.pallas_call(kernel, out_shape=shapes, name=name, cost_estimate=FACTOR_...  19.9 us
    ppermute x3, starting transfers between devices, diagonal_along(): got = lax.ppermute(quarters, ('row', 'col'), pairs)  7.53 us
    ppermute x8, starting transfers between devices, swap(): return lax.ppermute(block, axis, [(d, d ^ distance) for d in range(count)])  5.69 us
    ppermute x1, waiting for transfers between devices, first_stride(): return (block, lax.ppermute(block, 'col', pairs))  5.15 us
    pallas_call x1, Pallas kernels, update(): pl.pallas_call(update_kernel, grid=(row_blocks // batch,), in_specs=[pl.B...  4.51 us
    ppermute x8, waiting for transfers between devices, swap(): return lax.ppermute(block, axis, [(d, d ^ distance) for d in range(count)])  4.29 us
    unnamed x6, local copies, waits for them, and re-layouts  1.92 us
    ppermute x1, starting transfers between devices, first_stride(): return (block, lax.ppermute(block, 'col', pairs))  1.32 us
  transfers between devices with their start and end apart: 12, of which 5 were waited for; matrix products, arithmetic and copies ran while one was open for 4% of the time, Pallas kernels for 37%

profile of v3, /device:TPU:1, one launch (start us, length us, event | category | flops | bytes accessed | tf_op | source)
XLA Modules:
  0.0 54.2 jit_solution(7760666932958367625)
XLA Ops:
  0.6 0.0 copy-start
  0.6 1.2 %copy-done = bf16[1,4,1,2,256,256]{5,4,3,2,1,0:T(8,128)(2,1)S(1)} copy-done((bf16[1,4,1,2,256,256]{5,4,3,2,1,0:T(8,128)(2,1)S(1)}, bf16[1,4,1,2,256,256]{5,4,3,2,1,0:T(8,128)(2,1)}, u32[]{:S(2)}) %copy-start) | copy-done | bytes 1048600
  1.9 0.1 pack.1
  1.9 4.2 %collective-permute-start.2 = (bf16[384,128]{1,0:T(8,128)(2,1)S(1)}, bf16[384,128]{1,0:T(8,128)(2,1)S(1)}, u32[]{:S(2)}, u32[]{:S(2)}) collective-permute-start(bf16[384,128]{1,0:T(8,128)(2,1)S(1)} %pack.1), channel_id=1, source_target_pairs={{0,2},{1,3},{8,10},{9,11}} | collective-permute-start | bytes 294920 | tf_op jit(solution)/shard_map/ppermute | solution.py:296
  6.1 1.7 %collective-permute-start.1 = (bf16[384,128]{1,0:T(8,128)(2,1)S(1)}, bf16[384,128]{1,0:T(8,128)(2,1)S(1)}, u32[]{:S(2)}, u32[]{:S(2)}) collective-permute-start(bf16[384,128]{1,0:T(8,128)(2,1)S(1)} %pack.1), channel_id=1, source_target_pairs={{0,4},{1,5},{8,12},{9,13}} | collective-permute-start | bytes 294920 | tf_op jit(solution)/shard_map/ppermute | solution.py:296
  7.8 1.7 %collective-permute-start = (bf16[384,128]{1,0:T(8,128)(2,1)S(1)}, bf16[384,128]{1,0:T(8,128)(2,1)S(1)}, u32[]{:S(2)}, u32[]{:S(2)}) collective-permute-start(bf16[384,128]{1,0:T(8,128)(2,1)S(1)} %pack.1), channel_id=1, source_target_pairs={{0,6},{1,7},{8,14},{9,15}} | collective-permute-start | bytes 294920 | tf_op jit(solution)/shard_map/ppermute | solution.py:296
  9.5 1.1 %slice_bitcast_fusion = bf16[4,256,256]{2,1,0:T(8,128)(2,1)S(1)} fusion(bf16[4,2,256,256]{3,2,1,0:T(8,128)(2,1)} %bitcast.29), kind=kLoop, calls=%fused_computation | loop fusion | bytes 1048576 | tf_op jit(solution)/shard_map/squeeze | solution.py:366
  10.6 1.3 %collective-permute-start.6 = (bf16[4,256,256]{2,1,0:T(8,128)(2,1)S(1)}, bf16[4,256,256]{2,1,0:T(8,128)(2,1)S(1)}, u32[]{:S(2)}, u32[]{:S(2)}) collective-permute-start(bf16[4,256,256]{2,1,0:T(8,128)(2,1)S(1)} %slice_bitcast_fusion), channel_id=1, source_target_pairs={{0,4},{1,5},{8,12},{9,13},{16,20},{17,21},{24,28},{25,29}} | collective-permute-start | bytes 1572872 | tf_op jit(solution)/shard_map/ppermute | solution.py:340
  12.0 0.4 collective-permute-done
  12.3 1.3 %collective-permute-start.5 = (bf16[384,128]{1,0:T(8,128)(2,1)S(1)}, bf16[384,128]{1,0:T(8,128)(2,1)S(1)}, u32[]{:S(2)}, u32[]{:S(2)}) collective-permute-start(bf16[384,128]{1,0:T(8,128)(2,1)S(1)} %select_select_fusion), channel_id=1, source_target_pairs={{0,8},{8,0},{16,24},{24,16},{1,9},{9,1},{17,25},{25,17},{2,10},{10... | collective-permute-start | bytes 294920 | tf_op jit(solution)/shard_map/ppermute | solution.py:285
  13.6 1.4 %collective-permute-start.3 = (bf16[384,128]{1,0:T(8,128)(2,1)S(1)}, bf16[384,128]{1,0:T(8,128)(2,1)S(1)}, u32[]{:S(2)}, u32[]{:S(2)}) collective-permute-start(bf16[384,128]{1,0:T(8,128)(2,1)S(1)} %select_select_fusion), channel_id=1, source_target_pairs={{0,24},{8,16},{16,8},{24,0},{1,25},{9,17},{17,9},{25,1},{2,26},{10... | collective-permute-start | bytes 294920 | tf_op jit(solution)/shard_map/ppermute | solution.py:285
  15.1 0.0 collective-permute-start.8
  15.1 0.8 %collective-permute-done.5 = bf16[384,128]{1,0:T(8,128)(2,1)S(1)} collective-permute-done((bf16[384,128]{1,0:T(8,128)(2,1)S(1)}, bf16[384,128]{1,0:T(8,128)(2,1)S(1)}, u32[]{:S(2)}, u32[]{:S(2)}) %collective-permute-start.5) | collective-permute-done | bytes 98336 | tf_op jit(solution)/shard_map/ppermute | solution.py:285
  15.9 2.6 %collective-permute-done.4 = bf16[384,128]{1,0:T(8,128)(2,1)S(1)} collective-permute-done((bf16[384,128]{1,0:T(8,128)(2,1)S(1)}, bf16[384,128]{1,0:T(8,128)(2,1)S(1)}, u32[]{:S(2)}, u32[]{:S(2)}) %collective-permute-start.4) | collective-permute-done | bytes 98336 | tf_op jit(solution)/shard_map/ppermute | solution.py:285
  18.5 5.2 %collective-permute-done.6 = bf16[4,256,256]{2,1,0:T(8,128)(2,1)S(1)} collective-permute-done((bf16[4,256,256]{2,1,0:T(8,128)(2,1)S(1)}, bf16[4,256,256]{2,1,0:T(8,128)(2,1)S(1)}, u32[]{:S(2)}, u32[]{:S(2)}) %collective-permute-start.6) | collective-permute-done | bytes 524320 | tf_op jit(solution)/shard_map/ppermute | solution.py:340
  23.7 0.9 %collective-permute-start.9 = (bf16[2,384,128]{2,1,0:T(8,128)(2,1)S(1)}, bf16[2,384,128]{2,1,0:T(8,128)(2,1)S(1)}, u32[]{:S(2)}, u32[]{:S(2)}) collective-permute-start(bf16[2,384,128]{2,1,0:T(8,128)(2,1)S(1)} %pad_maximum_fusion), channel_id=1, source_target_pairs={{0,1},{1,0},{2,3},{3,2},{4,5},{5,4},{6,7},{7,6},{8,9},{9,8},{10,11... | collective-permute-start | bytes 589832 | tf_op jit(solution)/shard_map/ppermute | solution.py:285
  24.6 0.1 broadcast_select_fusion
  24.7 0.1 collective-permute-start.7
  24.7 0.9 %collective-permute-done.9 = bf16[2,384,128]{2,1,0:T(8,128)(2,1)S(1)} collective-permute-done((bf16[2,384,128]{2,1,0:T(8,128)(2,1)S(1)}, bf16[2,384,128]{2,1,0:T(8,128)(2,1)S(1)}, u32[]{:S(2)}, u32[]{:S(2)}) %collective-permute-start.9) | collective-permute-done | bytes 196640 | tf_op jit(solution)/shard_map/ppermute | solution.py:285
  25.7 4.3 %factor_start.1 = (f32[128,128]{1,0:T(8,128)S(1)}, f32[128,128]{1,0:T(8,128)S(1)}) custom-call(bf16[128,128]{1,0:T(8,128)(2,1)S(1)} %get-tuple-element.73.quarter_ref), custom_call_target="tpu_custom_call" | custom-call | flops 1000000 | bytes 10000 | tf_op jit(solution)/shard_map/factor_start/pallas_call | solution.py:224
  30.1 1.3 %collective-permute-start.10 = (bf16[2,256,256]{2,1,0:T(8,128)(2,1)S(1)}, bf16[2,256,256]{2,1,0:T(8,128)(2,1)S(1)}, u32[]{:S(2)}, u32[]{:S(2)}) collective-permute-start(bf16[2,256,256]{2,1,0:T(8,128)(2,1)S(1)} %broadcast_select_fusion.6), channel_id=1, source_target_pairs={{0,8},{8,0},{16,24},{24,16},{1,9},{9,1},{17,25},{25,17},{2,10},{10... | collective-permute-start | bytes 786440 | tf_op jit(solution)/shard_map/ppermute | solution.py:285
  31.4 5.4 %factor_first.1 = (f32[256,256]{1,0:T(8,128)S(1)}, bf16[3,256,256]{2,1,0:T(8,128)(2,1)S(1)}) custom-call(bf16[256,128]{1,0:T(8,128)(2,1)S(1)} %get-tuple-element.68.rest_ref, f32[128,128]{1,0:T(8,128)S(1)} %get-tuple-element.38.upper_ref, f32[128,128]{1,0:T(8,128)S(1)} %get-tuple-element.39.tile_inverse_ref), custom_call_target="tpu_custom_call" | custom-call | flops 1000000 | bytes 10000 | tf_op jit(solution)/shard_map/factor_first/pallas_call | solution.py:224
  36.8 4.8 %factor_second_start.1 = (bf16[256,256]{1,0:T(8,128)(2,1)S(1)}, bf16[256,128]{1,0:T(8,128)(2,1)S(1)}, f32[128,128]{1,0:T(8,128)S(1)}, f32[128,128]{1,0:T(8,128)S(1)}) custom-call(bf16[128,128]{1,0:T(8,128)(2,1)S(1)} %get-tuple-element.72.top_10_ref, bf16[256,128]{1,0:T(8,128)(2,1)S(1)} %get-tuple-element.69.rest_10_ref, ...), custom_call_target="tpu_custom_call" | custom-call | flops 1000000 | bytes 10000 | tf_op jit(solution)/shard_map/factor_second_start/pallas_call | solution.py:224
  41.6 0.1 broadcast_select_fusion.1
  41.7 0.0 copy-start.2
  41.7 0.7 %copy-done.2 = bf16[2,256,256]{2,1,0:T(8,128)(2,1)} copy-done((bf16[2,256,256]{2,1,0:T(8,128)(2,1)}, bf16[2,256,256]{2,1,0:T(8,128)(2,1)S(1)}, u32[]{:S(2)}) %copy-start.2) | copy-done | bytes 262168
  42.4 0.7 %collective-permute-start.11 = (bf16[4,256,256]{2,1,0:T(8,128)(2,1)S(1)}, bf16[4,256,256]{2,1,0:T(8,128)(2,1)S(1)}, u32[]{:S(2)}, u32[]{:S(2)}) collective-permute-start(bf16[4,256,256]{2,1,0:T(8,128)(2,1)S(1)} %broadcast_select_fusion.1), channel_id=1, source_target_pairs={{0,1},{1,0},{2,3},{3,2},{4,5},{5,4},{6,7},{7,6},{8,9},{9,8},{10,11... | collective-permute-start | bytes 1572872 | tf_op jit(solution)/shard_map/ppermute | solution.py:285
  43.0 0.1 pad_add_fusion.ids_ref
  43.1 1.0 %broadcast_select_fusion.4 = (bf16[2,256,256]{2,1,0:T(8,128)(2,1)S(1)}, bf16[2,256,256]{2,1,0:T(8,128)(2,1)S(1)}) fusion(bf16[2,256,256]{2,1,0:T(8,128)(2,1)} %copy-done.2, bf16[2,256,256]{2,1,0:T(8,128)(2,1)S(1)} %broadcast_select_fusion.6, pred[]{:T(512)S(6)} %eq.52), kind=kLoop, calls=%fused_computation.6 | loop fusion | flops 262144 | bytes 1048577 | tf_op jit(solution)/shard_map/jit(_where)/select_n | solution.py:334
  44.1 5.5 %factor_second.1 = (f32[256,256]{1,0:T(8,128)S(1)}, bf16[3,256,256]{2,1,0:T(8,128)(2,1)S(1)}, bf16[2,256,256]{2,1,0:T(8,128)(2,1)S(1)}, bf16[2,256,256]{2,1,0:T(8,128)(2,1)S(1)}) custom-call(bf16[256,128]{1,0:T(8,128)(2,1)S(1)} %get-tuple-element.43.rest_ref, f32[128,128]{1,0:T(8,128)S(1)} %get-tuple-element.44.upper_ref, ...), custom_call_target="tpu_custom_call" | custom-call | flops 1000000 | bytes 10000 | tf_op jit(solution)/shard_map/factor_second/pallas_call | solution.py:224
  49.6 0.1 broadcast_select_fusion.2
  49.7 4.5 %solve_and_update.1 = (f32[4,2,256,256]{3,2,1,0:T(8,128)}, bf16[4,2,256,256]{3,2,1,0:T(8,128)(2,1)}) custom-call(s32[4]{0:T(128)S(1)} %pad_add_fusion.ids_ref, bf16[4,256,256]{2,1,0:T(8,128)(2,1)S(1)} %get-tuple-element.61.column_0_ref, bf16[4,256,256]{2,1,0:T(8,128)(2,1)S(1)} %get-tuple-element.60.column_1_ref, bf16[4,2,256,256]{3,2,1,0:T(8,128)(2,1)S(1)} %bitcast.30, ...), custom_call_target="tpu_custom_call" | custom-call | flops 2000000000 | bytes 6000000 | tf_op jit(solution)/shard_map/solve_and_update/pallas_call | solution.py:242
  (19 shorter events, 0.2 us)
Async XLA Ops:
  0.6 1.2 %copy-start = (bf16[1,4,1,2,256,256]{5,4,3,2,1,0:T(8,128)(2,1)S(1)}, bf16[1,4,1,2,256,256]{5,4,3,2,1,0:T(8,128)(2,1)}, u32[]{:S(2)}) copy-start(bf16[1,4,1,2,256,256]{5,4,3,2,1,0:T(8,128)(2,1)} %kernel_ref.1) | copy-start | bytes 3145732
  1.9 8.7 %copy-start.1 = (bf16[1,4,1,2,256,256]{5,4,3,2,1,0:T(8,128)(2,1)S(1)}, bf16[1,4,1,2,256,256]{5,4,3,2,1,0:T(8,128)(2,1)}, u32[]{:S(2)}) copy-start(bf16[1,4,1,2,256,256]{5,4,3,2,1,0:T(8,128)(2,1)} %kernel_ref.1) | copy-start | bytes 3145732
  1.9 10.0 %collective-permute-start.2 = (bf16[384,128]{1,0:T(8,128)(2,1)S(1)}, bf16[384,128]{1,0:T(8,128)(2,1)S(1)}, u32[]{:S(2)}, u32[]{:S(2)}) collective-permute-start(bf16[384,128]{1,0:T(8,128)(2,1)S(1)} %pack.1), channel_id=1, source_target_pairs={{0,2},{1,3},{8,10},{9,11}} | collective-permute-start | bytes 294920 | tf_op jit(solution)/shard_map/ppermute | solution.py:296
  6.1 5.9 %collective-permute-start.1 = (bf16[384,128]{1,0:T(8,128)(2,1)S(1)}, bf16[384,128]{1,0:T(8,128)(2,1)S(1)}, u32[]{:S(2)}, u32[]{:S(2)}) collective-permute-start(bf16[384,128]{1,0:T(8,128)(2,1)S(1)} %pack.1), channel_id=1, source_target_pairs={{0,4},{1,5},{8,12},{9,13}} | collective-permute-start | bytes 294920 | tf_op jit(solution)/shard_map/ppermute | solution.py:296
  7.8 4.5 %collective-permute-start = (bf16[384,128]{1,0:T(8,128)(2,1)S(1)}, bf16[384,128]{1,0:T(8,128)(2,1)S(1)}, u32[]{:S(2)}, u32[]{:S(2)}) collective-permute-start(bf16[384,128]{1,0:T(8,128)(2,1)S(1)} %pack.1), channel_id=1, source_target_pairs={{0,6},{1,7},{8,14},{9,15}} | collective-permute-start | bytes 294920 | tf_op jit(solution)/shard_map/ppermute | solution.py:296
  10.6 13.1 %collective-permute-start.6 = (bf16[4,256,256]{2,1,0:T(8,128)(2,1)S(1)}, bf16[4,256,256]{2,1,0:T(8,128)(2,1)S(1)}, u32[]{:S(2)}, u32[]{:S(2)}) collective-permute-start(bf16[4,256,256]{2,1,0:T(8,128)(2,1)S(1)} %slice_bitcast_fusion), channel_id=1, source_target_pairs={{0,4},{1,5},{8,12},{9,13},{16,20},{17,21},{24,28},{25,29}} | collective-permute-start | bytes 1572872 | tf_op jit(solution)/shard_map/ppermute | solution.py:340
  12.3 3.5 %collective-permute-start.5 = (bf16[384,128]{1,0:T(8,128)(2,1)S(1)}, bf16[384,128]{1,0:T(8,128)(2,1)S(1)}, u32[]{:S(2)}, u32[]{:S(2)}) collective-permute-start(bf16[384,128]{1,0:T(8,128)(2,1)S(1)} %select_select_fusion), channel_id=1, source_target_pairs={{0,8},{8,0},{16,24},{24,16},{1,9},{9,1},{17,25},{25,17},{2,10},{10... | collective-permute-start | bytes 294920 | tf_op jit(solution)/shard_map/ppermute | solution.py:285
  13.6 4.8 %collective-permute-start.4 = (bf16[384,128]{1,0:T(8,128)(2,1)S(1)}, bf16[384,128]{1,0:T(8,128)(2,1)S(1)}, u32[]{:S(2)}, u32[]{:S(2)}) collective-permute-start(bf16[384,128]{1,0:T(8,128)(2,1)S(1)} %select_select_fusion), channel_id=1, source_target_pairs={{0,16},{8,24},{16,0},{24,8},{1,17},{9,25},{17,1},{25,9},{2,18},{10... | collective-permute-start | bytes 294920 | tf_op jit(solution)/shard_map/ppermute | solution.py:285
  13.6 4.8 %collective-permute-start.3 = (bf16[384,128]{1,0:T(8,128)(2,1)S(1)}, bf16[384,128]{1,0:T(8,128)(2,1)S(1)}, u32[]{:S(2)}, u32[]{:S(2)}) collective-permute-start(bf16[384,128]{1,0:T(8,128)(2,1)S(1)} %select_select_fusion), channel_id=1, source_target_pairs={{0,24},{8,16},{16,8},{24,0},{1,25},{9,17},{17,9},{25,1},{2,26},{10... | collective-permute-start | bytes 294920 | tf_op jit(solution)/shard_map/ppermute | solution.py:285
  15.1 15.0 %collective-permute-start.8 = (bf16[2,256,256]{2,1,0:T(8,128)(2,1)S(1)}, bf16[2,256,256]{2,1,0:T(8,128)(2,1)S(1)}, u32[]{:S(2)}, u32[]{:S(2)}) collective-permute-start(bf16[2,256,256]{2,1,0:T(8,128)(2,1)S(1)} %slice_bitcast_fusion.1), channel_id=1, source_target_pairs={{0,16},{8,24},{16,0},{24,8},{1,17},{9,25},{17,1},{25,9},{2,18},{10... | collective-permute-start | bytes 786440 | tf_op jit(solution)/shard_map/ppermute | solution.py:285
  23.7 2.0 %collective-permute-start.9 = (bf16[2,384,128]{2,1,0:T(8,128)(2,1)S(1)}, bf16[2,384,128]{2,1,0:T(8,128)(2,1)S(1)}, u32[]{:S(2)}, u32[]{:S(2)}) collective-permute-start(bf16[2,384,128]{2,1,0:T(8,128)(2,1)S(1)} %pad_maximum_fusion), channel_id=1, source_target_pairs={{0,1},{1,0},{2,3},{3,2},{4,5},{5,4},{6,7},{7,6},{8,9},{9,8},{10,11... | collective-permute-start | bytes 589832 | tf_op jit(solution)/shard_map/ppermute | solution.py:285
  24.7 16.9 %collective-permute-start.7 = (bf16[4,256,256]{2,1,0:T(8,128)(2,1)S(1)}, bf16[4,256,256]{2,1,0:T(8,128)(2,1)S(1)}, u32[]{:S(2)}, u32[]{:S(2)}) collective-permute-start(bf16[4,256,256]{2,1,0:T(8,128)(2,1)S(1)} %broadcast_select_fusion), channel_id=1, source_target_pairs={{0,2},{1,3},{2,0},{3,1},{4,6},{5,7},{6,4},{7,5},{8,10},{9,11},{10,... | collective-permute-start | bytes 1572872 | tf_op jit(solution)/shard_map/ppermute | solution.py:285
  30.1 11.6 %collective-permute-start.10 = (bf16[2,256,256]{2,1,0:T(8,128)(2,1)S(1)}, bf16[2,256,256]{2,1,0:T(8,128)(2,1)S(1)}, u32[]{:S(2)}, u32[]{:S(2)}) collective-permute-start(bf16[2,256,256]{2,1,0:T(8,128)(2,1)S(1)} %broadcast_select_fusion.6), channel_id=1, source_target_pairs={{0,8},{8,0},{16,24},{24,16},{1,9},{9,1},{17,25},{25,17},{2,10},{10... | collective-permute-start | bytes 786440 | tf_op jit(solution)/shard_map/ppermute | solution.py:285
  41.7 0.7 %copy-start.2 = (bf16[2,256,256]{2,1,0:T(8,128)(2,1)}, bf16[2,256,256]{2,1,0:T(8,128)(2,1)S(1)}, u32[]{:S(2)}) copy-start(bf16[2,256,256]{2,1,0:T(8,128)(2,1)S(1)} %collective-permute-done.10) | copy-start | bytes 786436
  42.4 7.2 %collective-permute-start.11 = (bf16[4,256,256]{2,1,0:T(8,128)(2,1)S(1)}, bf16[4,256,256]{2,1,0:T(8,128)(2,1)S(1)}, u32[]{:S(2)}, u32[]{:S(2)}) collective-permute-start(bf16[4,256,256]{2,1,0:T(8,128)(2,1)S(1)} %broadcast_select_fusion.1), channel_id=1, source_target_pairs={{0,1},{1,0},{2,3},{3,2},{4,5},{5,4},{6,7},{7,6},{8,9},{9,8},{10,11... | collective-permute-start | bytes 1572872 | tf_op jit(solution)/shard_map/ppermute | solution.py:285

commit v4 on v3

--- a/solution.py
+++ b/solution.py
@@ -29,8 +29,8 @@
         v = [spread(right[s][k:k + 1, :]) for k in range(8)]
         d = [[lane(y[i], 8 * s + k) if k >= i else None for k in range(8)] for i in range(8)]
         last = s + 1 == groups
-        columns = [[lane(left[g], 8 * s + k) for k in range(8)] for g in range(s + 1, groups)]
-        e = list(columns[0]) if not last else None
+        near = None if last else [lane(left[s + 1], 8 * s + k) for k in range(8)]
+        e = None if last else list(near)
         ratio = [[None] * 8 for _ in range(8)]
         inv = []
         for k in range(8):
@@ -65,7 +65,7 @@
                 x[k] = x[k] - ratio[j][k] * x[j]
                 w[k] = w[k] - ratio[j][k] * w[j]
         for g in range(s + 1, groups):
-            f = columns[g - s - 1]
+            f = near if g == s + 1 else [lane(left[g], 8 * s + k) for k in range(8)]
             for k in reversed(range(8)):
                 if g > s + 1:
                     left[g] = left[g] - f[k] * x[k]
@@ -159,22 +159,22 @@
 
 
 def second_kernel(
-    rest_ref, upper_ref, tile_inverse_ref, pieces_0_ref, panel_ref, above_0_ref, above_1_ref,
+    ids_ref, rest_ref, upper_ref, tile_inverse_ref, pieces_0_ref, panel_ref, above_ref, other_ref,
     lower_ref, pieces_1_ref, mirror_ref, later_ref,
 ):
     half = rest_ref.shape[1]
+    even = ids_ref[0] % 2 == 0
     tasks = []
-    for m in range(above_0_ref.shape[0]):
-        for part in (pl.ds(0, half), pl.ds(half, half)):
-            def mirror(m=m, part=part):
-                mirror_ref[m, part] = sum(mul(pieces_0_ref[p, part], above_0_ref[m]) for p in (2, 1, 0)).astype(jnp.bfloat16)
-            tasks.append(mirror)
-    for m in range(above_0_ref.shape[0]):
-        for part in (pl.ds(0, half), pl.ds(half, half)):
-            def later(m=m, part=part):
-                change = mul(panel_ref[part], mirror_ref[m])
-                later_ref[m, part] = (above_1_ref[m, part].astype(jnp.float32) - change).astype(jnp.bfloat16)
-            tasks.append(later)
+    for m in range(above_ref.shape[0]):
+        def mirror(m=m):
+            above = jnp.where(even, above_ref[m], other_ref[m])
+            mirror_ref[m] = product(pieces_0_ref, above).astype(jnp.bfloat16)
+
+        def later(m=m):
+            above = jnp.where(even, other_ref[m], above_ref[m]).astype(jnp.float32)
+            later_ref[m] = (above - mul(panel_ref[...], mirror_ref[m])).astype(jnp.bfloat16)
+
+        tasks += [mirror, later]
     factor_rest(
         upper_ref[...], tile_inverse_ref[...], rest_ref[:half], rest_ref[half:], lower_ref, pieces_1_ref, tasks)
 
@@ -182,47 +182,62 @@
 def update_kernel(
     ids_ref, column_0_ref, column_1_ref, blocks_ref, mirror_0_ref, later_ref,
     lower_0_ref, lower_1_ref, pieces_0_ref, pieces_1_ref, panel_10_ref,
-    panels_ref, schur_ref, mirror_1_ref,
+    panels_ref, schur_ref, panels_here, schur_here, mirror_1_ref, panels_done, schur_done,
 ):
-    step = pl.program_id(0)
-    batch, col_blocks, width = blocks_ref.shape[:3]
-
-    @pl.when(step == 0)
-    def _():
-        for m in range(col_blocks):
-            mirror_1_ref[m] = product(pieces_1_ref, later_ref[m]).astype(jnp.bfloat16)
-
-    ids = [(step * batch + i) * ids_ref[2] + ids_ref[0] for i in range(batch)]
-
-    def below(solved, panel, lower_ref):
+    row_blocks, col_blocks, width = blocks_ref.shape[:3]
+    size = 2 if row_blocks % 2 == 0 else 1
+    batches = range(0, row_blocks, size)
+    ids = [i * ids_ref[2] + ids_ref[0] for i in range(row_blocks)]
+    copies = []
+
+    def send(source, target, semaphore):
+        copies.append(pltpu.make_async_copy(source, target, semaphore))
+        copies[-1].start()
+
+    def below(solved, panel, lower_ref, start):
         parts = []
-        for i, block_row in enumerate(ids):
-            part = jnp.where(block_row > panel, solved[i * width:(i + 1) * width], 0.0)
-            panels_ref[i, panel] = jnp.where(block_row == panel, lower_ref[...], part)
+        for i in range(start, start + size):
+            part = jnp.where(ids[i] > panel, solved[(i - start) * width:(i - start + 1) * width], 0.0)
+            panels_here[i, panel] = jnp.where(ids[i] == panel, lower_ref[...], part)
+            send(panels_here.at[i, panel], panels_ref.at[i, panel], panels_done.at[i, panel])
             parts.append(part)
         return jnp.concatenate(parts, axis=0).astype(jnp.bfloat16)
 
-    rounded_0 = below(solve(column_0_ref[...].reshape(batch * width, width), pieces_0_ref), 0, lower_0_ref)
-    column = column_1_ref[...].reshape(batch * width, width).astype(jnp.float32)
-    column = (column - mul(rounded_0, panel_10_ref[...], ROWS)).astype(jnp.bfloat16)
-    rounded_1 = below(solve(column, pieces_1_ref), 1, lower_1_ref)
+    def batch(column_ref, start):
+        return column_ref[start:start + size].reshape(size * width, width)
+
+    rounded_0 = [below(solve(batch(column_0_ref, b), pieces_0_ref), 0, lower_0_ref, b) for b in batches]
+    columns = []
+    for b, rounded in zip(batches, rounded_0):
+        change = mul(rounded, panel_10_ref[...], ROWS)
+        columns.append((batch(column_1_ref, b).astype(jnp.float32) - change).astype(jnp.bfloat16))
     for m in range(col_blocks):
-        change_0 = mul(rounded_0, mirror_0_ref[m])
-        change_1 = mul(rounded_1, mirror_1_ref[m])
-        for i, block_row in enumerate(ids):
-            part = slice(i * width, (i + 1) * width)
-            block = blocks_ref[i, m].astype(jnp.float32) - change_0[part]
-            block = block.astype(jnp.bfloat16).astype(jnp.float32) - change_1[part]
-            keep = (block_row >= PANELS) & (m * ids_ref[3] + ids_ref[1] >= PANELS)
-            schur_ref[i, m] = jnp.where(keep, block, 0.0).astype(jnp.bfloat16)
+        mirror_1_ref[m] = product(pieces_1_ref, later_ref[m]).astype(jnp.bfloat16)
+    rounded_1 = [below(solve(column, pieces_1_ref), 1, lower_1_ref, b) for b, column in zip(batches, columns)]
+    for b, left_0, left_1 in zip(batches, rounded_0, rounded_1):
+        for m in range(col_blocks):
+            change_0 = mul(left_0, mirror_0_ref[m])
+            change_1 = mul(left_1, mirror_1_ref[m])
+            for i in range(b, b + size):
+                part = slice((i - b) * width, (i - b + 1) * width)
+                block = blocks_ref[i, m].astype(jnp.float32) - change_0[part]
+                block = block.astype(jnp.bfloat16).astype(jnp.float32) - change_1[part]
+                keep = (ids[i] >= PANELS) & (m * ids_ref[3] + ids_ref[1] >= PANELS)
+                schur_here[i, m] = jnp.where(keep, block, 0.0).astype(jnp.bfloat16)
+        for i in range(b, b + size):
+            send(schur_here.at[i], schur_ref.at[i], schur_done.at[i])
+    for copy in copies:
+        copy.wait()
 
 
 FACTOR_COST = pl.CostEstimate(flops=10**6, bytes_accessed=10**4, transcendentals=0)
 
 
 def call_factor(kernel, name, shapes, *operands):
+    in_specs = [
+        pl.BlockSpec(memory_space=pltpu.SMEM if x.dtype == jnp.int32 else pltpu.VMEM) for x in operands]
     return pl.pallas_call(
-        kernel, out_shape=shapes, name=name, cost_estimate=FACTOR_COST,
+        kernel, in_specs=in_specs, out_shape=shapes, name=name, cost_estimate=FACTOR_COST,
         compiler_params=pltpu.CompilerParams(vmem_limit_bytes=VMEM_LIMIT),
     )(*operands)
 
@@ -233,23 +248,20 @@
 
 def update(ids, column_0, column_1, blocks, mirror_0, later, lower_0, lower_1, pieces_0, pieces_1, panel_10):
     row_blocks, col_blocks, width = blocks.shape[:3]
-    batch = 2 if row_blocks % 2 == 0 else 1
-    rows_spec = pl.BlockSpec((batch, width, width), lambda i: (i, 0, 0))
-    square_spec = pl.BlockSpec((width, width), lambda i: (0, 0))
-    mirror_spec = pl.BlockSpec((col_blocks, width, width), lambda i: (0, 0, 0))
-    pieces_spec = pl.BlockSpec((3, width, width), lambda i: (0, 0, 0))
-    block_spec = pl.BlockSpec((batch, col_blocks, width, width), lambda i: (i, 0, 0, 0))
+    panels = jax.ShapeDtypeStruct((row_blocks, PANELS, width, width), jnp.float32)
+    schur = jax.ShapeDtypeStruct(blocks.shape, jnp.bfloat16)
     return pl.pallas_call(
         update_kernel,
-        grid=(row_blocks // batch,),
-        in_specs=[pl.BlockSpec(memory_space=pltpu.SMEM), rows_spec, rows_spec, block_spec, mirror_spec, mirror_spec]
-        + [square_spec] * 2 + [pieces_spec] * 2 + [square_spec],
-        out_specs=[pl.BlockSpec((batch, PANELS, width, width), lambda i: (i, 0, 0, 0)), block_spec],
-        out_shape=[
-            jax.ShapeDtypeStruct((row_blocks, PANELS, width, width), jnp.float32),
-            jax.ShapeDtypeStruct(blocks.shape, jnp.bfloat16),
+        in_specs=[pl.BlockSpec(memory_space=pltpu.SMEM)] + [pl.BlockSpec(memory_space=pltpu.VMEM)] * 10,
+        out_specs=[pl.BlockSpec(memory_space=pl.ANY)] * 2,
+        out_shape=[panels, schur],
+        scratch_shapes=[
+            pltpu.VMEM(panels.shape, panels.dtype),
+            pltpu.VMEM(schur.shape, schur.dtype),
+            pltpu.VMEM((col_blocks, width, width), jnp.bfloat16),
+            pltpu.SemaphoreType.DMA((row_blocks, PANELS)),
+            pltpu.SemaphoreType.DMA((row_blocks,)),
         ],
-        scratch_shapes=[pltpu.VMEM((col_blocks, width, width), jnp.bfloat16)],
         compiler_params=pltpu.CompilerParams(vmem_limit_bytes=VMEM_LIMIT),
         cost_estimate=pl.CostEstimate(flops=2 * 10**9, bytes_accessed=6 * 10**6, transcendentals=0),
         name="solve_and_update",
@@ -327,11 +339,6 @@
         if reach >= lax.axis_size("row"):
             return block
         got = swap(block, "row", reach)
-
-
-def by_row(block, other, my_row):
-    even = my_row % 2 == 0
-    return jnp.where(even, block, other), jnp.where(even, other, block)
 
 
 def first_stride(block):
@@ -362,6 +369,7 @@
     blocks = kernel[0, :, 0]
     col_blocks, width = blocks.shape[1:3]
     half = width // 2
+    ids = jnp.stack([my_row, my_col, lax.axis_size("row"), lax.axis_size("col")]).astype(jnp.int32)
     quarters = pack(kernel)
     rows, above, _ = lax.optimization_barrier((blocks[:, 0], blocks[0], quarters))
     rows, rows_got = first_stride(rows)
@@ -383,16 +391,14 @@
         [square(width, jnp.bfloat16), jax.ShapeDtypeStruct((width, half), jnp.bfloat16), square(half), square(half)],
         block_10[:half], block_10[half:], block_01[half:], block_11[:half], block_11[half:], pieces_0)
     rows, above, above_other, tile_inverse_1 = lax.optimization_barrier((rows, above, above_other, tile_inverse_1))
-    above_0, above_1 = by_row(above, above_other, my_row)
     other = swap(rows, "col", 1)
     mirror = jax.ShapeDtypeStruct((col_blocks, width, width), jnp.bfloat16)
     lower_1, pieces_1, mirror_0, later = call_factor(
         second_kernel, "factor_second", [square(width), pieces, mirror, mirror],
-        rest_11, upper_1, tile_inverse_1, pieces_0, panel_10, above_0, above_1)
+        ids, rest_11, upper_1, tile_inverse_1, pieces_0, panel_10, above, above_other)
     other, lower_1 = lax.optimization_barrier((other, lower_1))
     column_0 = jnp.where(even, rows, other)
     column_1 = jnp.where(even, other, rows)
-    ids = jnp.stack([my_row, my_col, lax.axis_size("row"), lax.axis_size("col")]).astype(jnp.int32)
     panels, schur = update(
         ids, column_0, column_1, blocks, mirror_0, later, lower_0, lower_1, pieces_0, pieces_1, panel_10)
     return (panels[None], schur[None, :, None])

time: 54.5 us -> 52.7 us (0.967)
  other arithmetic: 1.38 us -> 0.41 us
  local copies, waits for them, and re-layouts: 3.05 us -> 2.35 us
    select_n x1 -> x0, other arithmetic: 0.99 us -> none  [by_row(): return (jnp.where(even, block, other), jnp.where(even, other, block))]
    unnamed x6 -> x4, local copies, waits for them, and re-layouts: 1.92 us -> 1.22 us
  transfers between devices with their start and end apart: 12 -> 12, of which waited for: 5 -> 5; matrix products, arithmetic and copies ran while one was open for 4% -> 3% of each run, Pallas kernels for 37% -> 39%
where the time goes in v4:
time: 52.7 us; the launch traced here: 52.4 us
  Pallas kernels  24 us (46%)
  starting transfers between devices  14.8 us (28%)
  waiting for transfers between devices  9.81 us (19%)
  local copies, waits for them, and re-layouts  2.35 us (4%)
  between operations  1.03 us (2%)
    pallas_call x4, Pallas kernels, call_factor(): pl.pallas_call(kernel, in_specs=in_specs, out_shape=shapes, name=name, co...  20.5 us
    ppermute x3, starting transfers between devices, diagonal_along(): got = lax.ppermute(quarters, ('row', 'col'), pairs)  7.53 us
    ppermute x8, starting transfers between devices, swap(): return lax.ppermute(block, axis, [(d, d ^ distance) for d in range(count)])  5.94 us
    ppermute x1, waiting for transfers between devices, first_stride(): return (block, lax.ppermute(block, 'col', pairs))  5.15 us
    ppermute x8, waiting for transfers between devices, swap(): return lax.ppermute(block, axis, [(d, d ^ distance) for d in range(count)])  4.29 us
    pallas_call x1, Pallas kernels, update(): pl.pallas_call(update_kernel, in_specs=[pl.BlockSpec(memory_space=pltpu.S...  3.48 us
    ppermute x1, starting transfers between devices, first_stride(): return (block, lax.ppermute(block, 'col', pairs))  1.32 us
    unnamed x4, local copies, waits for them, and re-layouts  1.22 us
  transfers between devices with their start and end apart: 12, of which 5 were waited for; matrix products, arithmetic and copies ran while one was open for 3% of the time, Pallas kernels for 39%

profile of v4, /device:TPU:1, one launch (start us, length us, event | category | flops | bytes accessed | tf_op | source)
XLA Modules:
  0.0 52.4 jit_solution(12183998977117215056)
XLA Ops:
  0.6 0.0 copy-start
  0.6 1.2 %copy-done = bf16[1,4,1,2,256,256]{5,4,3,2,1,0:T(8,128)(2,1)S(1)} copy-done((bf16[1,4,1,2,256,256]{5,4,3,2,1,0:T(8,128)(2,1)S(1)}, bf16[1,4,1,2,256,256]{5,4,3,2,1,0:T(8,128)(2,1)}, u32[]{:S(2)}) %copy-start) | copy-done | bytes 1048600
  1.9 0.1 pack.1
  1.9 4.2 %collective-permute-start.2 = (bf16[384,128]{1,0:T(8,128)(2,1)S(1)}, bf16[384,128]{1,0:T(8,128)(2,1)S(1)}, u32[]{:S(2)}, u32[]{:S(2)}) collective-permute-start(bf16[384,128]{1,0:T(8,128)(2,1)S(1)} %pack.1), channel_id=1, source_target_pairs={{0,2},{1,3},{8,10},{9,11}} | collective-permute-start | bytes 294920 | tf_op jit(solution)/shard_map/ppermute | solution.py:308
  6.1 1.7 %collective-permute-start.1 = (bf16[384,128]{1,0:T(8,128)(2,1)S(1)}, bf16[384,128]{1,0:T(8,128)(2,1)S(1)}, u32[]{:S(2)}, u32[]{:S(2)}) collective-permute-start(bf16[384,128]{1,0:T(8,128)(2,1)S(1)} %pack.1), channel_id=1, source_target_pairs={{0,4},{1,5},{8,12},{9,13}} | collective-permute-start | bytes 294920 | tf_op jit(solution)/shard_map/ppermute | solution.py:308
  7.8 1.7 %collective-permute-start = (bf16[384,128]{1,0:T(8,128)(2,1)S(1)}, bf16[384,128]{1,0:T(8,128)(2,1)S(1)}, u32[]{:S(2)}, u32[]{:S(2)}) collective-permute-start(bf16[384,128]{1,0:T(8,128)(2,1)S(1)} %pack.1), channel_id=1, source_target_pairs={{0,6},{1,7},{8,14},{9,15}} | collective-permute-start | bytes 294920 | tf_op jit(solution)/shard_map/ppermute | solution.py:308
  9.5 1.1 %slice_bitcast_fusion = bf16[4,256,256]{2,1,0:T(8,128)(2,1)S(1)} fusion(bf16[4,2,256,256]{3,2,1,0:T(8,128)(2,1)} %bitcast.29), kind=kLoop, calls=%fused_computation | loop fusion | bytes 1048576 | tf_op jit(solution)/shard_map/squeeze | solution.py:374
  10.6 1.3 %collective-permute-start.6 = (bf16[4,256,256]{2,1,0:T(8,128)(2,1)S(1)}, bf16[4,256,256]{2,1,0:T(8,128)(2,1)S(1)}, u32[]{:S(2)}, u32[]{:S(2)}) collective-permute-start(bf16[4,256,256]{2,1,0:T(8,128)(2,1)S(1)} %slice_bitcast_fusion), channel_id=1, source_target_pairs={{0,4},{1,5},{8,12},{9,13},{16,20},{17,21},{24,28},{25,29}} | collective-permute-start | bytes 1572872 | tf_op jit(solution)/shard_map/ppermute | solution.py:347
  11.9 0.0 collective-permute-done.2
  12.0 0.4 collective-permute-done
  12.3 1.3 %collective-permute-start.5 = (bf16[384,128]{1,0:T(8,128)(2,1)S(1)}, bf16[384,128]{1,0:T(8,128)(2,1)S(1)}, u32[]{:S(2)}, u32[]{:S(2)}) collective-permute-start(bf16[384,128]{1,0:T(8,128)(2,1)S(1)} %select_select_fusion), channel_id=1, source_target_pairs={{0,8},{8,0},{16,24},{24,16},{1,9},{9,1},{17,25},{25,17},{2,10},{10... | collective-permute-start | bytes 294920 | tf_op jit(solution)/shard_map/ppermute | solution.py:297
  13.6 0.0 collective-permute-start.4
  13.6 1.4 %collective-permute-start.3 = (bf16[384,128]{1,0:T(8,128)(2,1)S(1)}, bf16[384,128]{1,0:T(8,128)(2,1)S(1)}, u32[]{:S(2)}, u32[]{:S(2)}) collective-permute-start(bf16[384,128]{1,0:T(8,128)(2,1)S(1)} %select_select_fusion), channel_id=1, source_target_pairs={{0,24},{8,16},{16,8},{24,0},{1,25},{9,17},{17,9},{25,1},{2,26},{10... | collective-permute-start | bytes 294920 | tf_op jit(solution)/shard_map/ppermute | solution.py:297
  15.1 0.0 collective-permute-start.8
  15.1 0.8 %collective-permute-done.5 = bf16[384,128]{1,0:T(8,128)(2,1)S(1)} collective-permute-done((bf16[384,128]{1,0:T(8,128)(2,1)S(1)}, bf16[384,128]{1,0:T(8,128)(2,1)S(1)}, u32[]{:S(2)}, u32[]{:S(2)}) %collective-permute-start.5) | collective-permute-done | bytes 98336 | tf_op jit(solution)/shard_map/ppermute | solution.py:297
  15.9 2.6 %collective-permute-done.4 = bf16[384,128]{1,0:T(8,128)(2,1)S(1)} collective-permute-done((bf16[384,128]{1,0:T(8,128)(2,1)S(1)}, bf16[384,128]{1,0:T(8,128)(2,1)S(1)}, u32[]{:S(2)}, u32[]{:S(2)}) %collective-permute-start.4) | collective-permute-done | bytes 98336 | tf_op jit(solution)/shard_map/ppermute | solution.py:297
  18.5 5.2 %collective-permute-done.6 = bf16[4,256,256]{2,1,0:T(8,128)(2,1)S(1)} collective-permute-done((bf16[4,256,256]{2,1,0:T(8,128)(2,1)S(1)}, bf16[4,256,256]{2,1,0:T(8,128)(2,1)S(1)}, u32[]{:S(2)}, u32[]{:S(2)}) %collective-permute-start.6) | collective-permute-done | bytes 524320 | tf_op jit(solution)/shard_map/ppermute | solution.py:347
  23.7 0.9 %collective-permute-start.9 = (bf16[2,384,128]{2,1,0:T(8,128)(2,1)S(1)}, bf16[2,384,128]{2,1,0:T(8,128)(2,1)S(1)}, u32[]{:S(2)}, u32[]{:S(2)}) collective-permute-start(bf16[2,384,128]{2,1,0:T(8,128)(2,1)S(1)} %pad_maximum_fusion), channel_id=1, source_target_pairs={{0,1},{1,0},{2,3},{3,2},{4,5},{5,4},{6,7},{7,6},{8,9},{9,8},{10,11... | collective-permute-start | bytes 589832 | tf_op jit(solution)/shard_map/ppermute | solution.py:297
  24.6 0.1 broadcast_select_fusion
  24.7 0.1 collective-permute-start.7
  24.7 0.9 %collective-permute-done.9 = bf16[2,384,128]{2,1,0:T(8,128)(2,1)S(1)} collective-permute-done((bf16[2,384,128]{2,1,0:T(8,128)(2,1)S(1)}, bf16[2,384,128]{2,1,0:T(8,128)(2,1)S(1)}, u32[]{:S(2)}, u32[]{:S(2)}) %collective-permute-start.9) | collective-permute-done | bytes 196640 | tf_op jit(solution)/shard_map/ppermute | solution.py:297
  25.7 4.3 %factor_start.1 = (f32[128,128]{1,0:T(8,128)S(1)}, f32[128,128]{1,0:T(8,128)S(1)}) custom-call(bf16[128,128]{1,0:T(8,128)(2,1)S(1)} %get-tuple-element.71.quarter_ref), custom_call_target="tpu_custom_call" | custom-call | flops 1000000 | bytes 10000 | tf_op jit(solution)/shard_map/factor_start/pallas_call | solution.py:239
  30.0 0.0 collective-permute-done.8
  30.1 1.3 %collective-permute-start.10 = (bf16[2,256,256]{2,1,0:T(8,128)(2,1)S(1)}, bf16[2,256,256]{2,1,0:T(8,128)(2,1)S(1)}, u32[]{:S(2)}, u32[]{:S(2)}) collective-permute-start(bf16[2,256,256]{2,1,0:T(8,128)(2,1)S(1)} %broadcast_select_fusion.4.above_ref), channel_id=1, source_target_pairs={{0,8},{8,0},{16,24},{24,16},{1,9},{9,1},{17,25},{25,17},{2,10},{10... | collective-permute-start | bytes 786440 | tf_op jit(solution)/shard_map/ppermute | solution.py:297
  31.4 5.4 %factor_first.1 = (f32[256,256]{1,0:T(8,128)S(1)}, bf16[3,256,256]{2,1,0:T(8,128)(2,1)S(1)}) custom-call(bf16[256,128]{1,0:T(8,128)(2,1)S(1)} %get-tuple-element.66.rest_ref, f32[128,128]{1,0:T(8,128)S(1)} %get-tuple-element.38.upper_ref, f32[128,128]{1,0:T(8,128)S(1)} %get-tuple-element.39.tile_inverse_ref), custom_call_target="tpu_custom_call" | custom-call | flops 1000000 | bytes 10000 | tf_op jit(solution)/shard_map/factor_first/pallas_call | solution.py:239
  36.8 4.8 %factor_second_start.1 = (bf16[256,256]{1,0:T(8,128)(2,1)S(1)}, bf16[256,128]{1,0:T(8,128)(2,1)S(1)}, f32[128,128]{1,0:T(8,128)S(1)}, f32[128,128]{1,0:T(8,128)S(1)}) custom-call(bf16[128,128]{1,0:T(8,128)(2,1)S(1)} %get-tuple-element.70.top_10_ref, bf16[256,128]{1,0:T(8,128)(2,1)S(1)} %get-tuple-element.67.rest_10_ref, ...), custom_call_target="tpu_custom_call" | custom-call | flops 1000000 | bytes 10000 | tf_op jit(solution)/shard_map/factor_second_start/pallas_call | solution.py:239
  41.6 0.1 broadcast_select_fusion.1
  41.7 0.9 %collective-permute-start.11 = (bf16[4,256,256]{2,1,0:T(8,128)(2,1)S(1)}, bf16[4,256,256]{2,1,0:T(8,128)(2,1)S(1)}, u32[]{:S(2)}, u32[]{:S(2)}) collective-permute-start(bf16[4,256,256]{2,1,0:T(8,128)(2,1)S(1)} %broadcast_select_fusion.1), channel_id=1, source_target_pairs={{0,1},{1,0},{2,3},{3,2},{4,5},{5,4},{6,7},{7,6},{8,9},{9,8},{10,11... | collective-permute-start | bytes 1572872 | tf_op jit(solution)/shard_map/ppermute | solution.py:297
  42.6 0.1 pad_add_fusion.ids_ref
  42.7 6.0 %factor_second.1 = (f32[256,256]{1,0:T(8,128)S(1)}, bf16[3,256,256]{2,1,0:T(8,128)(2,1)S(1)}, bf16[2,256,256]{2,1,0:T(8,128)(2,1)S(1)}, bf16[2,256,256]{2,1,0:T(8,128)(2,1)S(1)}) custom-call(s32[4]{0:T(128)S(1)} %pad_add_fusion.ids_ref, bf16[256,128]{1,0:T(8,128)(2,1)S(1)} %get-tuple-element.43.rest_ref, f32[128,128]{1,0:T(8,128)S(1)} %get-tuple-element.44.upper_ref, ...), custom_call_target="tpu_custom_call" | custom-call | flops 1000000 | bytes 10000 | tf_op jit(solution)/shard_map/factor_second/pallas_call | solution.py:239
  48.7 0.1 broadcast_select_fusion.2
  48.8 3.5 %solve_and_update.1 = (f32[4,2,256,256]{3,2,1,0:T(8,128)}, bf16[4,2,256,256]{3,2,1,0:T(8,128)(2,1)}) custom-call(s32[4]{0:T(128)S(1)} %pad_add_fusion.ids_ref, bf16[4,256,256]{2,1,0:T(8,128)(2,1)S(1)} %get-tuple-element.61.column_0_ref, bf16[4,256,256]{2,1,0:T(8,128)(2,1)S(1)} %get-tuple-element.60.column_1_ref, bf16[4,2,256,256]{3,2,1,0:T(8,128)(2,1)S(1)} %bitcast.30, ...), custom_call_target="tpu_custom_call" | custom-call | flops 2000000000 | bytes 6000000 | tf_op jit(solution)/shard_map/solve_and_update/pallas_call | solution.py:253
  (16 shorter events, 0.2 us)
Async XLA Ops:
  0.6 1.2 %copy-start = (bf16[1,4,1,2,256,256]{5,4,3,2,1,0:T(8,128)(2,1)S(1)}, bf16[1,4,1,2,256,256]{5,4,3,2,1,0:T(8,128)(2,1)}, u32[]{:S(2)}) copy-start(bf16[1,4,1,2,256,256]{5,4,3,2,1,0:T(8,128)(2,1)} %kernel_ref.1) | copy-start | bytes 3145732
  1.9 8.7 %copy-start.1 = (bf16[1,4,1,2,256,256]{5,4,3,2,1,0:T(8,128)(2,1)S(1)}, bf16[1,4,1,2,256,256]{5,4,3,2,1,0:T(8,128)(2,1)}, u32[]{:S(2)}) copy-start(bf16[1,4,1,2,256,256]{5,4,3,2,1,0:T(8,128)(2,1)} %kernel_ref.1) | copy-start | bytes 3145732
  1.9 10.0 %collective-permute-start.2 = (bf16[384,128]{1,0:T(8,128)(2,1)S(1)}, bf16[384,128]{1,0:T(8,128)(2,1)S(1)}, u32[]{:S(2)}, u32[]{:S(2)}) collective-permute-start(bf16[384,128]{1,0:T(8,128)(2,1)S(1)} %pack.1), channel_id=1, source_target_pairs={{0,2},{1,3},{8,10},{9,11}} | collective-permute-start | bytes 294920 | tf_op jit(solution)/shard_map/ppermute | solution.py:308
  6.1 5.9 %collective-permute-start.1 = (bf16[384,128]{1,0:T(8,128)(2,1)S(1)}, bf16[384,128]{1,0:T(8,128)(2,1)S(1)}, u32[]{:S(2)}, u32[]{:S(2)}) collective-permute-start(bf16[384,128]{1,0:T(8,128)(2,1)S(1)} %pack.1), channel_id=1, source_target_pairs={{0,4},{1,5},{8,12},{9,13}} | collective-permute-start | bytes 294920 | tf_op jit(solution)/shard_map/ppermute | solution.py:308
  7.8 4.5 %collective-permute-start = (bf16[384,128]{1,0:T(8,128)(2,1)S(1)}, bf16[384,128]{1,0:T(8,128)(2,1)S(1)}, u32[]{:S(2)}, u32[]{:S(2)}) collective-permute-start(bf16[384,128]{1,0:T(8,128)(2,1)S(1)} %pack.1), channel_id=1, source_target_pairs={{0,6},{1,7},{8,14},{9,15}} | collective-permute-start | bytes 294920 | tf_op jit(solution)/shard_map/ppermute | solution.py:308
  10.6 13.1 %collective-permute-start.6 = (bf16[4,256,256]{2,1,0:T(8,128)(2,1)S(1)}, bf16[4,256,256]{2,1,0:T(8,128)(2,1)S(1)}, u32[]{:S(2)}, u32[]{:S(2)}) collective-permute-start(bf16[4,256,256]{2,1,0:T(8,128)(2,1)S(1)} %slice_bitcast_fusion), channel_id=1, source_target_pairs={{0,4},{1,5},{8,12},{9,13},{16,20},{17,21},{24,28},{25,29}} | collective-permute-start | bytes 1572872 | tf_op jit(solution)/shard_map/ppermute | solution.py:347
  12.3 3.5 %collective-permute-start.5 = (bf16[384,128]{1,0:T(8,128)(2,1)S(1)}, bf16[384,128]{1,0:T(8,128)(2,1)S(1)}, u32[]{:S(2)}, u32[]{:S(2)}) collective-permute-start(bf16[384,128]{1,0:T(8,128)(2,1)S(1)} %select_select_fusion), channel_id=1, source_target_pairs={{0,8},{8,0},{16,24},{24,16},{1,9},{9,1},{17,25},{25,17},{2,10},{10... | collective-permute-start | bytes 294920 | tf_op jit(solution)/shard_map/ppermute | solution.py:297
  13.6 4.8 %collective-permute-start.4 = (bf16[384,128]{1,0:T(8,128)(2,1)S(1)}, bf16[384,128]{1,0:T(8,128)(2,1)S(1)}, u32[]{:S(2)}, u32[]{:S(2)}) collective-permute-start(bf16[384,128]{1,0:T(8,128)(2,1)S(1)} %select_select_fusion), channel_id=1, source_target_pairs={{0,16},{8,24},{16,0},{24,8},{1,17},{9,25},{17,1},{25,9},{2,18},{10... | collective-permute-start | bytes 294920 | tf_op jit(solution)/shard_map/ppermute | solution.py:297
  13.6 4.8 %collective-permute-start.3 = (bf16[384,128]{1,0:T(8,128)(2,1)S(1)}, bf16[384,128]{1,0:T(8,128)(2,1)S(1)}, u32[]{:S(2)}, u32[]{:S(2)}) collective-permute-start(bf16[384,128]{1,0:T(8,128)(2,1)S(1)} %select_select_fusion), channel_id=1, source_target_pairs={{0,24},{8,16},{16,8},{24,0},{1,25},{9,17},{17,9},{25,1},{2,26},{10... | collective-permute-start | bytes 294920 | tf_op jit(solution)/shard_map/ppermute | solution.py:297
  15.1 15.0 %collective-permute-start.8 = (bf16[2,256,256]{2,1,0:T(8,128)(2,1)S(1)}, bf16[2,256,256]{2,1,0:T(8,128)(2,1)S(1)}, u32[]{:S(2)}, u32[]{:S(2)}) collective-permute-start(bf16[2,256,256]{2,1,0:T(8,128)(2,1)S(1)} %slice_bitcast_fusion.1), channel_id=1, source_target_pairs={{0,16},{8,24},{16,0},{24,8},{1,17},{9,25},{17,1},{25,9},{2,18},{10... | collective-permute-start | bytes 786440 | tf_op jit(solution)/shard_map/ppermute | solution.py:297
  23.7 2.0 %collective-permute-start.9 = (bf16[2,384,128]{2,1,0:T(8,128)(2,1)S(1)}, bf16[2,384,128]{2,1,0:T(8,128)(2,1)S(1)}, u32[]{:S(2)}, u32[]{:S(2)}) collective-permute-start(bf16[2,384,128]{2,1,0:T(8,128)(2,1)S(1)} %pad_maximum_fusion), channel_id=1, source_target_pairs={{0,1},{1,0},{2,3},{3,2},{4,5},{5,4},{6,7},{7,6},{8,9},{9,8},{10,11... | collective-permute-start | bytes 589832 | tf_op jit(solution)/shard_map/ppermute | solution.py:297
  24.7 16.9 %collective-permute-start.7 = (bf16[4,256,256]{2,1,0:T(8,128)(2,1)S(1)}, bf16[4,256,256]{2,1,0:T(8,128)(2,1)S(1)}, u32[]{:S(2)}, u32[]{:S(2)}) collective-permute-start(bf16[4,256,256]{2,1,0:T(8,128)(2,1)S(1)} %broadcast_select_fusion), channel_id=1, source_target_pairs={{0,2},{1,3},{2,0},{3,1},{4,6},{5,7},{6,4},{7,5},{8,10},{9,11},{10,... | collective-permute-start | bytes 1572872 | tf_op jit(solution)/shard_map/ppermute | solution.py:297
  30.1 11.6 %collective-permute-start.10 = (bf16[2,256,256]{2,1,0:T(8,128)(2,1)S(1)}, bf16[2,256,256]{2,1,0:T(8,128)(2,1)S(1)}, u32[]{:S(2)}, u32[]{:S(2)}) collective-permute-start(bf16[2,256,256]{2,1,0:T(8,128)(2,1)S(1)} %broadcast_select_fusion.4.above_ref), channel_id=1, source_target_pairs={{0,8},{8,0},{16,24},{24,16},{1,9},{9,1},{17,25},{25,17},{2,10},{10... | collective-permute-start | bytes 786440 | tf_op jit(solution)/shard_map/ppermute | solution.py:297
  41.7 7.0 %collective-permute-start.11 = (bf16[4,256,256]{2,1,0:T(8,128)(2,1)S(1)}, bf16[4,256,256]{2,1,0:T(8,128)(2,1)S(1)}, u32[]{:S(2)}, u32[]{:S(2)}) collective-permute-start(bf16[4,256,256]{2,1,0:T(8,128)(2,1)S(1)} %broadcast_select_fusion.1), channel_id=1, source_target_pairs={{0,1},{1,0},{2,3},{3,2},{4,5},{5,4},{6,7},{7,6},{8,9},{9,8},{10,11... | collective-permute-start | bytes 1572872 | tf_op jit(solution)/shard_map/ppermute | solution.py:297

commit v5 on v4

--- a/solution.py
+++ b/solution.py
@@ -160,19 +160,29 @@
 
 def second_kernel(
     ids_ref, rest_ref, upper_ref, tile_inverse_ref, pieces_0_ref, panel_ref, above_ref, other_ref,
-    lower_ref, pieces_1_ref, mirror_ref, later_ref,
+    lower_ref, pieces_1_ref, mirror_ref, later_ref, above_0_ref, above_1_ref,
 ):
     half = rest_ref.shape[1]
     even = ids_ref[0] % 2 == 0
     tasks = []
+
+    @pl.when(even)
+    def _():
+        above_0_ref[...] = above_ref[...]
+        above_1_ref[...] = other_ref[...]
+
+    @pl.when(jnp.logical_not(even))
+    def _():
+        above_0_ref[...] = other_ref[...]
+        above_1_ref[...] = above_ref[...]
+
     for m in range(above_ref.shape[0]):
         def mirror(m=m):
-            above = jnp.where(even, above_ref[m], other_ref[m])
-            mirror_ref[m] = product(pieces_0_ref, above).astype(jnp.bfloat16)
+            mirror_ref[m] = product(pieces_0_ref, above_0_ref[m]).astype(jnp.bfloat16)
 
         def later(m=m):
-            above = jnp.where(even, other_ref[m], above_ref[m]).astype(jnp.float32)
-            later_ref[m] = (above - mul(panel_ref[...], mirror_ref[m])).astype(jnp.bfloat16)
+            change = mul(panel_ref[...], mirror_ref[m])
+            later_ref[m] = (above_1_ref[m].astype(jnp.float32) - change).astype(jnp.bfloat16)
 
         tasks += [mirror, later]
     factor_rest(
@@ -233,11 +243,11 @@
 FACTOR_COST = pl.CostEstimate(flops=10**6, bytes_accessed=10**4, transcendentals=0)
 
 
-def call_factor(kernel, name, shapes, *operands):
+def call_factor(kernel, name, shapes, *operands, scratch=()):
     in_specs = [
         pl.BlockSpec(memory_space=pltpu.SMEM if x.dtype == jnp.int32 else pltpu.VMEM) for x in operands]
     return pl.pallas_call(
-        kernel, in_specs=in_specs, out_shape=shapes, name=name, cost_estimate=FACTOR_COST,
+        kernel, in_specs=in_specs, out_shape=shapes, scratch_shapes=scratch, name=name, cost_estimate=FACTOR_COST,
         compiler_params=pltpu.CompilerParams(vmem_limit_bytes=VMEM_LIMIT),
     )(*operands)
 
@@ -371,11 +381,12 @@
     half = width // 2
     ids = jnp.stack([my_row, my_col, lax.axis_size("row"), lax.axis_size("col")]).astype(jnp.int32)
     quarters = pack(kernel)
-    rows, above, _ = lax.optimization_barrier((blocks[:, 0], blocks[0], quarters))
+    rows, _ = lax.optimization_barrier((blocks[:, 0], quarters))
     rows, rows_got = first_stride(rows)
-    above, above_got = first_reach(above)
     along = diagonal_along(quarters, my_col)
     pair = diagonal_down(along, my_row)
+    pair, above = lax.optimization_barrier((pair, blocks[0]))
+    above, above_got = first_reach(above)
     pair, rows, rows_got = lax.optimization_barrier((pair, rows, rows_got))
     block_00, block_01, block_10, block_11 = both_cores(pair, my_col)
     rows = other_strides(rows, rows_got, my_col)
@@ -395,7 +406,8 @@
     mirror = jax.ShapeDtypeStruct((col_blocks, width, width), jnp.bfloat16)
     lower_1, pieces_1, mirror_0, later = call_factor(
         second_kernel, "factor_second", [square(width), pieces, mirror, mirror],
-        ids, rest_11, upper_1, tile_inverse_1, pieces_0, panel_10, above, above_other)
+        ids, rest_11, upper_1, tile_inverse_1, pieces_0, panel_10, above, above_other,
+        scratch=[pltpu.VMEM(mirror.shape, mirror.dtype)] * 2)
     other, lower_1 = lax.optimization_barrier((other, lower_1))
     column_0 = jnp.where(even, rows, other)
     column_1 = jnp.where(even, other, rows)

time: 52.7 us -> 52.7 us (level)
  waiting for transfers between devices: 9.81 us -> 7.93 us
  starting transfers between devices: 14.8 us -> 16.6 us
    ppermute x1, waiting for transfers between devices: 5.15 us -> 3.29 us  [first_stride(): return (block, lax.ppermute(block, 'col', pairs))]
    ppermute x8, starting transfers between devices: 5.94 us -> 7.77 us  [swap(): return lax.ppermute(block, axis, [(d, d ^ distance) for d in range(count)])]
where the time goes in v5:
time: 52.7 us; the launch traced here: 52.5 us
  Pallas kernels  24.1 us (46%)
  starting transfers between devices  16.6 us (31%)
  waiting for transfers between devices  7.93 us (15%)
  local copies, waits for them, and re-layouts  2.35 us (4%)
  between operations  1.07 us (2%)
    pallas_call x4, Pallas kernels, call_factor(): pl.pallas_call(kernel, in_specs=in_specs, out_shape=shapes, scratch_shape...  20.5 us
    ppermute x8, starting transfers between devices, swap(): return lax.ppermute(block, axis, [(d, d ^ distance) for d in range(count)])  7.77 us
    ppermute x3, starting transfers between devices, diagonal_along(): got = lax.ppermute(quarters, ('row', 'col'), pairs)  7.53 us
    ppermute x8, waiting for transfers between devices, swap(): return lax.ppermute(block, axis, [(d, d ^ distance) for d in range(count)])  4.24 us
    pallas_call x1, Pallas kernels, update(): pl.pallas_call(update_kernel, in_specs=[pl.BlockSpec(memory_space=pltpu.S...  3.48 us
    ppermute x1, waiting for transfers between devices, first_stride(): return (block, lax.ppermute(block, 'col', pairs))  3.29 us
    ppermute x1, starting transfers between devices, first_stride(): return (block, lax.ppermute(block, 'col', pairs))  1.32 us
    unnamed x4, local copies, waits for them, and re-layouts  1.22 us
  transfers between devices with their start and end apart: 12, of which 5 were waited for; matrix products, arithmetic and copies ran while one was open for 3% of the time, Pallas kernels for 39%

profile of v5, /device:TPU:1, one launch (start us, length us, event | category | flops | bytes accessed | tf_op | source)
XLA Modules:
  0.0 52.5 jit_solution(13338840891981731837)
XLA Ops:
  0.6 0.0 copy-start
  0.6 1.2 %copy-done = bf16[1,4,1,2,256,256]{5,4,3,2,1,0:T(8,128)(2,1)S(1)} copy-done((bf16[1,4,1,2,256,256]{5,4,3,2,1,0:T(8,128)(2,1)S(1)}, bf16[1,4,1,2,256,256]{5,4,3,2,1,0:T(8,128)(2,1)}, u32[]{:S(2)}) %copy-start) | copy-done | bytes 1048600
  1.9 0.1 pack.1
  1.9 4.2 %collective-permute-start.2 = (bf16[384,128]{1,0:T(8,128)(2,1)S(1)}, bf16[384,128]{1,0:T(8,128)(2,1)S(1)}, u32[]{:S(2)}, u32[]{:S(2)}) collective-permute-start(bf16[384,128]{1,0:T(8,128)(2,1)S(1)} %pack.1), channel_id=1, source_target_pairs={{0,2},{1,3},{8,10},{9,11}} | collective-permute-start | bytes 294920 | tf_op jit(solution)/shard_map/ppermute | solution.py:318
  6.1 1.7 %collective-permute-start.1 = (bf16[384,128]{1,0:T(8,128)(2,1)S(1)}, bf16[384,128]{1,0:T(8,128)(2,1)S(1)}, u32[]{:S(2)}, u32[]{:S(2)}) collective-permute-start(bf16[384,128]{1,0:T(8,128)(2,1)S(1)} %pack.1), channel_id=1, source_target_pairs={{0,4},{1,5},{8,12},{9,13}} | collective-permute-start | bytes 294920 | tf_op jit(solution)/shard_map/ppermute | solution.py:318
  7.8 1.7 %collective-permute-start = (bf16[384,128]{1,0:T(8,128)(2,1)S(1)}, bf16[384,128]{1,0:T(8,128)(2,1)S(1)}, u32[]{:S(2)}, u32[]{:S(2)}) collective-permute-start(bf16[384,128]{1,0:T(8,128)(2,1)S(1)} %pack.1), channel_id=1, source_target_pairs={{0,6},{1,7},{8,14},{9,15}} | collective-permute-start | bytes 294920 | tf_op jit(solution)/shard_map/ppermute | solution.py:318
  9.5 1.1 %slice_bitcast_fusion = bf16[4,256,256]{2,1,0:T(8,128)(2,1)S(1)} fusion(bf16[4,2,256,256]{3,2,1,0:T(8,128)(2,1)} %bitcast.29), kind=kLoop, calls=%fused_computation | loop fusion | bytes 1048576 | tf_op jit(solution)/shard_map/squeeze | solution.py:384
  10.6 1.3 %collective-permute-start.6 = (bf16[4,256,256]{2,1,0:T(8,128)(2,1)S(1)}, bf16[4,256,256]{2,1,0:T(8,128)(2,1)S(1)}, u32[]{:S(2)}, u32[]{:S(2)}) collective-permute-start(bf16[4,256,256]{2,1,0:T(8,128)(2,1)S(1)} %slice_bitcast_fusion), channel_id=1, source_target_pairs={{0,4},{1,5},{8,12},{9,13},{16,20},{17,21},{24,28},{25,29}} | collective-permute-start | bytes 1572872 | tf_op jit(solution)/shard_map/ppermute | solution.py:357
  11.9 0.0 collective-permute-done.2
  11.9 0.0 collective-permute-done.1
  11.9 0.4 collective-permute-done
  12.3 1.3 %collective-permute-start.5 = (bf16[384,128]{1,0:T(8,128)(2,1)S(1)}, bf16[384,128]{1,0:T(8,128)(2,1)S(1)}, u32[]{:S(2)}, u32[]{:S(2)}) collective-permute-start(bf16[384,128]{1,0:T(8,128)(2,1)S(1)} %select_select_fusion), channel_id=1, source_target_pairs={{0,8},{8,0},{16,24},{24,16},{1,9},{9,1},{17,25},{25,17},{2,10},{10... | collective-permute-start | bytes 294920 | tf_op jit(solution)/shard_map/ppermute | solution.py:307
  13.6 0.0 collective-permute-start.4
  13.6 1.4 %collective-permute-start.3 = (bf16[384,128]{1,0:T(8,128)(2,1)S(1)}, bf16[384,128]{1,0:T(8,128)(2,1)S(1)}, u32[]{:S(2)}, u32[]{:S(2)}) collective-permute-start(bf16[384,128]{1,0:T(8,128)(2,1)S(1)} %select_select_fusion), channel_id=1, source_target_pairs={{0,24},{8,16},{16,8},{24,0},{1,25},{9,17},{17,9},{25,1},{2,26},{10... | collective-permute-start | bytes 294920 | tf_op jit(solution)/shard_map/ppermute | solution.py:307
  15.1 0.7 %collective-permute-done.5 = bf16[384,128]{1,0:T(8,128)(2,1)S(1)} collective-permute-done((bf16[384,128]{1,0:T(8,128)(2,1)S(1)}, bf16[384,128]{1,0:T(8,128)(2,1)S(1)}, u32[]{:S(2)}, u32[]{:S(2)}) %collective-permute-start.5) | collective-permute-done | bytes 98336 | tf_op jit(solution)/shard_map/ppermute | solution.py:307
  15.9 2.6 %collective-permute-done.4 = bf16[384,128]{1,0:T(8,128)(2,1)S(1)} collective-permute-done((bf16[384,128]{1,0:T(8,128)(2,1)S(1)}, bf16[384,128]{1,0:T(8,128)(2,1)S(1)}, u32[]{:S(2)}, u32[]{:S(2)}) %collective-permute-start.4) | collective-permute-done | bytes 98336 | tf_op jit(solution)/shard_map/ppermute | solution.py:307
  18.5 1.8 %collective-permute-start.8 = (bf16[2,256,256]{2,1,0:T(8,128)(2,1)S(1)}, bf16[2,256,256]{2,1,0:T(8,128)(2,1)S(1)}, u32[]{:S(2)}, u32[]{:S(2)}) collective-permute-start(bf16[2,256,256]{2,1,0:T(8,128)(2,1)S(1)} %slice_bitcast_fusion.1), channel_id=1, source_target_pairs={{0,16},{8,24},{16,0},{24,8},{1,17},{9,25},{17,1},{25,9},{2,18},{10... | collective-permute-start | bytes 786440 | tf_op jit(solution)/shard_map/ppermute | solution.py:307
  20.4 3.3 %collective-permute-done.6 = bf16[4,256,256]{2,1,0:T(8,128)(2,1)S(1)} collective-permute-done((bf16[4,256,256]{2,1,0:T(8,128)(2,1)S(1)}, bf16[4,256,256]{2,1,0:T(8,128)(2,1)S(1)}, u32[]{:S(2)}, u32[]{:S(2)}) %collective-permute-start.6) | collective-permute-done | bytes 524320 | tf_op jit(solution)/shard_map/ppermute | solution.py:357
  23.6 1.0 %collective-permute-start.9 = (bf16[2,384,128]{2,1,0:T(8,128)(2,1)S(1)}, bf16[2,384,128]{2,1,0:T(8,128)(2,1)S(1)}, u32[]{:S(2)}, u32[]{:S(2)}) collective-permute-start(bf16[2,384,128]{2,1,0:T(8,128)(2,1)S(1)} %pad_maximum_fusion), channel_id=1, source_target_pairs={{0,1},{1,0},{2,3},{3,2},{4,5},{5,4},{6,7},{7,6},{8,9},{9,8},{10,11... | collective-permute-start | bytes 589832 | tf_op jit(solution)/shard_map/ppermute | solution.py:307
  24.6 0.1 broadcast_select_fusion
  24.7 0.1 collective-permute-start.7
  24.7 0.9 %collective-permute-done.9 = bf16[2,384,128]{2,1,0:T(8,128)(2,1)S(1)} collective-permute-done((bf16[2,384,128]{2,1,0:T(8,128)(2,1)S(1)}, bf16[2,384,128]{2,1,0:T(8,128)(2,1)S(1)}, u32[]{:S(2)}, u32[]{:S(2)}) %collective-permute-start.9) | collective-permute-done | bytes 196640 | tf_op jit(solution)/shard_map/ppermute | solution.py:307
  25.7 4.3 %factor_start.1 = (f32[128,128]{1,0:T(8,128)S(1)}, f32[128,128]{1,0:T(8,128)S(1)}) custom-call(bf16[128,128]{1,0:T(8,128)(2,1)S(1)} %get-tuple-element.73.quarter_ref), custom_call_target="tpu_custom_call" | custom-call | flops 1000000 | bytes 10000 | tf_op jit(solution)/shard_map/factor_start/pallas_call | solution.py:249
  30.1 1.3 %collective-permute-start.10 = (bf16[2,256,256]{2,1,0:T(8,128)(2,1)S(1)}, bf16[2,256,256]{2,1,0:T(8,128)(2,1)S(1)}, u32[]{:S(2)}, u32[]{:S(2)}) collective-permute-start(bf16[2,256,256]{2,1,0:T(8,128)(2,1)S(1)} %broadcast_select_fusion.4.above_ref), channel_id=1, source_target_pairs={{0,8},{8,0},{16,24},{24,16},{1,9},{9,1},{17,25},{25,17},{2,10},{10... | collective-permute-start | bytes 786440 | tf_op jit(solution)/shard_map/ppermute | solution.py:307
  31.4 5.4 %factor_first.1 = (f32[256,256]{1,0:T(8,128)S(1)}, bf16[3,256,256]{2,1,0:T(8,128)(2,1)S(1)}) custom-call(bf16[256,128]{1,0:T(8,128)(2,1)S(1)} %get-tuple-element.68.rest_ref, f32[128,128]{1,0:T(8,128)S(1)} %get-tuple-element.40.upper_ref, f32[128,128]{1,0:T(8,128)S(1)} %get-tuple-element.41.tile_inverse_ref), custom_call_target="tpu_custom_call" | custom-call | flops 1000000 | bytes 10000 | tf_op jit(solution)/shard_map/factor_first/pallas_call | solution.py:249
  36.8 4.8 %factor_second_start.1 = (bf16[256,256]{1,0:T(8,128)(2,1)S(1)}, bf16[256,128]{1,0:T(8,128)(2,1)S(1)}, f32[128,128]{1,0:T(8,128)S(1)}, f32[128,128]{1,0:T(8,128)S(1)}) custom-call(bf16[128,128]{1,0:T(8,128)(2,1)S(1)} %get-tuple-element.72.top_10_ref, bf16[256,128]{1,0:T(8,128)(2,1)S(1)} %get-tuple-element.69.rest_10_ref, ...), custom_call_target="tpu_custom_call" | custom-call | flops 1000000 | bytes 10000 | tf_op jit(solution)/shard_map/factor_second_start/pallas_call | solution.py:249
  41.6 0.1 broadcast_select_fusion.1
  41.7 0.9 %collective-permute-start.11 = (bf16[4,256,256]{2,1,0:T(8,128)(2,1)S(1)}, bf16[4,256,256]{2,1,0:T(8,128)(2,1)S(1)}, u32[]{:S(2)}, u32[]{:S(2)}) collective-permute-start(bf16[4,256,256]{2,1,0:T(8,128)(2,1)S(1)} %broadcast_select_fusion.1), channel_id=1, source_target_pairs={{0,1},{1,0},{2,3},{3,2},{4,5},{5,4},{6,7},{7,6},{8,9},{9,8},{10,11... | collective-permute-start | bytes 1572872 | tf_op jit(solution)/shard_map/ppermute | solution.py:307
  42.6 0.1 pad_add_fusion.ids_ref
  42.7 6.1 %factor_second.1 = (f32[256,256]{1,0:T(8,128)S(1)}, bf16[3,256,256]{2,1,0:T(8,128)(2,1)S(1)}, bf16[2,256,256]{2,1,0:T(8,128)(2,1)S(1)}, bf16[2,256,256]{2,1,0:T(8,128)(2,1)S(1)}) custom-call(s32[4]{0:T(128)S(1)} %pad_add_fusion.ids_ref, bf16[256,128]{1,0:T(8,128)(2,1)S(1)} %get-tuple-element.45.rest_ref, f32[128,128]{1,0:T(8,128)S(1)} %get-tuple-element.46.upper_ref, ...), custom_call_target="tpu_custom_call" | custom-call | flops 1000000 | bytes 10000 | tf_op jit(solution)/shard_map/factor_second/pallas_call | solution.py:249
  48.7 0.1 broadcast_select_fusion.2
  48.8 3.5 %solve_and_update.1 = (f32[4,2,256,256]{3,2,1,0:T(8,128)}, bf16[4,2,256,256]{3,2,1,0:T(8,128)(2,1)}) custom-call(s32[4]{0:T(128)S(1)} %pad_add_fusion.ids_ref, bf16[4,256,256]{2,1,0:T(8,128)(2,1)S(1)} %get-tuple-element.63.column_0_ref, bf16[4,256,256]{2,1,0:T(8,128)(2,1)S(1)} %get-tuple-element.62.column_1_ref, bf16[4,2,256,256]{3,2,1,0:T(8,128)(2,1)S(1)} %bitcast.30, ...), custom_call_target="tpu_custom_call" | custom-call | flops 2000000000 | bytes 6000000 | tf_op jit(solution)/shard_map/solve_and_update/pallas_call | solution.py:263
  (16 shorter events, 0.2 us)
Async XLA Ops:
  0.6 1.2 %copy-start = (bf16[1,4,1,2,256,256]{5,4,3,2,1,0:T(8,128)(2,1)S(1)}, bf16[1,4,1,2,256,256]{5,4,3,2,1,0:T(8,128)(2,1)}, u32[]{:S(2)}) copy-start(bf16[1,4,1,2,256,256]{5,4,3,2,1,0:T(8,128)(2,1)} %kernel_ref.1) | copy-start | bytes 3145732
  1.9 13.2 %copy-start.1 = (bf16[1,4,1,2,256,256]{5,4,3,2,1,0:T(8,128)(2,1)S(1)}, bf16[1,4,1,2,256,256]{5,4,3,2,1,0:T(8,128)(2,1)}, u32[]{:S(2)}) copy-start(bf16[1,4,1,2,256,256]{5,4,3,2,1,0:T(8,128)(2,1)} %kernel_ref.1) | copy-start | bytes 3145732
  1.9 10.0 %collective-permute-start.2 = (bf16[384,128]{1,0:T(8,128)(2,1)S(1)}, bf16[384,128]{1,0:T(8,128)(2,1)S(1)}, u32[]{:S(2)}, u32[]{:S(2)}) collective-permute-start(bf16[384,128]{1,0:T(8,128)(2,1)S(1)} %pack.1), channel_id=1, source_target_pairs={{0,2},{1,3},{8,10},{9,11}} | collective-permute-start | bytes 294920 | tf_op jit(solution)/shard_map/ppermute | solution.py:318
  6.1 5.8 %collective-permute-start.1 = (bf16[384,128]{1,0:T(8,128)(2,1)S(1)}, bf16[384,128]{1,0:T(8,128)(2,1)S(1)}, u32[]{:S(2)}, u32[]{:S(2)}) collective-permute-start(bf16[384,128]{1,0:T(8,128)(2,1)S(1)} %pack.1), channel_id=1, source_target_pairs={{0,4},{1,5},{8,12},{9,13}} | collective-permute-start | bytes 294920 | tf_op jit(solution)/shard_map/ppermute | solution.py:318
  7.8 4.5 %collective-permute-start = (bf16[384,128]{1,0:T(8,128)(2,1)S(1)}, bf16[384,128]{1,0:T(8,128)(2,1)S(1)}, u32[]{:S(2)}, u32[]{:S(2)}) collective-permute-start(bf16[384,128]{1,0:T(8,128)(2,1)S(1)} %pack.1), channel_id=1, source_target_pairs={{0,6},{1,7},{8,14},{9,15}} | collective-permute-start | bytes 294920 | tf_op jit(solution)/shard_map/ppermute | solution.py:318
  10.6 13.1 %collective-permute-start.6 = (bf16[4,256,256]{2,1,0:T(8,128)(2,1)S(1)}, bf16[4,256,256]{2,1,0:T(8,128)(2,1)S(1)}, u32[]{:S(2)}, u32[]{:S(2)}) collective-permute-start(bf16[4,256,256]{2,1,0:T(8,128)(2,1)S(1)} %slice_bitcast_fusion), channel_id=1, source_target_pairs={{0,4},{1,5},{8,12},{9,13},{16,20},{17,21},{24,28},{25,29}} | collective-permute-start | bytes 1572872 | tf_op jit(solution)/shard_map/ppermute | solution.py:357
  12.3 3.5 %collective-permute-start.5 = (bf16[384,128]{1,0:T(8,128)(2,1)S(1)}, bf16[384,128]{1,0:T(8,128)(2,1)S(1)}, u32[]{:S(2)}, u32[]{:S(2)}) collective-permute-start(bf16[384,128]{1,0:T(8,128)(2,1)S(1)} %select_select_fusion), channel_id=1, source_target_pairs={{0,8},{8,0},{16,24},{24,16},{1,9},{9,1},{17,25},{25,17},{2,10},{10... | collective-permute-start | bytes 294920 | tf_op jit(solution)/shard_map/ppermute | solution.py:307
  13.6 4.8 %collective-permute-start.4 = (bf16[384,128]{1,0:T(8,128)(2,1)S(1)}, bf16[384,128]{1,0:T(8,128)(2,1)S(1)}, u32[]{:S(2)}, u32[]{:S(2)}) collective-permute-start(bf16[384,128]{1,0:T(8,128)(2,1)S(1)} %select_select_fusion), channel_id=1, source_target_pairs={{0,16},{8,24},{16,0},{24,8},{1,17},{9,25},{17,1},{25,9},{2,18},{10... | collective-permute-start | bytes 294920 | tf_op jit(solution)/shard_map/ppermute | solution.py:307
  13.6 4.8 %collective-permute-start.3 = (bf16[384,128]{1,0:T(8,128)(2,1)S(1)}, bf16[384,128]{1,0:T(8,128)(2,1)S(1)}, u32[]{:S(2)}, u32[]{:S(2)}) collective-permute-start(bf16[384,128]{1,0:T(8,128)(2,1)S(1)} %select_select_fusion), channel_id=1, source_target_pairs={{0,24},{8,16},{16,8},{24,0},{1,25},{9,17},{17,9},{25,1},{2,26},{10... | collective-permute-start | bytes 294920 | tf_op jit(solution)/shard_map/ppermute | solution.py:307
  18.5 11.5 %collective-permute-start.8 = (bf16[2,256,256]{2,1,0:T(8,128)(2,1)S(1)}, bf16[2,256,256]{2,1,0:T(8,128)(2,1)S(1)}, u32[]{:S(2)}, u32[]{:S(2)}) collective-permute-start(bf16[2,256,256]{2,1,0:T(8,128)(2,1)S(1)} %slice_bitcast_fusion.1), channel_id=1, source_target_pairs={{0,16},{8,24},{16,0},{24,8},{1,17},{9,25},{17,1},{25,9},{2,18},{10... | collective-permute-start | bytes 786440 | tf_op jit(solution)/shard_map/ppermute | solution.py:307
  23.6 2.0 %collective-permute-start.9 = (bf16[2,384,128]{2,1,0:T(8,128)(2,1)S(1)}, bf16[2,384,128]{2,1,0:T(8,128)(2,1)S(1)}, u32[]{:S(2)}, u32[]{:S(2)}) collective-permute-start(bf16[2,384,128]{2,1,0:T(8,128)(2,1)S(1)} %pad_maximum_fusion), channel_id=1, source_target_pairs={{0,1},{1,0},{2,3},{3,2},{4,5},{5,4},{6,7},{7,6},{8,9},{9,8},{10,11... | collective-permute-start | bytes 589832 | tf_op jit(solution)/shard_map/ppermute | solution.py:307
  24.7 16.9 %collective-permute-start.7 = (bf16[4,256,256]{2,1,0:T(8,128)(2,1)S(1)}, bf16[4,256,256]{2,1,0:T(8,128)(2,1)S(1)}, u32[]{:S(2)}, u32[]{:S(2)}) collective-permute-start(bf16[4,256,256]{2,1,0:T(8,128)(2,1)S(1)} %broadcast_select_fusion), channel_id=1, source_target_pairs={{0,2},{1,3},{2,0},{3,1},{4,6},{5,7},{6,4},{7,5},{8,10},{9,11},{10,... | collective-permute-start | bytes 1572872 | tf_op jit(solution)/shard_map/ppermute | solution.py:307
  30.1 11.6 %collective-permute-start.10 = (bf16[2,256,256]{2,1,0:T(8,128)(2,1)S(1)}, bf16[2,256,256]{2,1,0:T(8,128)(2,1)S(1)}, u32[]{:S(2)}, u32[]{:S(2)}) collective-permute-start(bf16[2,256,256]{2,1,0:T(8,128)(2,1)S(1)} %broadcast_select_fusion.4.above_ref), channel_id=1, source_target_pairs={{0,8},{8,0},{16,24},{24,16},{1,9},{9,1},{17,25},{25,17},{2,10},{10... | collective-permute-start | bytes 786440 | tf_op jit(solution)/shard_map/ppermute | solution.py:307
  41.7 7.1 %collective-permute-start.11 = (bf16[4,256,256]{2,1,0:T(8,128)(2,1)S(1)}, bf16[4,256,256]{2,1,0:T(8,128)(2,1)S(1)}, u32[]{:S(2)}, u32[]{:S(2)}) collective-permute-start(bf16[4,256,256]{2,1,0:T(8,128)(2,1)S(1)} %broadcast_select_fusion.1), channel_id=1, source_target_pairs={{0,1},{1,0},{2,3},{3,2},{4,5},{5,4},{6,7},{7,6},{8,9},{9,8},{10,11... | collective-permute-start | bytes 1572872 | tf_op jit(solution)/shard_map/ppermute | solution.py:307

commit v6 on v5

--- a/solution.py
+++ b/solution.py
@@ -176,15 +176,19 @@
         above_0_ref[...] = other_ref[...]
         above_1_ref[...] = above_ref[...]
 
+    parts = (pl.ds(0, half), pl.ds(half, half))
     for m in range(above_ref.shape[0]):
-        def mirror(m=m):
-            mirror_ref[m] = product(pieces_0_ref, above_0_ref[m]).astype(jnp.bfloat16)
-
-        def later(m=m):
-            change = mul(panel_ref[...], mirror_ref[m])
-            later_ref[m] = (above_1_ref[m].astype(jnp.float32) - change).astype(jnp.bfloat16)
-
-        tasks += [mirror, later]
+        for part in parts:
+            def mirror(m=m, part=part):
+                terms = [mul(pieces_0_ref[p, part], above_0_ref[m]) for p in (2, 1, 0)]
+                mirror_ref[m, part] = sum(terms).astype(jnp.bfloat16)
+            tasks.append(mirror)
+    for m in range(above_ref.shape[0]):
+        for part in parts:
+            def later(m=m, part=part):
+                change = mul(panel_ref[part], mirror_ref[m])
+                later_ref[m, part] = (above_1_ref[m, part].astype(jnp.float32) - change).astype(jnp.bfloat16)
+            tasks.append(later)
     factor_rest(
         upper_ref[...], tile_inverse_ref[...], rest_ref[:half], rest_ref[half:], lower_ref, pieces_1_ref, tasks)
 
@@ -381,12 +385,11 @@
     half = width // 2
     ids = jnp.stack([my_row, my_col, lax.axis_size("row"), lax.axis_size("col")]).astype(jnp.int32)
     quarters = pack(kernel)
-    rows, _ = lax.optimization_barrier((blocks[:, 0], quarters))
+    rows, above, _ = lax.optimization_barrier((blocks[:, 0], blocks[0], quarters))
     rows, rows_got = first_stride(rows)
+    above, above_got = first_reach(above)
     along = diagonal_along(quarters, my_col)
     pair = diagonal_down(along, my_row)
-    pair, above = lax.optimization_barrier((pair, blocks[0]))
-    above, above_got = first_reach(above)
     pair, rows, rows_got = lax.optimization_barrier((pair, rows, rows_got))
     block_00, block_01, block_10, block_11 = both_cores(pair, my_col)
     rows = other_strides(rows, rows_got, my_col)

time: 52.7 us -> 52.7 us (level)
  waiting for transfers between devices: 7.93 us -> 9.81 us
  starting transfers between devices: 16.6 us -> 14.8 us
    ppermute x1, waiting for transfers between devices: 3.29 us -> 5.15 us  [first_stride(): return (block, lax.ppermute(block, 'col', pairs))]
    ppermute x8, starting transfers between devices: 7.77 us -> 5.94 us  [swap(): return lax.ppermute(block, axis, [(d, d ^ distance) for d in range(count)])]
where the time goes in v6:
time: 52.7 us; the launch traced here: 52.4 us
  Pallas kernels  24 us (46%)
  starting transfers between devices  14.8 us (28%)
  waiting for transfers between devices  9.81 us (19%)
  local copies, waits for them, and re-layouts  2.35 us (4%)
  between operations  1.03 us (2%)
    pallas_call x4, Pallas kernels, call_factor(): pl.pallas_call(kernel, in_specs=in_specs, out_shape=shapes, scratch_shape...  20.5 us
    ppermute x3, starting transfers between devices, diagonal_along(): got = lax.ppermute(quarters, ('row', 'col'), pairs)  7.53 us
    ppermute x8, starting transfers between devices, swap(): return lax.ppermute(block, axis, [(d, d ^ distance) for d in range(count)])  5.94 us
    ppermute x1, waiting for transfers between devices, first_stride(): return (block, lax.ppermute(block, 'col', pairs))  5.15 us
    ppermute x8, waiting for transfers between devices, swap(): return lax.ppermute(block, axis, [(d, d ^ distance) for d in range(count)])  4.29 us
    pallas_call x1, Pallas kernels, update(): pl.pallas_call(update_kernel, in_specs=[pl.BlockSpec(memory_space=pltpu.S...  3.47 us
    ppermute x1, starting transfers between devices, first_stride(): return (block, lax.ppermute(block, 'col', pairs))  1.32 us
    unnamed x4, local copies, waits for them, and re-layouts  1.22 us
  transfers between devices with their start and end apart: 12, of which 5 were waited for; matrix products, arithmetic and copies ran while one was open for 3% of the time, Pallas kernels for 39%

profile of v6, /device:TPU:1, one launch (start us, length us, event | category | flops | bytes accessed | tf_op | source)
XLA Modules:
  0.0 52.4 jit_solution(6588864774468294310)
XLA Ops:
  0.6 0.0 copy-start
  0.6 1.2 %copy-done = bf16[1,4,1,2,256,256]{5,4,3,2,1,0:T(8,128)(2,1)S(1)} copy-done((bf16[1,4,1,2,256,256]{5,4,3,2,1,0:T(8,128)(2,1)S(1)}, bf16[1,4,1,2,256,256]{5,4,3,2,1,0:T(8,128)(2,1)}, u32[]{:S(2)}) %copy-start) | copy-done | bytes 1048600
  1.9 0.1 pack.1
  1.9 4.2 %collective-permute-start.2 = (bf16[384,128]{1,0:T(8,128)(2,1)S(1)}, bf16[384,128]{1,0:T(8,128)(2,1)S(1)}, u32[]{:S(2)}, u32[]{:S(2)}) collective-permute-start(bf16[384,128]{1,0:T(8,128)(2,1)S(1)} %pack.1), channel_id=1, source_target_pairs={{0,2},{1,3},{8,10},{9,11}} | collective-permute-start | bytes 294920 | tf_op jit(solution)/shard_map/ppermute | solution.py:322
  6.1 1.7 %collective-permute-start.1 = (bf16[384,128]{1,0:T(8,128)(2,1)S(1)}, bf16[384,128]{1,0:T(8,128)(2,1)S(1)}, u32[]{:S(2)}, u32[]{:S(2)}) collective-permute-start(bf16[384,128]{1,0:T(8,128)(2,1)S(1)} %pack.1), channel_id=1, source_target_pairs={{0,4},{1,5},{8,12},{9,13}} | collective-permute-start | bytes 294920 | tf_op jit(solution)/shard_map/ppermute | solution.py:322
  7.8 1.7 %collective-permute-start = (bf16[384,128]{1,0:T(8,128)(2,1)S(1)}, bf16[384,128]{1,0:T(8,128)(2,1)S(1)}, u32[]{:S(2)}, u32[]{:S(2)}) collective-permute-start(bf16[384,128]{1,0:T(8,128)(2,1)S(1)} %pack.1), channel_id=1, source_target_pairs={{0,6},{1,7},{8,14},{9,15}} | collective-permute-start | bytes 294920 | tf_op jit(solution)/shard_map/ppermute | solution.py:322
  9.5 1.1 %slice_bitcast_fusion = bf16[4,256,256]{2,1,0:T(8,128)(2,1)S(1)} fusion(bf16[4,2,256,256]{3,2,1,0:T(8,128)(2,1)} %bitcast.29), kind=kLoop, calls=%fused_computation | loop fusion | bytes 1048576 | tf_op jit(solution)/shard_map/squeeze | solution.py:388
  10.6 1.3 %collective-permute-start.6 = (bf16[4,256,256]{2,1,0:T(8,128)(2,1)S(1)}, bf16[4,256,256]{2,1,0:T(8,128)(2,1)S(1)}, u32[]{:S(2)}, u32[]{:S(2)}) collective-permute-start(bf16[4,256,256]{2,1,0:T(8,128)(2,1)S(1)} %slice_bitcast_fusion), channel_id=1, source_target_pairs={{0,4},{1,5},{8,12},{9,13},{16,20},{17,21},{24,28},{25,29}} | collective-permute-start | bytes 1572872 | tf_op jit(solution)/shard_map/ppermute | solution.py:361
  11.9 0.0 collective-permute-done.2
  12.0 0.0 collective-permute-done.1
  12.0 0.4 collective-permute-done
  12.3 1.3 %collective-permute-start.5 = (bf16[384,128]{1,0:T(8,128)(2,1)S(1)}, bf16[384,128]{1,0:T(8,128)(2,1)S(1)}, u32[]{:S(2)}, u32[]{:S(2)}) collective-permute-start(bf16[384,128]{1,0:T(8,128)(2,1)S(1)} %select_select_fusion), channel_id=1, source_target_pairs={{0,8},{8,0},{16,24},{24,16},{1,9},{9,1},{17,25},{25,17},{2,10},{10... | collective-permute-start | bytes 294920 | tf_op jit(solution)/shard_map/ppermute | solution.py:311
  13.6 0.0 collective-permute-start.4
  13.6 1.4 %collective-permute-start.3 = (bf16[384,128]{1,0:T(8,128)(2,1)S(1)}, bf16[384,128]{1,0:T(8,128)(2,1)S(1)}, u32[]{:S(2)}, u32[]{:S(2)}) collective-permute-start(bf16[384,128]{1,0:T(8,128)(2,1)S(1)} %select_select_fusion), channel_id=1, source_target_pairs={{0,24},{8,16},{16,8},{24,0},{1,25},{9,17},{17,9},{25,1},{2,26},{10... | collective-permute-start | bytes 294920 | tf_op jit(solution)/shard_map/ppermute | solution.py:311
  15.1 0.0 collective-permute-start.8
  15.1 0.8 %collective-permute-done.5 = bf16[384,128]{1,0:T(8,128)(2,1)S(1)} collective-permute-done((bf16[384,128]{1,0:T(8,128)(2,1)S(1)}, bf16[384,128]{1,0:T(8,128)(2,1)S(1)}, u32[]{:S(2)}, u32[]{:S(2)}) %collective-permute-start.5) | collective-permute-done | bytes 98336 | tf_op jit(solution)/shard_map/ppermute | solution.py:311
  15.9 2.6 %collective-permute-done.4 = bf16[384,128]{1,0:T(8,128)(2,1)S(1)} collective-permute-done((bf16[384,128]{1,0:T(8,128)(2,1)S(1)}, bf16[384,128]{1,0:T(8,128)(2,1)S(1)}, u32[]{:S(2)}, u32[]{:S(2)}) %collective-permute-start.4) | collective-permute-done | bytes 98336 | tf_op jit(solution)/shard_map/ppermute | solution.py:311
  18.5 5.2 %collective-permute-done.6 = bf16[4,256,256]{2,1,0:T(8,128)(2,1)S(1)} collective-permute-done((bf16[4,256,256]{2,1,0:T(8,128)(2,1)S(1)}, bf16[4,256,256]{2,1,0:T(8,128)(2,1)S(1)}, u32[]{:S(2)}, u32[]{:S(2)}) %collective-permute-start.6) | collective-permute-done | bytes 524320 | tf_op jit(solution)/shard_map/ppermute | solution.py:361
  23.7 0.9 %collective-permute-start.9 = (bf16[2,384,128]{2,1,0:T(8,128)(2,1)S(1)}, bf16[2,384,128]{2,1,0:T(8,128)(2,1)S(1)}, u32[]{:S(2)}, u32[]{:S(2)}) collective-permute-start(bf16[2,384,128]{2,1,0:T(8,128)(2,1)S(1)} %pad_maximum_fusion), channel_id=1, source_target_pairs={{0,1},{1,0},{2,3},{3,2},{4,5},{5,4},{6,7},{7,6},{8,9},{9,8},{10,11... | collective-permute-start | bytes 589832 | tf_op jit(solution)/shard_map/ppermute | solution.py:311
  24.6 0.1 broadcast_select_fusion
  24.7 0.1 collective-permute-start.7
  24.7 0.9 %collective-permute-done.9 = bf16[2,384,128]{2,1,0:T(8,128)(2,1)S(1)} collective-permute-done((bf16[2,384,128]{2,1,0:T(8,128)(2,1)S(1)}, bf16[2,384,128]{2,1,0:T(8,128)(2,1)S(1)}, u32[]{:S(2)}, u32[]{:S(2)}) %collective-permute-start.9) | collective-permute-done | bytes 196640 | tf_op jit(solution)/shard_map/ppermute | solution.py:311
  25.7 4.3 %factor_start.1 = (f32[128,128]{1,0:T(8,128)S(1)}, f32[128,128]{1,0:T(8,128)S(1)}) custom-call(bf16[128,128]{1,0:T(8,128)(2,1)S(1)} %get-tuple-element.71.quarter_ref), custom_call_target="tpu_custom_call" | custom-call | flops 1000000 | bytes 10000 | tf_op jit(solution)/shard_map/factor_start/pallas_call | solution.py:253
  30.1 1.3 %collective-permute-start.10 = (bf16[2,256,256]{2,1,0:T(8,128)(2,1)S(1)}, bf16[2,256,256]{2,1,0:T(8,128)(2,1)S(1)}, u32[]{:S(2)}, u32[]{:S(2)}) collective-permute-start(bf16[2,256,256]{2,1,0:T(8,128)(2,1)S(1)} %broadcast_select_fusion.4.above_ref), channel_id=1, source_target_pairs={{0,8},{8,0},{16,24},{24,16},{1,9},{9,1},{17,25},{25,17},{2,10},{10... | collective-permute-start | bytes 786440 | tf_op jit(solution)/shard_map/ppermute | solution.py:311
  31.4 5.4 %factor_first.1 = (f32[256,256]{1,0:T(8,128)S(1)}, bf16[3,256,256]{2,1,0:T(8,128)(2,1)S(1)}) custom-call(bf16[256,128]{1,0:T(8,128)(2,1)S(1)} %get-tuple-element.66.rest_ref, f32[128,128]{1,0:T(8,128)S(1)} %get-tuple-element.38.upper_ref, f32[128,128]{1,0:T(8,128)S(1)} %get-tuple-element.39.tile_inverse_ref), custom_call_target="tpu_custom_call" | custom-call | flops 1000000 | bytes 10000 | tf_op jit(solution)/shard_map/factor_first/pallas_call | solution.py:253
  36.8 4.8 %factor_second_start.1 = (bf16[256,256]{1,0:T(8,128)(2,1)S(1)}, bf16[256,128]{1,0:T(8,128)(2,1)S(1)}, f32[128,128]{1,0:T(8,128)S(1)}, f32[128,128]{1,0:T(8,128)S(1)}) custom-call(bf16[128,128]{1,0:T(8,128)(2,1)S(1)} %get-tuple-element.70.top_10_ref, bf16[256,128]{1,0:T(8,128)(2,1)S(1)} %get-tuple-element.67.rest_10_ref, ...), custom_call_target="tpu_custom_call" | custom-call | flops 1000000 | bytes 10000 | tf_op jit(solution)/shard_map/factor_second_start/pallas_call | solution.py:253
  41.6 0.1 broadcast_select_fusion.1
  41.7 0.9 %collective-permute-start.11 = (bf16[4,256,256]{2,1,0:T(8,128)(2,1)S(1)}, bf16[4,256,256]{2,1,0:T(8,128)(2,1)S(1)}, u32[]{:S(2)}, u32[]{:S(2)}) collective-permute-start(bf16[4,256,256]{2,1,0:T(8,128)(2,1)S(1)} %broadcast_select_fusion.1), channel_id=1, source_target_pairs={{0,1},{1,0},{2,3},{3,2},{4,5},{5,4},{6,7},{7,6},{8,9},{9,8},{10,11... | collective-permute-start | bytes 1572872 | tf_op jit(solution)/shard_map/ppermute | solution.py:311
  42.6 0.1 pad_add_fusion.ids_ref
  42.7 6.0 %factor_second.1 = (f32[256,256]{1,0:T(8,128)S(1)}, bf16[3,256,256]{2,1,0:T(8,128)(2,1)S(1)}, bf16[2,256,256]{2,1,0:T(8,128)(2,1)S(1)}, bf16[2,256,256]{2,1,0:T(8,128)(2,1)S(1)}) custom-call(s32[4]{0:T(128)S(1)} %pad_add_fusion.ids_ref, bf16[256,128]{1,0:T(8,128)(2,1)S(1)} %get-tuple-element.43.rest_ref, f32[128,128]{1,0:T(8,128)S(1)} %get-tuple-element.44.upper_ref, ...), custom_call_target="tpu_custom_call" | custom-call | flops 1000000 | bytes 10000 | tf_op jit(solution)/shard_map/factor_second/pallas_call | solution.py:253
  48.7 0.1 broadcast_select_fusion.2
  48.8 3.5 %solve_and_update.1 = (f32[4,2,256,256]{3,2,1,0:T(8,128)}, bf16[4,2,256,256]{3,2,1,0:T(8,128)(2,1)}) custom-call(s32[4]{0:T(128)S(1)} %pad_add_fusion.ids_ref, bf16[4,256,256]{2,1,0:T(8,128)(2,1)S(1)} %get-tuple-element.61.column_0_ref, bf16[4,256,256]{2,1,0:T(8,128)(2,1)S(1)} %get-tuple-element.60.column_1_ref, bf16[4,2,256,256]{3,2,1,0:T(8,128)(2,1)S(1)} %bitcast.30, ...), custom_call_target="tpu_custom_call" | custom-call | flops 2000000000 | bytes 6000000 | tf_op jit(solution)/shard_map/solve_and_update/pallas_call | solution.py:267
  (16 shorter events, 0.2 us)
Async XLA Ops:
  0.6 1.2 %copy-start = (bf16[1,4,1,2,256,256]{5,4,3,2,1,0:T(8,128)(2,1)S(1)}, bf16[1,4,1,2,256,256]{5,4,3,2,1,0:T(8,128)(2,1)}, u32[]{:S(2)}) copy-start(bf16[1,4,1,2,256,256]{5,4,3,2,1,0:T(8,128)(2,1)} %kernel_ref.1) | copy-start | bytes 3145732
  1.9 8.7 %copy-start.1 = (bf16[1,4,1,2,256,256]{5,4,3,2,1,0:T(8,128)(2,1)S(1)}, bf16[1,4,1,2,256,256]{5,4,3,2,1,0:T(8,128)(2,1)}, u32[]{:S(2)}) copy-start(bf16[1,4,1,2,256,256]{5,4,3,2,1,0:T(8,128)(2,1)} %kernel_ref.1) | copy-start | bytes 3145732
  1.9 10.0 %collective-permute-start.2 = (bf16[384,128]{1,0:T(8,128)(2,1)S(1)}, bf16[384,128]{1,0:T(8,128)(2,1)S(1)}, u32[]{:S(2)}, u32[]{:S(2)}) collective-permute-start(bf16[384,128]{1,0:T(8,128)(2,1)S(1)} %pack.1), channel_id=1, source_target_pairs={{0,2},{1,3},{8,10},{9,11}} | collective-permute-start | bytes 294920 | tf_op jit(solution)/shard_map/ppermute | solution.py:322
  6.1 5.9 %collective-permute-start.1 = (bf16[384,128]{1,0:T(8,128)(2,1)S(1)}, bf16[384,128]{1,0:T(8,128)(2,1)S(1)}, u32[]{:S(2)}, u32[]{:S(2)}) collective-permute-start(bf16[384,128]{1,0:T(8,128)(2,1)S(1)} %pack.1), channel_id=1, source_target_pairs={{0,4},{1,5},{8,12},{9,13}} | collective-permute-start | bytes 294920 | tf_op jit(solution)/shard_map/ppermute | solution.py:322
  7.8 4.5 %collective-permute-start = (bf16[384,128]{1,0:T(8,128)(2,1)S(1)}, bf16[384,128]{1,0:T(8,128)(2,1)S(1)}, u32[]{:S(2)}, u32[]{:S(2)}) collective-permute-start(bf16[384,128]{1,0:T(8,128)(2,1)S(1)} %pack.1), channel_id=1, source_target_pairs={{0,6},{1,7},{8,14},{9,15}} | collective-permute-start | bytes 294920 | tf_op jit(solution)/shard_map/ppermute | solution.py:322
  10.6 13.1 %collective-permute-start.6 = (bf16[4,256,256]{2,1,0:T(8,128)(2,1)S(1)}, bf16[4,256,256]{2,1,0:T(8,128)(2,1)S(1)}, u32[]{:S(2)}, u32[]{:S(2)}) collective-permute-start(bf16[4,256,256]{2,1,0:T(8,128)(2,1)S(1)} %slice_bitcast_fusion), channel_id=1, source_target_pairs={{0,4},{1,5},{8,12},{9,13},{16,20},{17,21},{24,28},{25,29}} | collective-permute-start | bytes 1572872 | tf_op jit(solution)/shard_map/ppermute | solution.py:361
  12.3 3.5 %collective-permute-start.5 = (bf16[384,128]{1,0:T(8,128)(2,1)S(1)}, bf16[384,128]{1,0:T(8,128)(2,1)S(1)}, u32[]{:S(2)}, u32[]{:S(2)}) collective-permute-start(bf16[384,128]{1,0:T(8,128)(2,1)S(1)} %select_select_fusion), channel_id=1, source_target_pairs={{0,8},{8,0},{16,24},{24,16},{1,9},{9,1},{17,25},{25,17},{2,10},{10... | collective-permute-start | bytes 294920 | tf_op jit(solution)/shard_map/ppermute | solution.py:311
  13.6 4.8 %collective-permute-start.4 = (bf16[384,128]{1,0:T(8,128)(2,1)S(1)}, bf16[384,128]{1,0:T(8,128)(2,1)S(1)}, u32[]{:S(2)}, u32[]{:S(2)}) collective-permute-start(bf16[384,128]{1,0:T(8,128)(2,1)S(1)} %select_select_fusion), channel_id=1, source_target_pairs={{0,16},{8,24},{16,0},{24,8},{1,17},{9,25},{17,1},{25,9},{2,18},{10... | collective-permute-start | bytes 294920 | tf_op jit(solution)/shard_map/ppermute | solution.py:311
  13.6 4.8 %collective-permute-start.3 = (bf16[384,128]{1,0:T(8,128)(2,1)S(1)}, bf16[384,128]{1,0:T(8,128)(2,1)S(1)}, u32[]{:S(2)}, u32[]{:S(2)}) collective-permute-start(bf16[384,128]{1,0:T(8,128)(2,1)S(1)} %select_select_fusion), channel_id=1, source_target_pairs={{0,24},{8,16},{16,8},{24,0},{1,25},{9,17},{17,9},{25,1},{2,26},{10... | collective-permute-start | bytes 294920 | tf_op jit(solution)/shard_map/ppermute | solution.py:311
  15.1 15.0 %collective-permute-start.8 = (bf16[2,256,256]{2,1,0:T(8,128)(2,1)S(1)}, bf16[2,256,256]{2,1,0:T(8,128)(2,1)S(1)}, u32[]{:S(2)}, u32[]{:S(2)}) collective-permute-start(bf16[2,256,256]{2,1,0:T(8,128)(2,1)S(1)} %slice_bitcast_fusion.1), channel_id=1, source_target_pairs={{0,16},{8,24},{16,0},{24,8},{1,17},{9,25},{17,1},{25,9},{2,18},{10... | collective-permute-start | bytes 786440 | tf_op jit(solution)/shard_map/ppermute | solution.py:311
  23.7 2.0 %collective-permute-start.9 = (bf16[2,384,128]{2,1,0:T(8,128)(2,1)S(1)}, bf16[2,384,128]{2,1,0:T(8,128)(2,1)S(1)}, u32[]{:S(2)}, u32[]{:S(2)}) collective-permute-start(bf16[2,384,128]{2,1,0:T(8,128)(2,1)S(1)} %pad_maximum_fusion), channel_id=1, source_target_pairs={{0,1},{1,0},{2,3},{3,2},{4,5},{5,4},{6,7},{7,6},{8,9},{9,8},{10,11... | collective-permute-start | bytes 589832 | tf_op jit(solution)/shard_map/ppermute | solution.py:311
  24.7 16.9 %collective-permute-start.7 = (bf16[4,256,256]{2,1,0:T(8,128)(2,1)S(1)}, bf16[4,256,256]{2,1,0:T(8,128)(2,1)S(1)}, u32[]{:S(2)}, u32[]{:S(2)}) collective-permute-start(bf16[4,256,256]{2,1,0:T(8,128)(2,1)S(1)} %broadcast_select_fusion), channel_id=1, source_target_pairs={{0,2},{1,3},{2,0},{3,1},{4,6},{5,7},{6,4},{7,5},{8,10},{9,11},{10,... | collective-permute-start | bytes 1572872 | tf_op jit(solution)/shard_map/ppermute | solution.py:311
  30.1 11.6 %collective-permute-start.10 = (bf16[2,256,256]{2,1,0:T(8,128)(2,1)S(1)}, bf16[2,256,256]{2,1,0:T(8,128)(2,1)S(1)}, u32[]{:S(2)}, u32[]{:S(2)}) collective-permute-start(bf16[2,256,256]{2,1,0:T(8,128)(2,1)S(1)} %broadcast_select_fusion.4.above_ref), channel_id=1, source_target_pairs={{0,8},{8,0},{16,24},{24,16},{1,9},{9,1},{17,25},{25,17},{2,10},{10... | collective-permute-start | bytes 786440 | tf_op jit(solution)/shard_map/ppermute | solution.py:311
  41.7 7.0 %collective-permute-start.11 = (bf16[4,256,256]{2,1,0:T(8,128)(2,1)S(1)}, bf16[4,256,256]{2,1,0:T(8,128)(2,1)S(1)}, u32[]{:S(2)}, u32[]{:S(2)}) collective-permute-start(bf16[4,256,256]{2,1,0:T(8,128)(2,1)S(1)} %broadcast_select_fusion.1), channel_id=1, source_target_pairs={{0,1},{1,0},{2,3},{3,2},{4,5},{5,4},{6,7},{7,6},{8,9},{9,8},{10,11... | collective-permute-start | bytes 1572872 | tf_op jit(solution)/shard_map/ppermute | solution.py:311

commit v7 on v6

--- a/solution.py
+++ b/solution.py
@@ -29,8 +29,8 @@
         v = [spread(right[s][k:k + 1, :]) for k in range(8)]
         d = [[lane(y[i], 8 * s + k) if k >= i else None for k in range(8)] for i in range(8)]
         last = s + 1 == groups
-        near = None if last else [lane(left[s + 1], 8 * s + k) for k in range(8)]
-        e = None if last else list(near)
+        columns = [[lane(left[g], 8 * s + k) for k in range(8)] for g in range(s + 1, groups)]
+        e = list(columns[0]) if not last else None
         ratio = [[None] * 8 for _ in range(8)]
         inv = []
         for k in range(8):
@@ -65,7 +65,7 @@
                 x[k] = x[k] - ratio[j][k] * x[j]
                 w[k] = w[k] - ratio[j][k] * w[j]
         for g in range(s + 1, groups):
-            f = near if g == s + 1 else [lane(left[g], 8 * s + k) for k in range(8)]
+            f = columns[g - s - 1]
             for k in reversed(range(8)):
                 if g > s + 1:
                     left[g] = left[g] - f[k] * x[k]

time: 52.7 us -> 52.7 us (level)
  no operation moved by 1% of the time
where the time goes in v7:
time: 52.7 us; the launch traced here: 52.4 us
  Pallas kernels  24.1 us (46%)
  starting transfers between devices  14.8 us (28%)
  waiting for transfers between devices  9.81 us (19%)
  local copies, waits for them, and re-layouts  2.35 us (4%)
  between operations  1.03 us (2%)
    pallas_call x4, Pallas kernels, call_factor(): pl.pallas_call(kernel, in_specs=in_specs, out_shape=shapes, scratch_shape...  20.5 us
    ppermute x3, starting transfers between devices, diagonal_along(): got = lax.ppermute(quarters, ('row', 'col'), pairs)  7.53 us
    ppermute x8, starting transfers between devices, swap(): return lax.ppermute(block, axis, [(d, d ^ distance) for d in range(count)])  5.94 us
    ppermute x1, waiting for transfers between devices, first_stride(): return (block, lax.ppermute(block, 'col', pairs))  5.15 us
    ppermute x8, waiting for transfers between devices, swap(): return lax.ppermute(block, axis, [(d, d ^ distance) for d in range(count)])  4.29 us
    pallas_call x1, Pallas kernels, update(): pl.pallas_call(update_kernel, in_specs=[pl.BlockSpec(memory_space=pltpu.S...  3.48 us
    ppermute x1, starting transfers between devices, first_stride(): return (block, lax.ppermute(block, 'col', pairs))  1.32 us
    unnamed x4, local copies, waits for them, and re-layouts  1.22 us
  transfers between devices with their start and end apart: 12, of which 5 were waited for; matrix products, arithmetic and copies ran while one was open for 3% of the time, Pallas kernels for 39%

profile of v7, /device:TPU:1, one launch (start us, length us, event | category | flops | bytes accessed | tf_op | source)
XLA Modules:
  0.0 52.4 jit_solution(7494368093333441422)
XLA Ops:
  0.6 0.0 copy-start
  0.6 1.2 %copy-done = bf16[1,4,1,2,256,256]{5,4,3,2,1,0:T(8,128)(2,1)S(1)} copy-done((bf16[1,4,1,2,256,256]{5,4,3,2,1,0:T(8,128)(2,1)S(1)}, bf16[1,4,1,2,256,256]{5,4,3,2,1,0:T(8,128)(2,1)}, u32[]{:S(2)}) %copy-start) | copy-done | bytes 1048600
  1.9 0.1 pack.1
  1.9 4.2 %collective-permute-start.2 = (bf16[384,128]{1,0:T(8,128)(2,1)S(1)}, bf16[384,128]{1,0:T(8,128)(2,1)S(1)}, u32[]{:S(2)}, u32[]{:S(2)}) collective-permute-start(bf16[384,128]{1,0:T(8,128)(2,1)S(1)} %pack.1), channel_id=1, source_target_pairs={{0,2},{1,3},{8,10},{9,11}} | collective-permute-start | bytes 294920 | tf_op jit(solution)/shard_map/ppermute | solution.py:322
  6.1 1.7 %collective-permute-start.1 = (bf16[384,128]{1,0:T(8,128)(2,1)S(1)}, bf16[384,128]{1,0:T(8,128)(2,1)S(1)}, u32[]{:S(2)}, u32[]{:S(2)}) collective-permute-start(bf16[384,128]{1,0:T(8,128)(2,1)S(1)} %pack.1), channel_id=1, source_target_pairs={{0,4},{1,5},{8,12},{9,13}} | collective-permute-start | bytes 294920 | tf_op jit(solution)/shard_map/ppermute | solution.py:322
  7.8 1.7 %collective-permute-start = (bf16[384,128]{1,0:T(8,128)(2,1)S(1)}, bf16[384,128]{1,0:T(8,128)(2,1)S(1)}, u32[]{:S(2)}, u32[]{:S(2)}) collective-permute-start(bf16[384,128]{1,0:T(8,128)(2,1)S(1)} %pack.1), channel_id=1, source_target_pairs={{0,6},{1,7},{8,14},{9,15}} | collective-permute-start | bytes 294920 | tf_op jit(solution)/shard_map/ppermute | solution.py:322
  9.5 1.1 %slice_bitcast_fusion = bf16[4,256,256]{2,1,0:T(8,128)(2,1)S(1)} fusion(bf16[4,2,256,256]{3,2,1,0:T(8,128)(2,1)} %bitcast.29), kind=kLoop, calls=%fused_computation | loop fusion | bytes 1048576 | tf_op jit(solution)/shard_map/squeeze | solution.py:388
  10.6 1.3 %collective-permute-start.6 = (bf16[4,256,256]{2,1,0:T(8,128)(2,1)S(1)}, bf16[4,256,256]{2,1,0:T(8,128)(2,1)S(1)}, u32[]{:S(2)}, u32[]{:S(2)}) collective-permute-start(bf16[4,256,256]{2,1,0:T(8,128)(2,1)S(1)} %slice_bitcast_fusion), channel_id=1, source_target_pairs={{0,4},{1,5},{8,12},{9,13},{16,20},{17,21},{24,28},{25,29}} | collective-permute-start | bytes 1572872 | tf_op jit(solution)/shard_map/ppermute | solution.py:361
  11.9 0.0 collective-permute-done.2
  12.0 0.0 collective-permute-done.1
  12.0 0.4 collective-permute-done
  12.3 1.3 %collective-permute-start.5 = (bf16[384,128]{1,0:T(8,128)(2,1)S(1)}, bf16[384,128]{1,0:T(8,128)(2,1)S(1)}, u32[]{:S(2)}, u32[]{:S(2)}) collective-permute-start(bf16[384,128]{1,0:T(8,128)(2,1)S(1)} %select_select_fusion), channel_id=1, source_target_pairs={{0,8},{8,0},{16,24},{24,16},{1,9},{9,1},{17,25},{25,17},{2,10},{10... | collective-permute-start | bytes 294920 | tf_op jit(solution)/shard_map/ppermute | solution.py:311
  13.6 0.0 collective-permute-start.4
  13.6 1.4 %collective-permute-start.3 = (bf16[384,128]{1,0:T(8,128)(2,1)S(1)}, bf16[384,128]{1,0:T(8,128)(2,1)S(1)}, u32[]{:S(2)}, u32[]{:S(2)}) collective-permute-start(bf16[384,128]{1,0:T(8,128)(2,1)S(1)} %select_select_fusion), channel_id=1, source_target_pairs={{0,24},{8,16},{16,8},{24,0},{1,25},{9,17},{17,9},{25,1},{2,26},{10... | collective-permute-start | bytes 294920 | tf_op jit(solution)/shard_map/ppermute | solution.py:311
  15.1 0.0 collective-permute-start.8
  15.1 0.8 %collective-permute-done.5 = bf16[384,128]{1,0:T(8,128)(2,1)S(1)} collective-permute-done((bf16[384,128]{1,0:T(8,128)(2,1)S(1)}, bf16[384,128]{1,0:T(8,128)(2,1)S(1)}, u32[]{:S(2)}, u32[]{:S(2)}) %collective-permute-start.5) | collective-permute-done | bytes 98336 | tf_op jit(solution)/shard_map/ppermute | solution.py:311
  15.9 2.6 %collective-permute-done.4 = bf16[384,128]{1,0:T(8,128)(2,1)S(1)} collective-permute-done((bf16[384,128]{1,0:T(8,128)(2,1)S(1)}, bf16[384,128]{1,0:T(8,128)(2,1)S(1)}, u32[]{:S(2)}, u32[]{:S(2)}) %collective-permute-start.4) | collective-permute-done | bytes 98336 | tf_op jit(solution)/shard_map/ppermute | solution.py:311
  18.5 5.2 %collective-permute-done.6 = bf16[4,256,256]{2,1,0:T(8,128)(2,1)S(1)} collective-permute-done((bf16[4,256,256]{2,1,0:T(8,128)(2,1)S(1)}, bf16[4,256,256]{2,1,0:T(8,128)(2,1)S(1)}, u32[]{:S(2)}, u32[]{:S(2)}) %collective-permute-start.6) | collective-permute-done | bytes 524320 | tf_op jit(solution)/shard_map/ppermute | solution.py:361
  23.7 0.9 %collective-permute-start.9 = (bf16[2,384,128]{2,1,0:T(8,128)(2,1)S(1)}, bf16[2,384,128]{2,1,0:T(8,128)(2,1)S(1)}, u32[]{:S(2)}, u32[]{:S(2)}) collective-permute-start(bf16[2,384,128]{2,1,0:T(8,128)(2,1)S(1)} %pad_maximum_fusion), channel_id=1, source_target_pairs={{0,1},{1,0},{2,3},{3,2},{4,5},{5,4},{6,7},{7,6},{8,9},{9,8},{10,11... | collective-permute-start | bytes 589832 | tf_op jit(solution)/shard_map/ppermute | solution.py:311
  24.6 0.1 broadcast_select_fusion
  24.7 0.1 collective-permute-start.7
  24.7 0.9 %collective-permute-done.9 = bf16[2,384,128]{2,1,0:T(8,128)(2,1)S(1)} collective-permute-done((bf16[2,384,128]{2,1,0:T(8,128)(2,1)S(1)}, bf16[2,384,128]{2,1,0:T(8,128)(2,1)S(1)}, u32[]{:S(2)}, u32[]{:S(2)}) %collective-permute-start.9) | collective-permute-done | bytes 196640 | tf_op jit(solution)/shard_map/ppermute | solution.py:311
  25.7 4.3 %factor_start.1 = (f32[128,128]{1,0:T(8,128)S(1)}, f32[128,128]{1,0:T(8,128)S(1)}) custom-call(bf16[128,128]{1,0:T(8,128)(2,1)S(1)} %get-tuple-element.71.quarter_ref), custom_call_target="tpu_custom_call" | custom-call | flops 1000000 | bytes 10000 | tf_op jit(solution)/shard_map/factor_start/pallas_call | solution.py:253
  30.1 1.3 %collective-permute-start.10 = (bf16[2,256,256]{2,1,0:T(8,128)(2,1)S(1)}, bf16[2,256,256]{2,1,0:T(8,128)(2,1)S(1)}, u32[]{:S(2)}, u32[]{:S(2)}) collective-permute-start(bf16[2,256,256]{2,1,0:T(8,128)(2,1)S(1)} %broadcast_select_fusion.4.above_ref), channel_id=1, source_target_pairs={{0,8},{8,0},{16,24},{24,16},{1,9},{9,1},{17,25},{25,17},{2,10},{10... | collective-permute-start | bytes 786440 | tf_op jit(solution)/shard_map/ppermute | solution.py:311
  31.4 5.4 %factor_first.1 = (f32[256,256]{1,0:T(8,128)S(1)}, bf16[3,256,256]{2,1,0:T(8,128)(2,1)S(1)}) custom-call(bf16[256,128]{1,0:T(8,128)(2,1)S(1)} %get-tuple-element.66.rest_ref, f32[128,128]{1,0:T(8,128)S(1)} %get-tuple-element.38.upper_ref, f32[128,128]{1,0:T(8,128)S(1)} %get-tuple-element.39.tile_inverse_ref), custom_call_target="tpu_custom_call" | custom-call | flops 1000000 | bytes 10000 | tf_op jit(solution)/shard_map/factor_first/pallas_call | solution.py:253
  36.8 4.8 %factor_second_start.1 = (bf16[256,256]{1,0:T(8,128)(2,1)S(1)}, bf16[256,128]{1,0:T(8,128)(2,1)S(1)}, f32[128,128]{1,0:T(8,128)S(1)}, f32[128,128]{1,0:T(8,128)S(1)}) custom-call(bf16[128,128]{1,0:T(8,128)(2,1)S(1)} %get-tuple-element.70.top_10_ref, bf16[256,128]{1,0:T(8,128)(2,1)S(1)} %get-tuple-element.67.rest_10_ref, ...), custom_call_target="tpu_custom_call" | custom-call | flops 1000000 | bytes 10000 | tf_op jit(solution)/shard_map/factor_second_start/pallas_call | solution.py:253
  41.6 0.1 broadcast_select_fusion.1
  41.7 0.9 %collective-permute-start.11 = (bf16[4,256,256]{2,1,0:T(8,128)(2,1)S(1)}, bf16[4,256,256]{2,1,0:T(8,128)(2,1)S(1)}, u32[]{:S(2)}, u32[]{:S(2)}) collective-permute-start(bf16[4,256,256]{2,1,0:T(8,128)(2,1)S(1)} %broadcast_select_fusion.1), channel_id=1, source_target_pairs={{0,1},{1,0},{2,3},{3,2},{4,5},{5,4},{6,7},{7,6},{8,9},{9,8},{10,11... | collective-permute-start | bytes 1572872 | tf_op jit(solution)/shard_map/ppermute | solution.py:311
  42.6 0.1 pad_add_fusion.ids_ref
  42.7 6.0 %factor_second.1 = (f32[256,256]{1,0:T(8,128)S(1)}, bf16[3,256,256]{2,1,0:T(8,128)(2,1)S(1)}, bf16[2,256,256]{2,1,0:T(8,128)(2,1)S(1)}, bf16[2,256,256]{2,1,0:T(8,128)(2,1)S(1)}) custom-call(s32[4]{0:T(128)S(1)} %pad_add_fusion.ids_ref, bf16[256,128]{1,0:T(8,128)(2,1)S(1)} %get-tuple-element.43.rest_ref, f32[128,128]{1,0:T(8,128)S(1)} %get-tuple-element.44.upper_ref, ...), custom_call_target="tpu_custom_call" | custom-call | flops 1000000 | bytes 10000 | tf_op jit(solution)/shard_map/factor_second/pallas_call | solution.py:253
  48.7 0.1 broadcast_select_fusion.2
  48.8 3.5 %solve_and_update.1 = (f32[4,2,256,256]{3,2,1,0:T(8,128)}, bf16[4,2,256,256]{3,2,1,0:T(8,128)(2,1)}) custom-call(s32[4]{0:T(128)S(1)} %pad_add_fusion.ids_ref, bf16[4,256,256]{2,1,0:T(8,128)(2,1)S(1)} %get-tuple-element.61.column_0_ref, bf16[4,256,256]{2,1,0:T(8,128)(2,1)S(1)} %get-tuple-element.60.column_1_ref, bf16[4,2,256,256]{3,2,1,0:T(8,128)(2,1)S(1)} %bitcast.30, ...), custom_call_target="tpu_custom_call" | custom-call | flops 2000000000 | bytes 6000000 | tf_op jit(solution)/shard_map/solve_and_update/pallas_call | solution.py:267
  (16 shorter events, 0.2 us)
Async XLA Ops:
  0.6 1.2 %copy-start = (bf16[1,4,1,2,256,256]{5,4,3,2,1,0:T(8,128)(2,1)S(1)}, bf16[1,4,1,2,256,256]{5,4,3,2,1,0:T(8,128)(2,1)}, u32[]{:S(2)}) copy-start(bf16[1,4,1,2,256,256]{5,4,3,2,1,0:T(8,128)(2,1)} %kernel_ref.1) | copy-start | bytes 3145732
  1.9 8.7 %copy-start.1 = (bf16[1,4,1,2,256,256]{5,4,3,2,1,0:T(8,128)(2,1)S(1)}, bf16[1,4,1,2,256,256]{5,4,3,2,1,0:T(8,128)(2,1)}, u32[]{:S(2)}) copy-start(bf16[1,4,1,2,256,256]{5,4,3,2,1,0:T(8,128)(2,1)} %kernel_ref.1) | copy-start | bytes 3145732
  1.9 10.0 %collective-permute-start.2 = (bf16[384,128]{1,0:T(8,128)(2,1)S(1)}, bf16[384,128]{1,0:T(8,128)(2,1)S(1)}, u32[]{:S(2)}, u32[]{:S(2)}) collective-permute-start(bf16[384,128]{1,0:T(8,128)(2,1)S(1)} %pack.1), channel_id=1, source_target_pairs={{0,2},{1,3},{8,10},{9,11}} | collective-permute-start | bytes 294920 | tf_op jit(solution)/shard_map/ppermute | solution.py:322
  6.1 5.9 %collective-permute-start.1 = (bf16[384,128]{1,0:T(8,128)(2,1)S(1)}, bf16[384,128]{1,0:T(8,128)(2,1)S(1)}, u32[]{:S(2)}, u32[]{:S(2)}) collective-permute-start(bf16[384,128]{1,0:T(8,128)(2,1)S(1)} %pack.1), channel_id=1, source_target_pairs={{0,4},{1,5},{8,12},{9,13}} | collective-permute-start | bytes 294920 | tf_op jit(solution)/shard_map/ppermute | solution.py:322
  7.8 4.5 %collective-permute-start = (bf16[384,128]{1,0:T(8,128)(2,1)S(1)}, bf16[384,128]{1,0:T(8,128)(2,1)S(1)}, u32[]{:S(2)}, u32[]{:S(2)}) collective-permute-start(bf16[384,128]{1,0:T(8,128)(2,1)S(1)} %pack.1), channel_id=1, source_target_pairs={{0,6},{1,7},{8,14},{9,15}} | collective-permute-start | bytes 294920 | tf_op jit(solution)/shard_map/ppermute | solution.py:322
  10.6 13.1 %collective-permute-start.6 = (bf16[4,256,256]{2,1,0:T(8,128)(2,1)S(1)}, bf16[4,256,256]{2,1,0:T(8,128)(2,1)S(1)}, u32[]{:S(2)}, u32[]{:S(2)}) collective-permute-start(bf16[4,256,256]{2,1,0:T(8,128)(2,1)S(1)} %slice_bitcast_fusion), channel_id=1, source_target_pairs={{0,4},{1,5},{8,12},{9,13},{16,20},{17,21},{24,28},{25,29}} | collective-permute-start | bytes 1572872 | tf_op jit(solution)/shard_map/ppermute | solution.py:361
  12.3 3.5 %collective-permute-start.5 = (bf16[384,128]{1,0:T(8,128)(2,1)S(1)}, bf16[384,128]{1,0:T(8,128)(2,1)S(1)}, u32[]{:S(2)}, u32[]{:S(2)}) collective-permute-start(bf16[384,128]{1,0:T(8,128)(2,1)S(1)} %select_select_fusion), channel_id=1, source_target_pairs={{0,8},{8,0},{16,24},{24,16},{1,9},{9,1},{17,25},{25,17},{2,10},{10... | collective-permute-start | bytes 294920 | tf_op jit(solution)/shard_map/ppermute | solution.py:311
  13.6 4.8 %collective-permute-start.4 = (bf16[384,128]{1,0:T(8,128)(2,1)S(1)}, bf16[384,128]{1,0:T(8,128)(2,1)S(1)}, u32[]{:S(2)}, u32[]{:S(2)}) collective-permute-start(bf16[384,128]{1,0:T(8,128)(2,1)S(1)} %select_select_fusion), channel_id=1, source_target_pairs={{0,16},{8,24},{16,0},{24,8},{1,17},{9,25},{17,1},{25,9},{2,18},{10... | collective-permute-start | bytes 294920 | tf_op jit(solution)/shard_map/ppermute | solution.py:311
  13.6 4.8 %collective-permute-start.3 = (bf16[384,128]{1,0:T(8,128)(2,1)S(1)}, bf16[384,128]{1,0:T(8,128)(2,1)S(1)}, u32[]{:S(2)}, u32[]{:S(2)}) collective-permute-start(bf16[384,128]{1,0:T(8,128)(2,1)S(1)} %select_select_fusion), channel_id=1, source_target_pairs={{0,24},{8,16},{16,8},{24,0},{1,25},{9,17},{17,9},{25,1},{2,26},{10... | collective-permute-start | bytes 294920 | tf_op jit(solution)/shard_map/ppermute | solution.py:311
  15.1 15.0 %collective-permute-start.8 = (bf16[2,256,256]{2,1,0:T(8,128)(2,1)S(1)}, bf16[2,256,256]{2,1,0:T(8,128)(2,1)S(1)}, u32[]{:S(2)}, u32[]{:S(2)}) collective-permute-start(bf16[2,256,256]{2,1,0:T(8,128)(2,1)S(1)} %slice_bitcast_fusion.1), channel_id=1, source_target_pairs={{0,16},{8,24},{16,0},{24,8},{1,17},{9,25},{17,1},{25,9},{2,18},{10... | collective-permute-start | bytes 786440 | tf_op jit(solution)/shard_map/ppermute | solution.py:311
  23.7 2.0 %collective-permute-start.9 = (bf16[2,384,128]{2,1,0:T(8,128)(2,1)S(1)}, bf16[2,384,128]{2,1,0:T(8,128)(2,1)S(1)}, u32[]{:S(2)}, u32[]{:S(2)}) collective-permute-start(bf16[2,384,128]{2,1,0:T(8,128)(2,1)S(1)} %pad_maximum_fusion), channel_id=1, source_target_pairs={{0,1},{1,0},{2,3},{3,2},{4,5},{5,4},{6,7},{7,6},{8,9},{9,8},{10,11... | collective-permute-start | bytes 589832 | tf_op jit(solution)/shard_map/ppermute | solution.py:311
  24.7 16.9 %collective-permute-start.7 = (bf16[4,256,256]{2,1,0:T(8,128)(2,1)S(1)}, bf16[4,256,256]{2,1,0:T(8,128)(2,1)S(1)}, u32[]{:S(2)}, u32[]{:S(2)}) collective-permute-start(bf16[4,256,256]{2,1,0:T(8,128)(2,1)S(1)} %broadcast_select_fusion), channel_id=1, source_target_pairs={{0,2},{1,3},{2,0},{3,1},{4,6},{5,7},{6,4},{7,5},{8,10},{9,11},{10,... | collective-permute-start | bytes 1572872 | tf_op jit(solution)/shard_map/ppermute | solution.py:311
  30.1 11.6 %collective-permute-start.10 = (bf16[2,256,256]{2,1,0:T(8,128)(2,1)S(1)}, bf16[2,256,256]{2,1,0:T(8,128)(2,1)S(1)}, u32[]{:S(2)}, u32[]{:S(2)}) collective-permute-start(bf16[2,256,256]{2,1,0:T(8,128)(2,1)S(1)} %broadcast_select_fusion.4.above_ref), channel_id=1, source_target_pairs={{0,8},{8,0},{16,24},{24,16},{1,9},{9,1},{17,25},{25,17},{2,10},{10... | collective-permute-start | bytes 786440 | tf_op jit(solution)/shard_map/ppermute | solution.py:311
  41.7 7.0 %collective-permute-start.11 = (bf16[4,256,256]{2,1,0:T(8,128)(2,1)S(1)}, bf16[4,256,256]{2,1,0:T(8,128)(2,1)S(1)}, u32[]{:S(2)}, u32[]{:S(2)}) collective-permute-start(bf16[4,256,256]{2,1,0:T(8,128)(2,1)S(1)} %broadcast_select_fusion.1), channel_id=1, source_target_pairs={{0,1},{1,0},{2,3},{3,2},{4,5},{5,4},{6,7},{7,6},{8,9},{9,8},{10,11... | collective-permute-start | bytes 1572872 | tf_op jit(solution)/shard_map/ppermute | solution.py:311

commit v8 on v6

--- a/solution.py
+++ b/solution.py
@@ -159,11 +159,11 @@
 
 
 def second_kernel(
-    ids_ref, rest_ref, upper_ref, tile_inverse_ref, pieces_0_ref, panel_ref, above_ref, other_ref,
+    rest_ref, upper_ref, tile_inverse_ref, pieces_0_ref, panel_ref, above_ref, other_ref,
     lower_ref, pieces_1_ref, mirror_ref, later_ref, above_0_ref, above_1_ref,
 ):
     half = rest_ref.shape[1]
-    even = ids_ref[0] % 2 == 0
+    even = lax.rem(lax.axis_index("row"), 2) == 0
     tasks = []
 
     @pl.when(even)
@@ -194,14 +194,16 @@
 
 
 def update_kernel(
-    ids_ref, column_0_ref, column_1_ref, blocks_ref, mirror_0_ref, later_ref,
+    column_0_ref, column_1_ref, blocks_ref, mirror_0_ref, later_ref,
     lower_0_ref, lower_1_ref, pieces_0_ref, pieces_1_ref, panel_10_ref,
     panels_ref, schur_ref, panels_here, schur_here, mirror_1_ref, panels_done, schur_done,
 ):
     row_blocks, col_blocks, width = blocks_ref.shape[:3]
     size = 2 if row_blocks % 2 == 0 else 1
     batches = range(0, row_blocks, size)
-    ids = [i * ids_ref[2] + ids_ref[0] for i in range(row_blocks)]
+    row_count, col_count = lax.axis_size("row"), lax.axis_size("col")
+    my_row, my_col = lax.axis_index("row"), lax.axis_index("col")
+    ids = [i * row_count + my_row for i in range(row_blocks)]
     copies = []
 
     def send(source, target, semaphore):
@@ -236,7 +238,7 @@
                 part = slice((i - b) * width, (i - b + 1) * width)
                 block = blocks_ref[i, m].astype(jnp.float32) - change_0[part]
                 block = block.astype(jnp.bfloat16).astype(jnp.float32) - change_1[part]
-                keep = (ids[i] >= PANELS) & (m * ids_ref[3] + ids_ref[1] >= PANELS)
+                keep = (ids[i] >= PANELS) & (m * col_count + my_col >= PANELS)
                 schur_here[i, m] = jnp.where(keep, block, 0.0).astype(jnp.bfloat16)
         for i in range(b, b + size):
             send(schur_here.at[i], schur_ref.at[i], schur_done.at[i])
@@ -248,8 +250,7 @@
 
 
 def call_factor(kernel, name, shapes, *operands, scratch=()):
-    in_specs = [
-        pl.BlockSpec(memory_space=pltpu.SMEM if x.dtype == jnp.int32 else pltpu.VMEM) for x in operands]
+    in_specs = [pl.BlockSpec(memory_space=pltpu.VMEM)] * len(operands)
     return pl.pallas_call(
         kernel, in_specs=in_specs, out_shape=shapes, scratch_shapes=scratch, name=name, cost_estimate=FACTOR_COST,
         compiler_params=pltpu.CompilerParams(vmem_limit_bytes=VMEM_LIMIT),
@@ -260,13 +261,13 @@
     return jax.ShapeDtypeStruct((width, width), dtype)
 
 
-def update(ids, column_0, column_1, blocks, mirror_0, later, lower_0, lower_1, pieces_0, pieces_1, panel_10):
+def update(column_0, column_1, blocks, mirror_0, later, lower_0, lower_1, pieces_0, pieces_1, panel_10):
     row_blocks, col_blocks, width = blocks.shape[:3]
     panels = jax.ShapeDtypeStruct((row_blocks, PANELS, width, width), jnp.float32)
     schur = jax.ShapeDtypeStruct(blocks.shape, jnp.bfloat16)
     return pl.pallas_call(
         update_kernel,
-        in_specs=[pl.BlockSpec(memory_space=pltpu.SMEM)] + [pl.BlockSpec(memory_space=pltpu.VMEM)] * 10,
+        in_specs=[pl.BlockSpec(memory_space=pltpu.VMEM)] * 10,
         out_specs=[pl.BlockSpec(memory_space=pl.ANY)] * 2,
         out_shape=[panels, schur],
         scratch_shapes=[
@@ -279,7 +280,7 @@
         compiler_params=pltpu.CompilerParams(vmem_limit_bytes=VMEM_LIMIT),
         cost_estimate=pl.CostEstimate(flops=2 * 10**9, bytes_accessed=6 * 10**6, transcendentals=0),
         name="solve_and_update",
-    )(ids, column_0, column_1, blocks, mirror_0, later, lower_0, lower_1, pieces_0, pieces_1, panel_10)
+    )(column_0, column_1, blocks, mirror_0, later, lower_0, lower_1, pieces_0, pieces_1, panel_10)
 
 
 def pack_kernel(kernel_ref, quarters_ref, semaphores):
@@ -383,7 +384,6 @@
     blocks = kernel[0, :, 0]
     col_blocks, width = blocks.shape[1:3]
     half = width // 2
-    ids = jnp.stack([my_row, my_col, lax.axis_size("row"), lax.axis_size("col")]).astype(jnp.int32)
     quarters = pack(kernel)
     rows, above, _ = lax.optimization_barrier((blocks[:, 0], blocks[0], quarters))
     rows, rows_got = first_stride(rows)
@@ -409,13 +409,13 @@
     mirror = jax.ShapeDtypeStruct((col_blocks, width, width), jnp.bfloat16)
     lower_1, pieces_1, mirror_0, later = call_factor(
         second_kernel, "factor_second", [square(width), pieces, mirror, mirror],
-        ids, rest_11, upper_1, tile_inverse_1, pieces_0, panel_10, above, above_other,
+        rest_11, upper_1, tile_inverse_1, pieces_0, panel_10, above, above_other,
         scratch=[pltpu.VMEM(mirror.shape, mirror.dtype)] * 2)
     other, lower_1 = lax.optimization_barrier((other, lower_1))
     column_0 = jnp.where(even, rows, other)
     column_1 = jnp.where(even, other, rows)
     panels, schur = update(
-        ids, column_0, column_1, blocks, mirror_0, later, lower_0, lower_1, pieces_0, pieces_1, panel_10)
+        column_0, column_1, blocks, mirror_0, later, lower_0, lower_1, pieces_0, pieces_1, panel_10)
     return (panels[None], schur[None, :, None])
 
 

time: 52.7 us -> 51.5 us (0.977)
  Pallas kernels: 24 us -> 22.9 us
    pallas_call x4, Pallas kernels: 20.5 us -> 20 us  [call_factor(): pl.pallas_call(kernel, in_specs=in_specs, out_shape=shapes, scratch_shape...]
    pallas_call x1, Pallas kernels: 3.47 us -> 2.92 us  [update(): pl.pallas_call(update_kernel, in_specs=[pl.BlockSpec(memory_space=pltpu.V...]
where the time goes in v8:
time: 51.5 us; the launch traced here: 51.2 us
  Pallas kernels  22.9 us (44%)
  starting transfers between devices  14.8 us (29%)
  waiting for transfers between devices  9.82 us (19%)
  local copies, waits for them, and re-layouts  2.35 us (5%)
  between operations  1.03 us (2%)
    pallas_call x4, Pallas kernels, call_factor(): pl.pallas_call(kernel, in_specs=in_specs, out_shape=shapes, scratch_shape...  20 us
    ppermute x3, starting transfers between devices, diagonal_along(): got = lax.ppermute(quarters, ('row', 'col'), pairs)  7.53 us
    ppermute x8, starting transfers between devices, swap(): return lax.ppermute(block, axis, [(d, d ^ distance) for d in range(count)])  5.94 us
    ppermute x1, waiting for transfers between devices, first_stride(): return (block, lax.ppermute(block, 'col', pairs))  5.15 us
    ppermute x8, waiting for transfers between devices, swap(): return lax.ppermute(block, axis, [(d, d ^ distance) for d in range(count)])  4.29 us
    pallas_call x1, Pallas kernels, update(): pl.pallas_call(update_kernel, in_specs=[pl.BlockSpec(memory_space=pltpu.V...  2.92 us
    ppermute x1, starting transfers between devices, first_stride(): return (block, lax.ppermute(block, 'col', pairs))  1.32 us
    unnamed x4, local copies, waits for them, and re-layouts  1.22 us
  transfers between devices with their start and end apart: 12, of which 5 were waited for; matrix products, arithmetic and copies ran while one was open for 3% of the time, Pallas kernels for 39%

profile of v8, /device:TPU:1, one launch (start us, length us, event | category | flops | bytes accessed | tf_op | source)
XLA Modules:
  0.0 51.2 jit_solution(3571835606958468169)
XLA Ops:
  0.6 0.0 copy-start
  0.6 1.2 %copy-done = bf16[1,4,1,2,256,256]{5,4,3,2,1,0:T(8,128)(2,1)S(1)} copy-done((bf16[1,4,1,2,256,256]{5,4,3,2,1,0:T(8,128)(2,1)S(1)}, bf16[1,4,1,2,256,256]{5,4,3,2,1,0:T(8,128)(2,1)}, u32[]{:S(2)}) %copy-start) | copy-done | bytes 1048600
  1.9 0.1 pack.1
  1.9 4.2 %collective-permute-start.2 = (bf16[384,128]{1,0:T(8,128)(2,1)S(1)}, bf16[384,128]{1,0:T(8,128)(2,1)S(1)}, u32[]{:S(2)}, u32[]{:S(2)}) collective-permute-start(bf16[384,128]{1,0:T(8,128)(2,1)S(1)} %pack.1), channel_id=1, source_target_pairs={{0,2},{1,3},{8,10},{9,11}} | collective-permute-start | bytes 294920 | tf_op jit(solution)/shard_map/ppermute | solution.py:323
  6.1 1.7 %collective-permute-start.1 = (bf16[384,128]{1,0:T(8,128)(2,1)S(1)}, bf16[384,128]{1,0:T(8,128)(2,1)S(1)}, u32[]{:S(2)}, u32[]{:S(2)}) collective-permute-start(bf16[384,128]{1,0:T(8,128)(2,1)S(1)} %pack.1), channel_id=1, source_target_pairs={{0,4},{1,5},{8,12},{9,13}} | collective-permute-start | bytes 294920 | tf_op jit(solution)/shard_map/ppermute | solution.py:323
  7.8 1.7 %collective-permute-start = (bf16[384,128]{1,0:T(8,128)(2,1)S(1)}, bf16[384,128]{1,0:T(8,128)(2,1)S(1)}, u32[]{:S(2)}, u32[]{:S(2)}) collective-permute-start(bf16[384,128]{1,0:T(8,128)(2,1)S(1)} %pack.1), channel_id=1, source_target_pairs={{0,6},{1,7},{8,14},{9,15}} | collective-permute-start | bytes 294920 | tf_op jit(solution)/shard_map/ppermute | solution.py:323
  9.5 1.1 %slice_bitcast_fusion = bf16[4,256,256]{2,1,0:T(8,128)(2,1)S(1)} fusion(bf16[4,2,256,256]{3,2,1,0:T(8,128)(2,1)} %bitcast.27), kind=kLoop, calls=%fused_computation | loop fusion | bytes 1048576 | tf_op jit(solution)/shard_map/squeeze | solution.py:388
  10.6 1.3 %collective-permute-start.6 = (bf16[4,256,256]{2,1,0:T(8,128)(2,1)S(1)}, bf16[4,256,256]{2,1,0:T(8,128)(2,1)S(1)}, u32[]{:S(2)}, u32[]{:S(2)}) collective-permute-start(bf16[4,256,256]{2,1,0:T(8,128)(2,1)S(1)} %slice_bitcast_fusion), channel_id=1, source_target_pairs={{0,4},{1,5},{8,12},{9,13},{16,20},{17,21},{24,28},{25,29}} | collective-permute-start | bytes 1572872 | tf_op jit(solution)/shard_map/ppermute | solution.py:362
  11.9 0.0 collective-permute-done.1
  12.0 0.4 collective-permute-done
  12.3 1.3 %collective-permute-start.5 = (bf16[384,128]{1,0:T(8,128)(2,1)S(1)}, bf16[384,128]{1,0:T(8,128)(2,1)S(1)}, u32[]{:S(2)}, u32[]{:S(2)}) collective-permute-start(bf16[384,128]{1,0:T(8,128)(2,1)S(1)} %select_select_fusion), channel_id=1, source_target_pairs={{0,8},{8,0},{16,24},{24,16},{1,9},{9,1},{17,25},{25,17},{2,10},{10... | collective-permute-start | bytes 294920 | tf_op jit(solution)/shard_map/ppermute | solution.py:312
  13.6 0.0 collective-permute-start.4
  13.6 1.4 %collective-permute-start.3 = (bf16[384,128]{1,0:T(8,128)(2,1)S(1)}, bf16[384,128]{1,0:T(8,128)(2,1)S(1)}, u32[]{:S(2)}, u32[]{:S(2)}) collective-permute-start(bf16[384,128]{1,0:T(8,128)(2,1)S(1)} %select_select_fusion), channel_id=1, source_target_pairs={{0,24},{8,16},{16,8},{24,0},{1,25},{9,17},{17,9},{25,1},{2,26},{10... | collective-permute-start | bytes 294920 | tf_op jit(solution)/shard_map/ppermute | solution.py:312
  15.1 0.0 collective-permute-start.8
  15.1 0.8 %collective-permute-done.5 = bf16[384,128]{1,0:T(8,128)(2,1)S(1)} collective-permute-done((bf16[384,128]{1,0:T(8,128)(2,1)S(1)}, bf16[384,128]{1,0:T(8,128)(2,1)S(1)}, u32[]{:S(2)}, u32[]{:S(2)}) %collective-permute-start.5) | collective-permute-done | bytes 98336 | tf_op jit(solution)/shard_map/ppermute | solution.py:312
  15.9 2.6 %collective-permute-done.4 = bf16[384,128]{1,0:T(8,128)(2,1)S(1)} collective-permute-done((bf16[384,128]{1,0:T(8,128)(2,1)S(1)}, bf16[384,128]{1,0:T(8,128)(2,1)S(1)}, u32[]{:S(2)}, u32[]{:S(2)}) %collective-permute-start.4) | collective-permute-done | bytes 98336 | tf_op jit(solution)/shard_map/ppermute | solution.py:312
  18.5 5.2 %collective-permute-done.6 = bf16[4,256,256]{2,1,0:T(8,128)(2,1)S(1)} collective-permute-done((bf16[4,256,256]{2,1,0:T(8,128)(2,1)S(1)}, bf16[4,256,256]{2,1,0:T(8,128)(2,1)S(1)}, u32[]{:S(2)}, u32[]{:S(2)}) %collective-permute-start.6) | collective-permute-done | bytes 524320 | tf_op jit(solution)/shard_map/ppermute | solution.py:362
  23.7 0.9 %collective-permute-start.9 = (bf16[2,384,128]{2,1,0:T(8,128)(2,1)S(1)}, bf16[2,384,128]{2,1,0:T(8,128)(2,1)S(1)}, u32[]{:S(2)}, u32[]{:S(2)}) collective-permute-start(bf16[2,384,128]{2,1,0:T(8,128)(2,1)S(1)} %pad_maximum_fusion), channel_id=1, source_target_pairs={{0,1},{1,0},{2,3},{3,2},{4,5},{5,4},{6,7},{7,6},{8,9},{9,8},{10,11... | collective-permute-start | bytes 589832 | tf_op jit(solution)/shard_map/ppermute | solution.py:312
  24.6 0.1 broadcast_select_fusion
  24.7 0.1 collective-permute-start.7
  24.7 0.9 %collective-permute-done.9 = bf16[2,384,128]{2,1,0:T(8,128)(2,1)S(1)} collective-permute-done((bf16[2,384,128]{2,1,0:T(8,128)(2,1)S(1)}, bf16[2,384,128]{2,1,0:T(8,128)(2,1)S(1)}, u32[]{:S(2)}, u32[]{:S(2)}) %collective-permute-start.9) | collective-permute-done | bytes 196640 | tf_op jit(solution)/shard_map/ppermute | solution.py:312
  25.7 4.3 %factor_start.1 = (f32[128,128]{1,0:T(8,128)S(1)}, f32[128,128]{1,0:T(8,128)S(1)}) custom-call(bf16[128,128]{1,0:T(8,128)(2,1)S(1)} %get-tuple-element.71.quarter_ref), custom_call_target="tpu_custom_call" | custom-call | flops 1000000 | bytes 10000 | tf_op jit(solution)/shard_map/factor_start/pallas_call | solution.py:254
  30.0 0.0 collective-permute-done.8
  30.1 1.3 %collective-permute-start.10 = (bf16[2,256,256]{2,1,0:T(8,128)(2,1)S(1)}, bf16[2,256,256]{2,1,0:T(8,128)(2,1)S(1)}, u32[]{:S(2)}, u32[]{:S(2)}) collective-permute-start(bf16[2,256,256]{2,1,0:T(8,128)(2,1)S(1)} %broadcast_select_fusion.4.above_ref), channel_id=1, source_target_pairs={{0,8},{8,0},{16,24},{24,16},{1,9},{9,1},{17,25},{25,17},{2,10},{10... | collective-permute-start | bytes 786440 | tf_op jit(solution)/shard_map/ppermute | solution.py:312
  31.4 5.4 %factor_first.1 = (f32[256,256]{1,0:T(8,128)S(1)}, bf16[3,256,256]{2,1,0:T(8,128)(2,1)S(1)}) custom-call(bf16[256,128]{1,0:T(8,128)(2,1)S(1)} %get-tuple-element.66.rest_ref, f32[128,128]{1,0:T(8,128)S(1)} %get-tuple-element.38.upper_ref, f32[128,128]{1,0:T(8,128)S(1)} %get-tuple-element.39.tile_inverse_ref), custom_call_target="tpu_custom_call" | custom-call | flops 1000000 | bytes 10000 | tf_op jit(solution)/shard_map/factor_first/pallas_call | solution.py:254
  36.8 4.8 %factor_second_start.1 = (bf16[256,256]{1,0:T(8,128)(2,1)S(1)}, bf16[256,128]{1,0:T(8,128)(2,1)S(1)}, f32[128,128]{1,0:T(8,128)S(1)}, f32[128,128]{1,0:T(8,128)S(1)}) custom-call(bf16[128,128]{1,0:T(8,128)(2,1)S(1)} %get-tuple-element.70.top_10_ref, bf16[256,128]{1,0:T(8,128)(2,1)S(1)} %get-tuple-element.67.rest_10_ref, ...), custom_call_target="tpu_custom_call" | custom-call | flops 1000000 | bytes 10000 | tf_op jit(solution)/shard_map/factor_second_start/pallas_call | solution.py:254
  41.6 0.1 broadcast_select_fusion.1
  41.7 0.0 collective-permute-done.10.other_ref
  41.7 0.9 %collective-permute-start.11 = (bf16[4,256,256]{2,1,0:T(8,128)(2,1)S(1)}, bf16[4,256,256]{2,1,0:T(8,128)(2,1)S(1)}, u32[]{:S(2)}, u32[]{:S(2)}) collective-permute-start(bf16[4,256,256]{2,1,0:T(8,128)(2,1)S(1)} %broadcast_select_fusion.1), channel_id=1, source_target_pairs={{0,1},{1,0},{2,3},{3,2},{4,5},{5,4},{6,7},{7,6},{8,9},{9,8},{10,11... | collective-permute-start | bytes 1572872 | tf_op jit(solution)/shard_map/ppermute | solution.py:312
  42.6 5.5 %factor_second.1 = (f32[256,256]{1,0:T(8,128)S(1)}, bf16[3,256,256]{2,1,0:T(8,128)(2,1)S(1)}, bf16[2,256,256]{2,1,0:T(8,128)(2,1)S(1)}, bf16[2,256,256]{2,1,0:T(8,128)(2,1)S(1)}) custom-call(bf16[256,128]{1,0:T(8,128)(2,1)S(1)} %get-tuple-element.43.rest_ref, f32[128,128]{1,0:T(8,128)S(1)} %get-tuple-element.44.upper_ref, ...), custom_call_target="tpu_custom_call" | custom-call | flops 1000000 | bytes 10000 | tf_op jit(solution)/shard_map/factor_second/pallas_call | solution.py:254
  48.1 0.1 broadcast_select_fusion.2
  48.1 2.9 %solve_and_update.1 = (f32[4,2,256,256]{3,2,1,0:T(8,128)}, bf16[4,2,256,256]{3,2,1,0:T(8,128)(2,1)}) custom-call(bf16[4,256,256]{2,1,0:T(8,128)(2,1)S(1)} %get-tuple-element.61.column_0_ref, bf16[4,256,256]{2,1,0:T(8,128)(2,1)S(1)} %get-tuple-element.60.column_1_ref, bf16[4,2,256,256]{3,2,1,0:T(8,128)(2,1)S(1)} %bitcast.28, ...), custom_call_target="tpu_custom_call" | custom-call | flops 2000000000 | bytes 6000000 | tf_op jit(solution)/shard_map/solve_and_update/pallas_call | solution.py:268
  (15 shorter events, 0.2 us)
Async XLA Ops:
  0.6 1.2 %copy-start = (bf16[1,4,1,2,256,256]{5,4,3,2,1,0:T(8,128)(2,1)S(1)}, bf16[1,4,1,2,256,256]{5,4,3,2,1,0:T(8,128)(2,1)}, u32[]{:S(2)}) copy-start(bf16[1,4,1,2,256,256]{5,4,3,2,1,0:T(8,128)(2,1)} %kernel_ref.1) | copy-start | bytes 3145732
  1.9 8.7 %copy-start.1 = (bf16[1,4,1,2,256,256]{5,4,3,2,1,0:T(8,128)(2,1)S(1)}, bf16[1,4,1,2,256,256]{5,4,3,2,1,0:T(8,128)(2,1)}, u32[]{:S(2)}) copy-start(bf16[1,4,1,2,256,256]{5,4,3,2,1,0:T(8,128)(2,1)} %kernel_ref.1) | copy-start | bytes 3145732
  1.9 10.0 %collective-permute-start.2 = (bf16[384,128]{1,0:T(8,128)(2,1)S(1)}, bf16[384,128]{1,0:T(8,128)(2,1)S(1)}, u32[]{:S(2)}, u32[]{:S(2)}) collective-permute-start(bf16[384,128]{1,0:T(8,128)(2,1)S(1)} %pack.1), channel_id=1, source_target_pairs={{0,2},{1,3},{8,10},{9,11}} | collective-permute-start | bytes 294920 | tf_op jit(solution)/shard_map/ppermute | solution.py:323
  6.1 5.9 %collective-permute-start.1 = (bf16[384,128]{1,0:T(8,128)(2,1)S(1)}, bf16[384,128]{1,0:T(8,128)(2,1)S(1)}, u32[]{:S(2)}, u32[]{:S(2)}) collective-permute-start(bf16[384,128]{1,0:T(8,128)(2,1)S(1)} %pack.1), channel_id=1, source_target_pairs={{0,4},{1,5},{8,12},{9,13}} | collective-permute-start | bytes 294920 | tf_op jit(solution)/shard_map/ppermute | solution.py:323
  7.8 4.5 %collective-permute-start = (bf16[384,128]{1,0:T(8,128)(2,1)S(1)}, bf16[384,128]{1,0:T(8,128)(2,1)S(1)}, u32[]{:S(2)}, u32[]{:S(2)}) collective-permute-start(bf16[384,128]{1,0:T(8,128)(2,1)S(1)} %pack.1), channel_id=1, source_target_pairs={{0,6},{1,7},{8,14},{9,15}} | collective-permute-start | bytes 294920 | tf_op jit(solution)/shard_map/ppermute | solution.py:323
  10.6 13.1 %collective-permute-start.6 = (bf16[4,256,256]{2,1,0:T(8,128)(2,1)S(1)}, bf16[4,256,256]{2,1,0:T(8,128)(2,1)S(1)}, u32[]{:S(2)}, u32[]{:S(2)}) collective-permute-start(bf16[4,256,256]{2,1,0:T(8,128)(2,1)S(1)} %slice_bitcast_fusion), channel_id=1, source_target_pairs={{0,4},{1,5},{8,12},{9,13},{16,20},{17,21},{24,28},{25,29}} | collective-permute-start | bytes 1572872 | tf_op jit(solution)/shard_map/ppermute | solution.py:362
  12.3 3.5 %collective-permute-start.5 = (bf16[384,128]{1,0:T(8,128)(2,1)S(1)}, bf16[384,128]{1,0:T(8,128)(2,1)S(1)}, u32[]{:S(2)}, u32[]{:S(2)}) collective-permute-start(bf16[384,128]{1,0:T(8,128)(2,1)S(1)} %select_select_fusion), channel_id=1, source_target_pairs={{0,8},{8,0},{16,24},{24,16},{1,9},{9,1},{17,25},{25,17},{2,10},{10... | collective-permute-start | bytes 294920 | tf_op jit(solution)/shard_map/ppermute | solution.py:312
  13.6 4.8 %collective-permute-start.4 = (bf16[384,128]{1,0:T(8,128)(2,1)S(1)}, bf16[384,128]{1,0:T(8,128)(2,1)S(1)}, u32[]{:S(2)}, u32[]{:S(2)}) collective-permute-start(bf16[384,128]{1,0:T(8,128)(2,1)S(1)} %select_select_fusion), channel_id=1, source_target_pairs={{0,16},{8,24},{16,0},{24,8},{1,17},{9,25},{17,1},{25,9},{2,18},{10... | collective-permute-start | bytes 294920 | tf_op jit(solution)/shard_map/ppermute | solution.py:312
  13.6 4.8 %collective-permute-start.3 = (bf16[384,128]{1,0:T(8,128)(2,1)S(1)}, bf16[384,128]{1,0:T(8,128)(2,1)S(1)}, u32[]{:S(2)}, u32[]{:S(2)}) collective-permute-start(bf16[384,128]{1,0:T(8,128)(2,1)S(1)} %select_select_fusion), channel_id=1, source_target_pairs={{0,24},{8,16},{16,8},{24,0},{1,25},{9,17},{17,9},{25,1},{2,26},{10... | collective-permute-start | bytes 294920 | tf_op jit(solution)/shard_map/ppermute | solution.py:312
  15.1 15.0 %collective-permute-start.8 = (bf16[2,256,256]{2,1,0:T(8,128)(2,1)S(1)}, bf16[2,256,256]{2,1,0:T(8,128)(2,1)S(1)}, u32[]{:S(2)}, u32[]{:S(2)}) collective-permute-start(bf16[2,256,256]{2,1,0:T(8,128)(2,1)S(1)} %slice_bitcast_fusion.1), channel_id=1, source_target_pairs={{0,16},{8,24},{16,0},{24,8},{1,17},{9,25},{17,1},{25,9},{2,18},{10... | collective-permute-start | bytes 786440 | tf_op jit(solution)/shard_map/ppermute | solution.py:312
  23.7 2.0 %collective-permute-start.9 = (bf16[2,384,128]{2,1,0:T(8,128)(2,1)S(1)}, bf16[2,384,128]{2,1,0:T(8,128)(2,1)S(1)}, u32[]{:S(2)}, u32[]{:S(2)}) collective-permute-start(bf16[2,384,128]{2,1,0:T(8,128)(2,1)S(1)} %pad_maximum_fusion), channel_id=1, source_target_pairs={{0,1},{1,0},{2,3},{3,2},{4,5},{5,4},{6,7},{7,6},{8,9},{9,8},{10,11... | collective-permute-start | bytes 589832 | tf_op jit(solution)/shard_map/ppermute | solution.py:312
  24.7 16.9 %collective-permute-start.7 = (bf16[4,256,256]{2,1,0:T(8,128)(2,1)S(1)}, bf16[4,256,256]{2,1,0:T(8,128)(2,1)S(1)}, u32[]{:S(2)}, u32[]{:S(2)}) collective-permute-start(bf16[4,256,256]{2,1,0:T(8,128)(2,1)S(1)} %broadcast_select_fusion), channel_id=1, source_target_pairs={{0,2},{1,3},{2,0},{3,1},{4,6},{5,7},{6,4},{7,5},{8,10},{9,11},{10,... | collective-permute-start | bytes 1572872 | tf_op jit(solution)/shard_map/ppermute | solution.py:312
  30.1 11.6 %collective-permute-start.10 = (bf16[2,256,256]{2,1,0:T(8,128)(2,1)S(1)}, bf16[2,256,256]{2,1,0:T(8,128)(2,1)S(1)}, u32[]{:S(2)}, u32[]{:S(2)}) collective-permute-start(bf16[2,256,256]{2,1,0:T(8,128)(2,1)S(1)} %broadcast_select_fusion.4.above_ref), channel_id=1, source_target_pairs={{0,8},{8,0},{16,24},{24,16},{1,9},{9,1},{17,25},{25,17},{2,10},{10... | collective-permute-start | bytes 786440 | tf_op jit(solution)/shard_map/ppermute | solution.py:312
  41.7 6.4 %collective-permute-start.11 = (bf16[4,256,256]{2,1,0:T(8,128)(2,1)S(1)}, bf16[4,256,256]{2,1,0:T(8,128)(2,1)S(1)}, u32[]{:S(2)}, u32[]{:S(2)}) collective-permute-start(bf16[4,256,256]{2,1,0:T(8,128)(2,1)S(1)} %broadcast_select_fusion.1), channel_id=1, source_target_pairs={{0,1},{1,0},{2,3},{3,2},{4,5},{5,4},{6,7},{7,6},{8,9},{9,8},{10,11... | collective-permute-start | bytes 1572872 | tf_op jit(solution)/shard_map/ppermute | solution.py:312
